TPU v7x, 32 devices: a whole 2x2x4 slice. The times are simulated.
32 devices in a mesh: groups: 2 (over x), expert: 16 (over z, y, core).
Axes of the slice: x: 2, y: 2, z: 4, core: 2. Of those that a mesh axis runs over, the one named last changes fastest.
Arguments:
- tokens: bfloat16 [1024, 7168], P(('groups', 'expert')), parts along dimension 0, may hold values from -6 to 6
- expert_ids: int32 [1024, 8], P(('groups', 'expert')), parts along dimension 0, may hold values from 0 to 255, as said below
- replica: int32 [1024, 8], P(('groups', 'expert')), parts along dimension 0, may hold values from 0 to 1
- gate_weights: float32 [1024, 8], P(('groups', 'expert')), parts along dimension 0, may hold values from 0.1 to 0.6
- slot_table: int32 [512, 2], P('groups'), parts along dimension 0, may hold values from 0 to 2, as said below
- gate_pieces: bfloat16 [32, 7168, 256], P(('groups', 'expert')), parts along dimension 0, as said below
- up_pieces: bfloat16 [32, 7168, 256], P(('groups', 'expert')), parts along dimension 0, as said below
- down_pieces: bfloat16 [32, 256, 7168], P(('groups', 'expert')), parts along dimension 0, as said below
Outputs:
- routed_output: bfloat16 [1024, 7168], P(('groups', 'expert')), parts along dimension 0
There are 2 independent parts, one for each index of `groups`. A program takes and returns all parts, laid end to end along the dimension named above; each array names one. Nothing has to cross between parts.
Inputs may be any that keep to these rules, and one draw needn't show every extreme that they name: `expert_ids`: each row names 8 different experts. `slot_table`: row e holds the copies hosting expert e for replicas 0 and 1, two different copies, or 2 twice where e is not hosted; every copy hosts exactly one expert, and 1 experts are hosted. `gate_pieces`: slots of copies that host the same expert hold equal weights. `up_pieces`: slots of copies that host the same expert hold equal weights. `down_pieces`: slots of copies that host the same expert hold equal weights.
All inputs are finite; a program needn't handle non-finite values.
Results may differ from a plain program's by a relative error of at most 0.0057.
Values may be sent and summed in bfloat16 or wider, within the bound.
No kernel may reach another device: no remote copies, remote signals or barrier semaphores. Data moves between devices by JAX's collectives and lax.ppermute only.
A program may use at most 128 MiB of HBM per device.

v0:
```python
import jax
import jax.numpy as jnp
from jax import lax
from jax.sharding import PartitionSpec as P

PIECES = 8
CAP = 12


def expert_rows(arrived, gate_part, up_part, down_part):
    flattened = arrived.reshape(-1, arrived.shape[-1])
    gate_act = jnp.dot(flattened, gate_part, preferred_element_type=jnp.float32)
    up_act = jnp.dot(flattened, up_part, preferred_element_type=jnp.float32)
    hidden = (jax.nn.silu(gate_act) * up_act).astype(jnp.bfloat16)
    result = jnp.dot(hidden, down_part, preferred_element_type=jnp.float32).astype(jnp.bfloat16)
    return result.reshape(arrived.shape[:-1] + (down_part.shape[1],))


def on_device(
    tokens, expert_ids, replica, gate_weights, slot_table, gate_pieces, up_pieces, down_pieces
):
    devices = lax.axis_size("expert")
    copies = devices // PIECES
    width = tokens.shape[1]
    specialist_extent = jnp.arange(slot_table.shape[0], dtype=jnp.int32)
    matches = (expert_ids[:, :, None] == specialist_extent[None, None, :]).astype(jnp.int32)
    per_replica = jnp.where(
        replica[:, :, None] == 0, slot_table[:, 0][None, None, :], slot_table[:, 1][None, None, :]
    )
    targets = jnp.sum(matches * per_replica, axis=2)
    copy_range = jnp.arange(copies, dtype=jnp.int32)
    members = (targets[:, :, None] == copy_range[None, None, :]).astype(jnp.int32)
    routed = jnp.sum(members, axis=1)
    position = jnp.cumsum(routed, axis=0) - routed
    retained = routed * (position < CAP).astype(jnp.int32)
    gate_copy = jnp.sum(gate_weights[:, :, None] * members.astype(jnp.float32), axis=1)
    slot_range = jnp.arange(CAP, dtype=jnp.int32)
    chosen_rows = retained.T[:, None, :] * (
        position.T[:, None, :] == slot_range[None, :, None]
    ).astype(jnp.int32)
    send_rows = jnp.einsum(
        "cjt,td->cjd", chosen_rows.astype(jnp.bfloat16), tokens, preferred_element_type=jnp.float32
    ).astype(jnp.bfloat16)
    gate_part = gate_pieces[0]
    up_part = up_pieces[0]
    down_part = down_pieces[0]
    outgoing = jnp.broadcast_to(send_rows[:, None], (copies, PIECES, CAP, width)).reshape(
        devices, CAP, width
    )
    arrived = lax.all_to_all(outgoing, "expert", split_axis=0, concat_axis=0, tiled=True)
    produced = expert_rows(arrived, gate_part, up_part, down_part)
    returned = lax.all_to_all(produced, "expert", split_axis=0, concat_axis=0, tiled=True)
    combined = jnp.sum(returned.reshape(copies, PIECES, CAP, width).astype(jnp.float32), axis=1)
    weighting = chosen_rows.astype(jnp.float32) * gate_copy.T[:, None, :]
    total = jnp.einsum("cjt,cjd->td", weighting, combined, precision=lax.Precision.HIGHEST)
    return total.astype(jnp.bfloat16)


def solution(mesh):
    placed = (
        P(("groups", "expert"), None),
        P(("groups", "expert"), None),
        P(("groups", "expert"), None),
        P(("groups", "expert"), None),
        P("groups", None),
        P(("groups", "expert"), None, None),
        P(("groups", "expert"), None, None),
        P(("groups", "expert"), None, None),
    )
    return jax.shard_map(
        on_device,
        mesh=mesh,
        in_specs=placed,
        out_specs=P(("groups", "expert"), None),
        check_vma=False,
    )
```

profile of v0, /device:TPU:13, one launch (start us, length us, event | category | flops | bytes accessed | tf_op | source)
XLA Modules:
  0.0 200.9 jit_solution(17423689711317048770)
XLA Ops:
  0.0 0.0 copy-start
  0.0 0.7 broadcast_compare_fusion
  0.7 0.8 fusion.35
  1.5 0.1 copy.20
  1.6 0.8 copy.19
  2.4 0.7 select_reduce_fusion
  3.1 0.1 copy.21
  3.2 0.1 copy.22
  3.2 0.1 reduce_window_sum.13
  3.3 0.1 copy.25
  3.4 0.1 copy.24
  3.5 0.0 copy-done
  3.5 0.3 convolution_convert_fusion.1
  3.8 0.4 broadcast_in_dim.49
  4.2 87.5 %all_to_all.10 = bf16[16,12,7168]{2,1,0:T(8,128)(2,1)} all-to-all(bf16[16,12,7168]{2,1,0:T(8,128)(2,1)S(1)} %bitcast.39), channel_id=1, replica_groups=mesh['groups'=2,'expert'=16] {'expert'}, dimensions={0} | all-to-all | bytes 5505024 | tf_op jit(solution)/shard_map/all_to_all | solution.py:50
  91.6 3.0 %reshape.24 = bf16[192,7168]{1,0:T(8,128)(2,1)S(1)} reshape(bf16[16,12,7168]{2,1,0:T(8,128)(2,1)} %all_to_all.10) | data formatting | bytes 5505024 | tf_op jit(solution)/shard_map/reshape | solution.py:11
  94.7 2.9 %fusion.4 = f32[192,256]{1,0:T(8,128)S(1)} fusion(bf16[192,7168]{1,0:T(8,128)(2,1)S(1)} %reshape.24, bf16[1,7168,256]{2,1,0:T(8,128)(2,1)} %param.13), kind=kOutput, calls=%fused_computation.8 | convolution fusion | flops 704643072 | bytes 6619136 | tf_op jit(solution)/shard_map/dot_general | solution.py:12
  97.6 7.8 %convolution_convert_fusion = bf16[192,7168]{1,0:T(8,128)(2,1)} fusion(bf16[1,256,7168]{2,1,0:T(8,128)(2,1)} %param.15, bf16[192,7168]{1,0:T(8,128)(2,1)S(1)} %reshape.24, bf16[1,7168,256]{2,1,0:T(8,128)(2,1)} %param.14, f32[192,256]{1,0:T(8,128)S(1)} %fusion.4), kind=kOutput, calls=%fused_computation | convolution fusion | flops 1410957312 | bytes 13041664 | tf_op jit(solution)/shard_map/dot_general | solution.py:15
  105.4 4.4 %reshape.25 = bf16[16,12,7168]{2,1,0:T(8,128)(2,1)} reshape(bf16[192,7168]{1,0:T(8,128)(2,1)} %convolution_convert_fusion) | data formatting | bytes 5505024 | tf_op jit(solution)/shard_map/reshape | solution.py:16
  109.8 0.0 copy-start.1
  109.8 5.4 %all-to-all-start.1 = ((bf16[16,12,7168]{2,1,0:T(8,128)(2,1)}), bf16[16,12,7168]{2,1,0:T(8,128)(2,1)}, u32[]{:S(2)}, u32[]{:S(2)}) async-start(bf16[16,12,7168]{2,1,0:T(8,128)(2,1)} %reshape.25), calls=%async_computation.1 | async-start | bytes 7340032 | tf_op jit(solution)/shard_map/all_to_all | solution.py:52
  115.2 0.0 copy-done.1
  115.2 81.2 %all-to-all-done.1 = bf16[16,12,7168]{2,1,0:T(8,128)(2,1)} async-done(((bf16[16,12,7168]{2,1,0:T(8,128)(2,1)}), bf16[16,12,7168]{2,1,0:T(8,128)(2,1)}, u32[]{:S(2)}, u32[]{:S(2)}) %all-to-all-start.1) | async-done | bytes 2752544 | tf_op jit(solution)/shard_map/all_to_all | solution.py:52
  196.4 2.8 %convert_reduce_fusion = f32[2,12,7168]{2,1,0:T(8,128)S(1)} fusion(bf16[16,12,7168]{2,1,0:T(8,128)(2,1)} %all-to-all-done.1), kind=kLoop, calls=%fused_computation.4 | loop fusion | flops 2580480 | bytes 3440640 | tf_op jit(solution)/shard_map/reduce_sum | solution.py:53
  199.2 1.7 fusion
  (3 shorter events, 0.1 us)
Async XLA Ops:
  0.0 3.5 %copy-start = (bf16[32,7168]{1,0:T(8,128)(2,1)S(1)}, bf16[32,7168]{1,0:T(8,128)(2,1)}, u32[]{:S(2)}) copy-start(bf16[32,7168]{1,0:T(8,128)(2,1)} %param.8) | copy-start | bytes 1376260
  109.8 5.4 %copy-start.1 = (f32[32,8]{0,1:T(8,128)S(1)}, f32[32,8]{0,1:T(8,128)}, u32[]{:S(2)}) copy-start(f32[32,8]{0,1:T(8,128)} %param.11) | copy-start | bytes 3076
  109.8 86.6 %all-to-all-start.1 = ((bf16[16,12,7168]{2,1,0:T(8,128)(2,1)}), bf16[16,12,7168]{2,1,0:T(8,128)(2,1)}, u32[]{:S(2)}, u32[]{:S(2)}) async-start(bf16[16,12,7168]{2,1,0:T(8,128)(2,1)} %reshape.25), calls=%async_computation.1 | async-start | bytes 7340032 | tf_op jit(solution)/shard_map/all_to_all | solution.py:52
where the time goes:
time: 201 us
  blocking collectives  87.5 us (44%)
  waiting for transfers between devices  81.2 us (40%)
  matrix products  12.7 us (6%)
  local copies, waits for them, and re-layouts  9.83 us (5%)
  starting transfers between devices  5.37 us (3%)
  other arithmetic  4.31 us (2%)
    all_to_all x1, blocking collectives, on_device(): lax.all_to_all(outgoing, 'expert', split_axis=0, concat_axis=0, tiled=True)  87.5 us
    all_to_all x1, waiting for transfers between devices, on_device(): lax.all_to_all(produced, 'expert', split_axis=0, concat_axis=0, tiled=True)  81.2 us
    dot_general x1, matrix products, expert_rows(): jnp.dot(hidden, down_part, preferred_element_type=jnp.float32)  7.77 us
    all_to_all x1, starting transfers between devices, on_device(): lax.all_to_all(produced, 'expert', split_axis=0, concat_axis=0, tiled=True)  5.37 us
    reshape x1, local copies, waits for them, and re-layouts, expert_rows(): return result.reshape(arrived.shape[:-1] + (down_part.shape[1],))  4.45 us
  transfers between devices with their start and end apart: 1, of which 1 were waited for; matrix products, arithmetic and copies ran while one was open for 0% of the time, Pallas kernels for 0%

commit v1 on v0

--- a/solution.py
+++ b/solution.py
@@ -1,10 +1,15 @@
+import functools
+
 import jax
 import jax.numpy as jnp
 from jax import lax
+from jax.experimental import pallas as pl
+from jax.experimental.pallas import tpu as pltpu
 from jax.sharding import PartitionSpec as P
 
 PIECES = 8
 CAP = 12
+VMEM_LIMIT = 56 * 1024 * 1024
 
 
 def expert_rows(arrived, gate_part, up_part, down_part):
@@ -16,7 +21,7 @@
     return result.reshape(arrived.shape[:-1] + (down_part.shape[1],))
 
 
-def on_device(
+def any_copies(
     tokens, expert_ids, replica, gate_weights, slot_table, gate_pieces, up_pieces, down_pieces
 ):
     devices = lax.axis_size("expert")
@@ -56,6 +61,129 @@
     return total.astype(jnp.bfloat16)
 
 
+def slots_of(ids, rep, table):
+    experts = lax.broadcasted_iota(jnp.int32, table.shape, 1)
+    here = table < 2
+    first = jnp.sum(jnp.where(here, table, 0)[0:1], axis=1, keepdims=True)
+    hosted = jnp.sum(jnp.where(here, experts, 0)[0:1], axis=1, keepdims=True)
+    hit = ids == hosted
+    copy = jnp.where(rep == 0, first, 1 - first)
+    count = ids.shape[1]
+    to = [jnp.sum(jnp.where(hit & (copy == c), 1.0, 0.0), axis=0, keepdims=True) for c in range(2)]
+    earlier = (
+        lax.broadcasted_iota(jnp.int32, (count, count), 0)
+        < lax.broadcasted_iota(jnp.int32, (count, count), 1)
+    ).astype(jnp.float32)
+    slot = jnp.full((1, count), -1, jnp.int32)
+    for c in range(2):
+        routed = jnp.broadcast_to(to[c], (8, count))
+        position = jnp.dot(routed, earlier, preferred_element_type=jnp.float32)[0:1]
+        position = position.astype(jnp.int32)
+        keep = (to[c] > 0.5) & (position < CAP)
+        slot = jnp.where(keep, position + c * CAP, slot)
+    return slot, hit
+
+
+def pick_kernel(tok_ref, ids_ref, rep_ref, table_ref, low_ref, high_ref):
+    slot, _ = slots_of(ids_ref[...], rep_ref[...], table_ref[...])
+    count = slot.shape[1]
+    chosen = lax.broadcasted_iota(jnp.int32, (2 * CAP, count), 0) == slot
+    chosen = chosen.astype(jnp.bfloat16)
+    half = low_ref.shape[1]
+    low_ref[...] = jnp.dot(
+        chosen, tok_ref[:, :half], preferred_element_type=jnp.float32
+    ).astype(jnp.bfloat16)
+    high_ref[...] = jnp.dot(
+        chosen, tok_ref[:, half:], preferred_element_type=jnp.float32
+    ).astype(jnp.bfloat16)
+
+
+def expert_kernel(*refs):
+    x_refs = refs[:16]
+    gate_ref, up_ref, down_ref, mine_ref, other_ref, x_all = refs[16:]
+    rows = x_refs[0].shape[0]
+    half = x_refs[0].shape[1]
+    for i in range(8):
+        x_all[i * rows : (i + 1) * rows, :half] = x_refs[2 * i][...]
+        x_all[i * rows : (i + 1) * rows, half:] = x_refs[2 * i + 1][...]
+    x = x_all[...]
+    gate = jnp.dot(x, gate_ref[...], preferred_element_type=jnp.float32)
+    up = jnp.dot(x, up_ref[...], preferred_element_type=jnp.float32)
+    hidden = (gate / (1.0 + jnp.exp(-gate)) * up).astype(jnp.bfloat16)
+    out = jnp.dot(hidden, down_ref[...], preferred_element_type=jnp.float32).astype(jnp.bfloat16)
+    mine_ref[...] = out[: 4 * rows]
+    other_ref[...] = out[4 * rows :]
+
+
+def combine_kernel(own_ref, y_ref, z_ref, ids_ref, rep_ref, table_ref, w_ref, out_ref):
+    slot, hit = slots_of(ids_ref[...], rep_ref[...], table_ref[...])
+    weight = jnp.sum(jnp.where(hit, w_ref[...], 0.0), axis=0, keepdims=True)
+    count = slot.shape[1]
+    chosen = lax.broadcasted_iota(jnp.int32, (2 * CAP, count), 0) == slot
+    spread = jnp.where(chosen, weight, 0.0)
+    spread_hi = spread.astype(jnp.bfloat16)
+    spread_lo = (spread - spread_hi.astype(jnp.float32)).astype(jnp.bfloat16)
+    total = own_ref[...].astype(jnp.float32) + y_ref[...].astype(jnp.float32)
+    total = total + z_ref[...].astype(jnp.float32)
+    total_hi = total.astype(jnp.bfloat16)
+    total_lo = (total - total_hi.astype(jnp.float32)).astype(jnp.bfloat16)
+    dims = (((0,), (0,)), ((), ()))
+    dot = functools.partial(
+        lax.dot_general, dimension_numbers=dims, preferred_element_type=jnp.float32
+    )
+    out = dot(spread_hi, total_hi) + (dot(spread_hi, total_lo) + dot(spread_lo, total_hi))
+    out_ref[...] = out.astype(jnp.bfloat16)
+
+
+def two_copies(
+    tokens, expert_ids, replica, gate_weights, slot_table, gate_pieces, up_pieces, down_pieces
+):
+    devices = lax.axis_size("expert")
+    count, width = tokens.shape
+    half = width // 2
+    rows = 2 * CAP
+    bf16 = jnp.bfloat16
+
+    def swap(a, bit):
+        return lax.ppermute(a, "expert", [(i, i ^ bit) for i in range(devices)])
+
+    params = pltpu.CompilerParams(vmem_limit_bytes=VMEM_LIMIT)
+    ids, rep, table, weights = expert_ids.T, replica.T, slot_table.T, gate_weights.T
+    low, high = pl.pallas_call(
+        pick_kernel,
+        out_shape=[jax.ShapeDtypeStruct((rows, half), bf16)] * 2,
+        compiler_params=params,
+    )(tokens, ids, rep, table)
+    y_low, z_high = swap(low, 2), swap(high, 4)
+    y_high, z_low = swap(high, 2), swap(low, 4)
+    d_low, d_high = swap(y_low, 4), swap(z_high, 2)
+    held = [low, high, y_low, y_high, z_low, z_high, d_low, d_high]
+    partner = [swap(a, 1) for a in held]
+    mine, other = pl.pallas_call(
+        expert_kernel,
+        out_shape=[jax.ShapeDtypeStruct((4 * rows, width), bf16)] * 2,
+        scratch_shapes=[pltpu.VMEM((8 * rows, width), bf16)],
+        compiler_params=params,
+    )(*held, *partner, gate_pieces[0], up_pieces[0], down_pieces[0])
+    met = swap(other, 1)
+    total = (mine.astype(jnp.float32) + met.astype(jnp.float32)).astype(bf16)
+    own, to_y, to_z, to_d = (total[i * rows : (i + 1) * rows] for i in range(4))
+    from_y, from_z = swap(to_d[:, :half], 2), swap(to_d[:, half:], 4)
+    f32 = jnp.float32
+    to_z = jnp.concatenate(
+        [(to_z[:, :half].astype(f32) + from_y.astype(f32)).astype(bf16), to_z[:, half:]], axis=1
+    )
+    to_y = jnp.concatenate(
+        [to_y[:, :half], (to_y[:, half:].astype(f32) + from_z.astype(f32)).astype(bf16)], axis=1
+    )
+    got_y, got_z = swap(to_y, 2), swap(to_z, 4)
+    return pl.pallas_call(
+        combine_kernel,
+        out_shape=jax.ShapeDtypeStruct((count, width), bf16),
+        compiler_params=params,
+    )(own, got_y, got_z, ids, rep, table, weights)
+
+
 def solution(mesh):
     placed = (
         P(("groups", "expert"), None),
@@ -68,7 +196,7 @@
         P(("groups", "expert"), None, None),
     )
     return jax.shard_map(
-        on_device,
+        two_copies if mesh.shape["expert"] == 2 * PIECES else any_copies,
         mesh=mesh,
         in_specs=placed,
         out_specs=P(("groups", "expert"), None),

time: 201 us -> 57.6 us (0.29)
  the two profiles are of different devices: /device:TPU:13 before, /device:TPU:0 now
where the time goes in v1:
time: 57.6 us; the launch traced here: 57.4 us
  waiting for transfers between devices  26.2 us (45%)
  Pallas kernels  14 us (24%)
  starting transfers between devices  12.9 us (22%)
  local copies, waits for them, and re-layouts  2.16 us (4%)
  other arithmetic  1.81 us (3%)
    ppermute x19, waiting for transfers between devices, swap(): return lax.ppermute(a, 'expert', [(i, i ^ bit) for i in range(devices)])  26.2 us
    ppermute x19, starting transfers between devices, swap(): return lax.ppermute(a, 'expert', [(i, i ^ bit) for i in range(devices)])  12.9 us
    pallas_call x1, Pallas kernels, two_copies(): pl.pallas_call(expert_kernel, out_shape=[jax.ShapeDtypeStruct((4 * rows,...  9.09 us
    pallas_call x1, Pallas kernels, two_copies(): pl.pallas_call(combine_kernel, out_shape=jax.ShapeDtypeStruct((count, wid...  2.76 us
    pallas_call x1, Pallas kernels, two_copies(): pl.pallas_call(pick_kernel, out_shape=[jax.ShapeDtypeStruct((rows, half),...  2.19 us
    convert_element_type x1, other arithmetic, two_copies(): total = (mine.astype(jnp.float32) + met.astype(jnp.float32)).astype(bf16)  1.68 us
    unnamed x32, local copies, waits for them, and re-layouts  1.36 us
  transfers between devices with their start and end apart: 19, of which 11 were waited for; matrix products, arithmetic and copies ran while one was open for 1% of the time, Pallas kernels for 0%

profile of v1, /device:TPU:0, one launch (start us, length us, event | category | flops | bytes accessed | tf_op | source)
XLA Modules:
  0.0 57.4 jit_solution(14984638840219630687)
XLA Ops:
  0.0 2.2 %shard_map.82 = (bf16[24,3584]{1,0:T(8,128)(2,1)}, bf16[24,3584]{1,0:T(8,128)(2,1)}) custom-call(bf16[32,7168]{1,0:T(8,128)(2,1)} %tok_ref.1, s32[8,32]{1,0:T(8,128)} %bitcast.10, s32[8,32]{1,0:T(8,128)} %bitcast.12, s32[2,256]{1,0:T(2,128)} %bitcast.14), custom_call_target="tpu_custom_call" | custom-call | tf_op jit(solution)/shard_map/pallas_call | solution.py:152
  2.2 0.5 collective-permute-start.6
  2.6 2.6 %collective-permute-start.2 = (bf16[24,3584]{1,0:T(8,128)(2,1)}, bf16[24,3584]{1,0:T(8,128)(2,1)S(1)}, u32[]{:S(2)}, u32[]{:S(2)}) collective-permute-start(bf16[24,3584]{1,0:T(8,128)(2,1)} %get-tuple-element.9.refs_0_), channel_id=1, source_target_pairs={{0,4},{1,5},{2,6},{3,7},{4,0},{5,1},{6,2},{7,3},{8,12},{9,13},{10,... | collective-permute-start | bytes 516104 | tf_op jit(solution)/shard_map/ppermute | solution.py:148
  5.2 1.5 %collective-permute-start = (bf16[24,3584]{1,0:T(8,128)(2,1)}, bf16[24,3584]{1,0:T(8,128)(2,1)S(1)}, u32[]{:S(2)}, u32[]{:S(2)}) collective-permute-start(bf16[24,3584]{1,0:T(8,128)(2,1)} %get-tuple-element.9.refs_0_), channel_id=1, source_target_pairs={{0,2},{1,3},{2,0},{3,1},{4,6},{5,7},{6,4},{7,5},{8,10},{9,11},{10,... | collective-permute-start | bytes 516104 | tf_op jit(solution)/shard_map/ppermute | solution.py:148
  6.7 0.4 collective-permute-start.3
  7.2 0.0 collective-permute-start.7
  7.2 0.0 collective-permute-done.6.refs_8_
  7.2 0.2 collective-permute-start.1
  7.4 3.3 %collective-permute-done.2.refs_4_ = bf16[24,3584]{1,0:T(8,128)(2,1)S(1)} collective-permute-done((bf16[24,3584]{1,0:T(8,128)(2,1)}, bf16[24,3584]{1,0:T(8,128)(2,1)S(1)}, u32[]{:S(2)}, u32[]{:S(2)}) %collective-permute-start.2) | collective-permute-done | bytes 172064 | tf_op jit(solution)/shard_map/ppermute | solution.py:148
  10.7 0.0 collective-permute-start.10
  10.7 2.0 %collective-permute-done.refs_2_ = bf16[24,3584]{1,0:T(8,128)(2,1)S(1)} collective-permute-done((bf16[24,3584]{1,0:T(8,128)(2,1)}, bf16[24,3584]{1,0:T(8,128)(2,1)S(1)}, u32[]{:S(2)}, u32[]{:S(2)}) %collective-permute-start) | collective-permute-done | bytes 172064 | tf_op jit(solution)/shard_map/ppermute | solution.py:148
  12.6 0.0 collective-permute-start.4
  12.7 1.7 %collective-permute-done.3.refs_5_ = bf16[24,3584]{1,0:T(8,128)(2,1)S(1)} collective-permute-done((bf16[24,3584]{1,0:T(8,128)(2,1)}, bf16[24,3584]{1,0:T(8,128)(2,1)S(1)}, u32[]{:S(2)}, u32[]{:S(2)}) %collective-permute-start.3) | collective-permute-done | bytes 172064 | tf_op jit(solution)/shard_map/ppermute | solution.py:148
  14.3 1.6 %collective-permute-start.5 = (bf16[24,3584]{1,0:T(8,128)(2,1)S(1)}, bf16[24,3584]{1,0:T(8,128)(2,1)S(1)}, u32[]{:S(2)}, u32[]{:S(2)}) collective-permute-start(bf16[24,3584]{1,0:T(8,128)(2,1)S(1)} %collective-permute-done.3.refs_5_), channel_id=1, source_target_pairs={{0,2},{1,3},{2,0},{3,1},{4,6},{5,7},{6,4},{7,5},{8,10},{9,11},{10,... | collective-permute-start | bytes 516104 | tf_op jit(solution)/shard_map/ppermute | solution.py:148
  16.0 0.0 collective-permute-done.7.refs_9_
  16.0 0.0 collective-permute-start.8
  16.0 0.0 collective-permute-done.1.refs_3_
  16.0 0.0 copy-start.7
  16.0 0.5 collective-permute-start.11
  16.5 0.0 collective-permute-done.10.refs_12_
  16.5 0.1 collective-permute-start.9
  16.6 1.5 %collective-permute-done.4.refs_6_ = bf16[24,3584]{1,0:T(8,128)(2,1)S(1)} collective-permute-done((bf16[24,3584]{1,0:T(8,128)(2,1)S(1)}, bf16[24,3584]{1,0:T(8,128)(2,1)S(1)}, u32[]{:S(2)}, u32[]{:S(2)}) %collective-permute-start.4) | collective-permute-done | bytes 172064 | tf_op jit(solution)/shard_map/ppermute | solution.py:148
  18.0 0.0 collective-permute-start.12
  18.1 2.3 %collective-permute-done.5.refs_7_ = bf16[24,3584]{1,0:T(8,128)(2,1)S(1)} collective-permute-done((bf16[24,3584]{1,0:T(8,128)(2,1)S(1)}, bf16[24,3584]{1,0:T(8,128)(2,1)S(1)}, u32[]{:S(2)}, u32[]{:S(2)}) %collective-permute-start.5) | collective-permute-done | bytes 172064 | tf_op jit(solution)/shard_map/ppermute | solution.py:148
  20.4 0.0 collective-permute-start.13
  20.4 0.0 collective-permute-done.8.refs_10_
  20.4 0.0 copy-start.11
  20.4 0.0 collective-permute-done.11.refs_13_
  20.4 0.0 copy-start.12
  20.4 0.0 collective-permute-done.9.refs_11_
  20.4 0.0 copy-start.13
  20.4 0.0 collective-permute-done.12.refs_14_
  20.4 0.0 copy-start.14
  20.5 1.3 %collective-permute-done.13.refs_15_ = bf16[24,3584]{1,0:T(8,128)(2,1)S(1)} collective-permute-done((bf16[24,3584]{1,0:T(8,128)(2,1)S(1)}, bf16[24,3584]{1,0:T(8,128)(2,1)S(1)}, u32[]{:S(2)}, u32[]{:S(2)}) %collective-permute-start.13) | collective-permute-done | bytes 172064 | tf_op jit(solution)/shard_map/ppermute | solution.py:148
  21.8 0.0 copy-done.2
  21.8 0.0 copy-done.3
  21.8 0.0 copy-done.4
  21.8 0.0 copy-done.5
  21.8 0.0 copy-done.6
  21.8 0.0 copy-done.7
  21.8 0.0 copy-done.8
  21.8 0.0 copy-done.9
  21.8 0.0 copy-done.10
  21.9 0.0 copy-done.11
  21.9 0.0 copy-done.12
  21.9 0.0 copy-done.13
  21.9 0.6 copy-done.15
  22.5 9.1 %shard_map.83 = (bf16[96,7168]{1,0:T(8,128)(2,1)}, bf16[96,7168]{1,0:T(8,128)(2,1)}) custom-call(bf16[24,3584]{1,0:T(8,128)(2,1)} %get-tuple-element.9.refs_0_, bf16[24,3584]{1,0:T(8,128)(2,1)} %get-tuple-element.10.refs_1_, bf16[24,3584]{1,0:T(8,128)(2,1)} %copy-done.4, bf16[24,3584]{1,0:T(8,128)(2,1)} %copy-done.7, bf16[24,3584]{1,0:T(8,128)(2,1)} %copy-done.3, ...), custom_call_target="tpu_custom_call" | custom-call | tf_op jit(solution)/shard_map/pallas_call | solution.py:162
  31.5 0.1 collective-permute-start.14
  31.7 3.2 %collective-permute-done.14 = bf16[96,7168]{1,0:T(8,128)(2,1)S(1)} collective-permute-done((bf16[96,7168]{1,0:T(8,128)(2,1)}, bf16[96,7168]{1,0:T(8,128)(2,1)S(1)}, u32[]{:S(2)}, u32[]{:S(2)}) %collective-permute-start.14) | collective-permute-done | bytes 1376288 | tf_op jit(solution)/shard_map/ppermute | solution.py:148
  34.9 1.7 %add_convert_fusion = bf16[96,7168]{1,0:T(8,128)(2,1)S(1)} fusion(bf16[96,7168]{1,0:T(8,128)(2,1)S(1)} %collective-permute-done.14, bf16[96,7168]{1,0:T(8,128)(2,1)} %get-tuple-element.11), kind=kLoop, calls=%fused_computation | loop fusion | flops 2752512 | bytes 4128768 | tf_op jit(solution)/shard_map/convert_element_type | solution.py:169
  36.6 1.5 %collective-permute-start.17 = (bf16[24,3584]{1,0:T(8,128)(2,1)S(1)}, bf16[24,3584]{1,0:T(8,128)(2,1)S(1)}, u32[]{:S(2)}, u32[]{:S(2)}) collective-permute-start(bf16[24,3584]{1,0:T(8,128)(2,1)S(1)} %get-tuple-element.15), channel_id=1, source_target_pairs={{0,2},{1,3},{2,0},{3,1},{4,6},{5,7},{6,4},{7,5},{8,10},{9,11},{10,... | collective-permute-start | bytes 516104 | tf_op jit(solution)/shard_map/ppermute | solution.py:148
  38.2 1.6 %collective-permute-start.15 = (bf16[24,3584]{1,0:T(8,128)(2,1)S(1)}, bf16[24,3584]{1,0:T(8,128)(2,1)S(1)}, u32[]{:S(2)}, u32[]{:S(2)}) collective-permute-start(bf16[24,3584]{1,0:T(8,128)(2,1)S(1)} %get-tuple-element.17), channel_id=1, source_target_pairs={{0,4},{1,5},{2,6},{3,7},{4,0},{5,1},{6,2},{7,3},{8,12},{9,13},{10,... | collective-permute-start | bytes 516104 | tf_op jit(solution)/shard_map/ppermute | solution.py:148
  39.7 3.4 %collective-permute-done.17 = bf16[24,3584]{1,0:T(8,128)(2,1)S(1)} collective-permute-done((bf16[24,3584]{1,0:T(8,128)(2,1)S(1)}, bf16[24,3584]{1,0:T(8,128)(2,1)S(1)}, u32[]{:S(2)}, u32[]{:S(2)}) %collective-permute-start.17) | collective-permute-done | bytes 172064 | tf_op jit(solution)/shard_map/ppermute | solution.py:148
  43.1 1.2 %collective-permute-done.15 = bf16[24,3584]{1,0:T(8,128)(2,1)S(1)} collective-permute-done((bf16[24,3584]{1,0:T(8,128)(2,1)S(1)}, bf16[24,3584]{1,0:T(8,128)(2,1)S(1)}, u32[]{:S(2)}, u32[]{:S(2)}) %collective-permute-start.15) | collective-permute-done | bytes 172064 | tf_op jit(solution)/shard_map/ppermute | solution.py:148
  44.3 0.1 add_convert_fusion.1
  44.4 0.6 %collective-permute-start.16 = (bf16[24,7168]{1,0:T(8,128)(2,1)S(1)}, bf16[24,7168]{1,0:T(8,128)(2,1)S(1)}, u32[]{:S(2)}, u32[]{:S(2)}) collective-permute-start(bf16[24,7168]{1,0:T(8,128)(2,1)S(1)} %pad_maximum_fusion), channel_id=1, source_target_pairs={{0,2},{1,3},{2,0},{3,1},{4,6},{5,7},{6,4},{7,5},{8,10},{9,11},{10,... | collective-permute-start | bytes 1032200 | tf_op jit(solution)/shard_map/ppermute | solution.py:148
  45.1 1.6 %collective-permute-start.18 = (bf16[24,7168]{1,0:T(8,128)(2,1)S(1)}, bf16[24,7168]{1,0:T(8,128)(2,1)S(1)}, u32[]{:S(2)}, u32[]{:S(2)}) collective-permute-start(bf16[24,7168]{1,0:T(8,128)(2,1)S(1)} %pad_maximum_fusion.1), channel_id=1, source_target_pairs={{0,4},{1,5},{2,6},{3,7},{4,0},{5,1},{6,2},{7,3},{8,12},{9,13},{10,... | collective-permute-start | bytes 1032200 | tf_op jit(solution)/shard_map/ppermute | solution.py:148
  46.7 0.8 %slice.37.own_ref = bf16[24,7168]{1,0:T(8,128)(2,1)} slice(bf16[96,7168]{1,0:T(8,128)(2,1)S(1)} %add_convert_fusion), slice={[0:24], [0:7168]} | slice | bytes 688128 | tf_op jit(solution)/shard_map/slice | solution.py:170
  47.4 6.0 %collective-permute-done.16.y_ref = bf16[24,7168]{1,0:T(8,128)(2,1)S(1)} collective-permute-done((bf16[24,7168]{1,0:T(8,128)(2,1)S(1)}, bf16[24,7168]{1,0:T(8,128)(2,1)S(1)}, u32[]{:S(2)}, u32[]{:S(2)}) %collective-permute-start.16) | collective-permute-done | bytes 344096 | tf_op jit(solution)/shard_map/ppermute | solution.py:148
  53.4 0.4 collective-permute-done.18.z_ref
  53.9 0.3 copy-done
  54.2 0.4 copy-done.1
  54.6 2.8 %shard_map.84 = bf16[32,7168]{1,0:T(8,128)(2,1)} custom-call(bf16[24,7168]{1,0:T(8,128)(2,1)} %slice.37.own_ref, bf16[24,7168]{1,0:T(8,128)(2,1)} %copy-done, bf16[24,7168]{1,0:T(8,128)(2,1)} %copy-done.1, s32[8,32]{1,0:T(8,128)} %bitcast.11, s32[8,32]{1,0:T(8,128)} %bitcast.13, s32[2,256]{1,0:T(2,128)} %bitcast.15, f32[8,32]{1,0:T(8,128)} %bitcast.16), custom_call_target="tpu_custom_call" | custom-call | tf_op jit(solution)/shard_map/pallas_call | solution.py:180
  (15 shorter events, 0.1 us)
Async XLA Ops:
  2.2 5.0 %collective-permute-start.6 = (bf16[24,3584]{1,0:T(8,128)(2,1)}, bf16[24,3584]{1,0:T(8,128)(2,1)S(1)}, u32[]{:S(2)}, u32[]{:S(2)}) collective-permute-start(bf16[24,3584]{1,0:T(8,128)(2,1)} %get-tuple-element.9.refs_0_), channel_id=1, source_target_pairs={{0,1},{1,0},{2,3},{3,2},{4,5},{5,4},{6,7},{7,6},{8,9},{9,8},{10,11... | collective-permute-start | bytes 516104 | tf_op jit(solution)/shard_map/ppermute | solution.py:148
  2.6 8.0 %collective-permute-start.2 = (bf16[24,3584]{1,0:T(8,128)(2,1)}, bf16[24,3584]{1,0:T(8,128)(2,1)S(1)}, u32[]{:S(2)}, u32[]{:S(2)}) collective-permute-start(bf16[24,3584]{1,0:T(8,128)(2,1)} %get-tuple-element.9.refs_0_), channel_id=1, source_target_pairs={{0,4},{1,5},{2,6},{3,7},{4,0},{5,1},{6,2},{7,3},{8,12},{9,13},{10,... | collective-permute-start | bytes 516104 | tf_op jit(solution)/shard_map/ppermute | solution.py:148
  5.2 7.4 %collective-permute-start = (bf16[24,3584]{1,0:T(8,128)(2,1)}, bf16[24,3584]{1,0:T(8,128)(2,1)S(1)}, u32[]{:S(2)}, u32[]{:S(2)}) collective-permute-start(bf16[24,3584]{1,0:T(8,128)(2,1)} %get-tuple-element.9.refs_0_), channel_id=1, source_target_pairs={{0,2},{1,3},{2,0},{3,1},{4,6},{5,7},{6,4},{7,5},{8,10},{9,11},{10,... | collective-permute-start | bytes 516104 | tf_op jit(solution)/shard_map/ppermute | solution.py:148
  6.7 7.6 %collective-permute-start.3 = (bf16[24,3584]{1,0:T(8,128)(2,1)}, bf16[24,3584]{1,0:T(8,128)(2,1)S(1)}, u32[]{:S(2)}, u32[]{:S(2)}) collective-permute-start(bf16[24,3584]{1,0:T(8,128)(2,1)} %get-tuple-element.10.refs_1_), channel_id=1, source_target_pairs={{0,4},{1,5},{2,6},{3,7},{4,0},{5,1},{6,2},{7,3},{8,12},{9,13},{10,... | collective-permute-start | bytes 516104 | tf_op jit(solution)/shard_map/ppermute | solution.py:148
  7.2 8.8 %collective-permute-start.7 = (bf16[24,3584]{1,0:T(8,128)(2,1)}, bf16[24,3584]{1,0:T(8,128)(2,1)S(1)}, u32[]{:S(2)}, u32[]{:S(2)}) collective-permute-start(bf16[24,3584]{1,0:T(8,128)(2,1)} %get-tuple-element.10.refs_1_), channel_id=1, source_target_pairs={{0,1},{1,0},{2,3},{3,2},{4,5},{5,4},{6,7},{7,6},{8,9},{9,8},{10,11... | collective-permute-start | bytes 516104 | tf_op jit(solution)/shard_map/ppermute | solution.py:148
  7.2 14.6 %copy-start.2 = (bf16[24,3584]{1,0:T(8,128)(2,1)}, bf16[24,3584]{1,0:T(8,128)(2,1)S(1)}, u32[]{:S(2)}) copy-start(bf16[24,3584]{1,0:T(8,128)(2,1)S(1)} %collective-permute-done.6.refs_8_) | copy-start | bytes 516100
  7.2 8.8 %collective-permute-start.1 = (bf16[24,3584]{1,0:T(8,128)(2,1)}, bf16[24,3584]{1,0:T(8,128)(2,1)S(1)}, u32[]{:S(2)}, u32[]{:S(2)}) collective-permute-start(bf16[24,3584]{1,0:T(8,128)(2,1)} %get-tuple-element.10.refs_1_), channel_id=1, source_target_pairs={{0,2},{1,3},{2,0},{3,1},{4,6},{5,7},{6,4},{7,5},{8,10},{9,11},{10,... | collective-permute-start | bytes 516104 | tf_op jit(solution)/shard_map/ppermute | solution.py:148
  10.7 11.1 %copy-start.3 = (bf16[24,3584]{1,0:T(8,128)(2,1)}, bf16[24,3584]{1,0:T(8,128)(2,1)S(1)}, u32[]{:S(2)}) copy-start(bf16[24,3584]{1,0:T(8,128)(2,1)S(1)} %collective-permute-done.2.refs_4_) | copy-start | bytes 516100
  10.7 5.8 %collective-permute-start.10 = (bf16[24,3584]{1,0:T(8,128)(2,1)S(1)}, bf16[24,3584]{1,0:T(8,128)(2,1)S(1)}, u32[]{:S(2)}, u32[]{:S(2)}) collective-permute-start(bf16[24,3584]{1,0:T(8,128)(2,1)S(1)} %collective-permute-done.2.refs_4_), channel_id=1, source_target_pairs={{0,1},{1,0},{2,3},{3,2},{4,5},{5,4},{6,7},{7,6},{8,9},{9,8},{10,11... | collective-permute-start | bytes 516104 | tf_op jit(solution)/shard_map/ppermute | solution.py:148
  12.6 9.2 %copy-start.4 = (bf16[24,3584]{1,0:T(8,128)(2,1)}, bf16[24,3584]{1,0:T(8,128)(2,1)S(1)}, u32[]{:S(2)}) copy-start(bf16[24,3584]{1,0:T(8,128)(2,1)S(1)} %collective-permute-done.refs_2_) | copy-start | bytes 516100
  12.6 5.4 %collective-permute-start.4 = (bf16[24,3584]{1,0:T(8,128)(2,1)S(1)}, bf16[24,3584]{1,0:T(8,128)(2,1)S(1)}, u32[]{:S(2)}, u32[]{:S(2)}) collective-permute-start(bf16[24,3584]{1,0:T(8,128)(2,1)S(1)} %collective-permute-done.refs_2_), channel_id=1, source_target_pairs={{0,4},{1,5},{2,6},{3,7},{4,0},{5,1},{6,2},{7,3},{8,12},{9,13},{10,... | collective-permute-start | bytes 516104 | tf_op jit(solution)/shard_map/ppermute | solution.py:148
  14.3 7.5 %copy-start.5 = (bf16[24,3584]{1,0:T(8,128)(2,1)}, bf16[24,3584]{1,0:T(8,128)(2,1)S(1)}, u32[]{:S(2)}) copy-start(bf16[24,3584]{1,0:T(8,128)(2,1)S(1)} %collective-permute-done.3.refs_5_) | copy-start | bytes 516100
  14.3 6.0 %collective-permute-start.5 = (bf16[24,3584]{1,0:T(8,128)(2,1)S(1)}, bf16[24,3584]{1,0:T(8,128)(2,1)S(1)}, u32[]{:S(2)}, u32[]{:S(2)}) collective-permute-start(bf16[24,3584]{1,0:T(8,128)(2,1)S(1)} %collective-permute-done.3.refs_5_), channel_id=1, source_target_pairs={{0,2},{1,3},{2,0},{3,1},{4,6},{5,7},{6,4},{7,5},{8,10},{9,11},{10,... | collective-permute-start | bytes 516104 | tf_op jit(solution)/shard_map/ppermute | solution.py:148
  16.0 5.8 %copy-start.6 = (bf16[24,3584]{1,0:T(8,128)(2,1)}, bf16[24,3584]{1,0:T(8,128)(2,1)S(1)}, u32[]{:S(2)}) copy-start(bf16[24,3584]{1,0:T(8,128)(2,1)S(1)} %collective-permute-done.7.refs_9_) | copy-start | bytes 516100
  16.0 4.4 %collective-permute-start.8 = (bf16[24,3584]{1,0:T(8,128)(2,1)S(1)}, bf16[24,3584]{1,0:T(8,128)(2,1)S(1)}, u32[]{:S(2)}, u32[]{:S(2)}) collective-permute-start(bf16[24,3584]{1,0:T(8,128)(2,1)S(1)} %collective-permute-done.refs_2_), channel_id=1, source_target_pairs={{0,1},{1,0},{2,3},{3,2},{4,5},{5,4},{6,7},{7,6},{8,9},{9,8},{10,11... | collective-permute-start | bytes 516104 | tf_op jit(solution)/shard_map/ppermute | solution.py:148
  16.0 5.8 %copy-start.7 = (bf16[24,3584]{1,0:T(8,128)(2,1)}, bf16[24,3584]{1,0:T(8,128)(2,1)S(1)}, u32[]{:S(2)}) copy-start(bf16[24,3584]{1,0:T(8,128)(2,1)S(1)} %collective-permute-done.1.refs_3_) | copy-start | bytes 516100
  16.0 4.4 %collective-permute-start.11 = (bf16[24,3584]{1,0:T(8,128)(2,1)S(1)}, bf16[24,3584]{1,0:T(8,128)(2,1)S(1)}, u32[]{:S(2)}, u32[]{:S(2)}) collective-permute-start(bf16[24,3584]{1,0:T(8,128)(2,1)S(1)} %collective-permute-done.3.refs_5_), channel_id=1, source_target_pairs={{0,1},{1,0},{2,3},{3,2},{4,5},{5,4},{6,7},{7,6},{8,9},{9,8},{10,11... | collective-permute-start | bytes 516104 | tf_op jit(solution)/shard_map/ppermute | solution.py:148
  16.5 5.3 %copy-start.8 = (bf16[24,3584]{1,0:T(8,128)(2,1)}, bf16[24,3584]{1,0:T(8,128)(2,1)S(1)}, u32[]{:S(2)}) copy-start(bf16[24,3584]{1,0:T(8,128)(2,1)S(1)} %collective-permute-done.10.refs_12_) | copy-start | bytes 516100
  16.5 3.9 %collective-permute-start.9 = (bf16[24,3584]{1,0:T(8,128)(2,1)S(1)}, bf16[24,3584]{1,0:T(8,128)(2,1)S(1)}, u32[]{:S(2)}, u32[]{:S(2)}) collective-permute-start(bf16[24,3584]{1,0:T(8,128)(2,1)S(1)} %collective-permute-done.1.refs_3_), channel_id=1, source_target_pairs={{0,1},{1,0},{2,3},{3,2},{4,5},{5,4},{6,7},{7,6},{8,9},{9,8},{10,11... | collective-permute-start | bytes 516104 | tf_op jit(solution)/shard_map/ppermute | solution.py:148
  18.0 3.8 %copy-start.9 = (bf16[24,3584]{1,0:T(8,128)(2,1)}, bf16[24,3584]{1,0:T(8,128)(2,1)S(1)}, u32[]{:S(2)}) copy-start(bf16[24,3584]{1,0:T(8,128)(2,1)S(1)} %collective-permute-done.4.refs_6_) | copy-start | bytes 516100
  18.0 2.4 %collective-permute-start.12 = (bf16[24,3584]{1,0:T(8,128)(2,1)S(1)}, bf16[24,3584]{1,0:T(8,128)(2,1)S(1)}, u32[]{:S(2)}, u32[]{:S(2)}) collective-permute-start(bf16[24,3584]{1,0:T(8,128)(2,1)S(1)} %collective-permute-done.4.refs_6_), channel_id=1, source_target_pairs={{0,1},{1,0},{2,3},{3,2},{4,5},{5,4},{6,7},{7,6},{8,9},{9,8},{10,11... | collective-permute-start | bytes 516104 | tf_op jit(solution)/shard_map/ppermute | solution.py:148
  20.4 1.5 %copy-start.10 = (bf16[24,3584]{1,0:T(8,128)(2,1)}, bf16[24,3584]{1,0:T(8,128)(2,1)S(1)}, u32[]{:S(2)}) copy-start(bf16[24,3584]{1,0:T(8,128)(2,1)S(1)} %collective-permute-done.5.refs_7_) | copy-start | bytes 516100
  20.4 1.4 %collective-permute-start.13 = (bf16[24,3584]{1,0:T(8,128)(2,1)S(1)}, bf16[24,3584]{1,0:T(8,128)(2,1)S(1)}, u32[]{:S(2)}, u32[]{:S(2)}) collective-permute-start(bf16[24,3584]{1,0:T(8,128)(2,1)S(1)} %collective-permute-done.5.refs_7_), channel_id=1, source_target_pairs={{0,1},{1,0},{2,3},{3,2},{4,5},{5,4},{6,7},{7,6},{8,9},{9,8},{10,11... | collective-permute-start | bytes 516104 | tf_op jit(solution)/shard_map/ppermute | solution.py:148
  20.4 1.5 %copy-start.11 = (bf16[24,3584]{1,0:T(8,128)(2,1)}, bf16[24,3584]{1,0:T(8,128)(2,1)S(1)}, u32[]{:S(2)}) copy-start(bf16[24,3584]{1,0:T(8,128)(2,1)S(1)} %collective-permute-done.8.refs_10_) | copy-start | bytes 516100
  20.4 1.5 %copy-start.12 = (bf16[24,3584]{1,0:T(8,128)(2,1)}, bf16[24,3584]{1,0:T(8,128)(2,1)S(1)}, u32[]{:S(2)}) copy-start(bf16[24,3584]{1,0:T(8,128)(2,1)S(1)} %collective-permute-done.11.refs_13_) | copy-start | bytes 516100
  20.4 1.5 %copy-start.13 = (bf16[24,3584]{1,0:T(8,128)(2,1)}, bf16[24,3584]{1,0:T(8,128)(2,1)S(1)}, u32[]{:S(2)}) copy-start(bf16[24,3584]{1,0:T(8,128)(2,1)S(1)} %collective-permute-done.9.refs_11_) | copy-start | bytes 516100
  20.4 1.4 %copy-start.14 = (bf16[24,3584]{1,0:T(8,128)(2,1)}, bf16[24,3584]{1,0:T(8,128)(2,1)S(1)}, u32[]{:S(2)}) copy-start(bf16[24,3584]{1,0:T(8,128)(2,1)S(1)} %collective-permute-done.12.refs_14_) | copy-start | bytes 516100
  21.8 0.7 %copy-start.15 = (bf16[24,3584]{1,0:T(8,128)(2,1)}, bf16[24,3584]{1,0:T(8,128)(2,1)S(1)}, u32[]{:S(2)}) copy-start(bf16[24,3584]{1,0:T(8,128)(2,1)S(1)} %collective-permute-done.13.refs_15_) | copy-start | bytes 516100
  31.5 3.3 %collective-permute-start.14 = (bf16[96,7168]{1,0:T(8,128)(2,1)}, bf16[96,7168]{1,0:T(8,128)(2,1)S(1)}, u32[]{:S(2)}, u32[]{:S(2)}) collective-permute-start(bf16[96,7168]{1,0:T(8,128)(2,1)} %get-tuple-element.12), channel_id=1, source_target_pairs={{0,1},{1,0},{2,3},{3,2},{4,5},{5,4},{6,7},{7,6},{8,9},{9,8},{10,11... | collective-permute-start | bytes 4128776 | tf_op jit(solution)/shard_map/ppermute | solution.py:148
  36.6 6.5 %collective-permute-start.17 = (bf16[24,3584]{1,0:T(8,128)(2,1)S(1)}, bf16[24,3584]{1,0:T(8,128)(2,1)S(1)}, u32[]{:S(2)}, u32[]{:S(2)}) collective-permute-start(bf16[24,3584]{1,0:T(8,128)(2,1)S(1)} %get-tuple-element.15), channel_id=1, source_target_pairs={{0,2},{1,3},{2,0},{3,1},{4,6},{5,7},{6,4},{7,5},{8,10},{9,11},{10,... | collective-permute-start | bytes 516104 | tf_op jit(solution)/shard_map/ppermute | solution.py:148
  38.2 6.1 %collective-permute-start.15 = (bf16[24,3584]{1,0:T(8,128)(2,1)S(1)}, bf16[24,3584]{1,0:T(8,128)(2,1)S(1)}, u32[]{:S(2)}, u32[]{:S(2)}) collective-permute-start(bf16[24,3584]{1,0:T(8,128)(2,1)S(1)} %get-tuple-element.17), channel_id=1, source_target_pairs={{0,4},{1,5},{2,6},{3,7},{4,0},{5,1},{6,2},{7,3},{8,12},{9,13},{10,... | collective-permute-start | bytes 516104 | tf_op jit(solution)/shard_map/ppermute | solution.py:148
  44.4 9.0 %collective-permute-start.16 = (bf16[24,7168]{1,0:T(8,128)(2,1)S(1)}, bf16[24,7168]{1,0:T(8,128)(2,1)S(1)}, u32[]{:S(2)}, u32[]{:S(2)}) collective-permute-start(bf16[24,7168]{1,0:T(8,128)(2,1)S(1)} %pad_maximum_fusion), channel_id=1, source_target_pairs={{0,2},{1,3},{2,0},{3,1},{4,6},{5,7},{6,4},{7,5},{8,10},{9,11},{10,... | collective-permute-start | bytes 1032200 | tf_op jit(solution)/shard_map/ppermute | solution.py:148
  45.1 8.8 %collective-permute-start.18 = (bf16[24,7168]{1,0:T(8,128)(2,1)S(1)}, bf16[24,7168]{1,0:T(8,128)(2,1)S(1)}, u32[]{:S(2)}, u32[]{:S(2)}) collective-permute-start(bf16[24,7168]{1,0:T(8,128)(2,1)S(1)} %pad_maximum_fusion.1), channel_id=1, source_target_pairs={{0,4},{1,5},{2,6},{3,7},{4,0},{5,1},{6,2},{7,3},{8,12},{9,13},{10,... | collective-permute-start | bytes 1032200 | tf_op jit(solution)/shard_map/ppermute | solution.py:148
  53.4 0.7 %copy-start = (bf16[24,7168]{1,0:T(8,128)(2,1)}, bf16[24,7168]{1,0:T(8,128)(2,1)S(1)}, u32[]{:S(2)}) copy-start(bf16[24,7168]{1,0:T(8,128)(2,1)S(1)} %collective-permute-done.16.y_ref) | copy-start | bytes 1032196
  53.9 0.7 %copy-start.1 = (bf16[24,7168]{1,0:T(8,128)(2,1)}, bf16[24,7168]{1,0:T(8,128)(2,1)S(1)}, u32[]{:S(2)}) copy-start(bf16[24,7168]{1,0:T(8,128)(2,1)S(1)} %collective-permute-done.18.z_ref) | copy-start | bytes 1032196

commit v2 on v0

--- a/solution.py
+++ b/solution.py
@@ -1,10 +1,18 @@
+import functools
+
 import jax
 import jax.numpy as jnp
 from jax import lax
+from jax.experimental import pallas as pl
+from jax.experimental.pallas import tpu as pltpu
 from jax.sharding import PartitionSpec as P
 
 PIECES = 8
 CAP = 12
+
+
+def within(mib):
+    return pltpu.CompilerParams(vmem_limit_bytes=mib * 2**20)
 
 
 def expert_rows(arrived, gate_part, up_part, down_part):
@@ -16,7 +24,7 @@
     return result.reshape(arrived.shape[:-1] + (down_part.shape[1],))
 
 
-def on_device(
+def any_copies(
     tokens, expert_ids, replica, gate_weights, slot_table, gate_pieces, up_pieces, down_pieces
 ):
     devices = lax.axis_size("expert")
@@ -56,6 +64,214 @@
     return total.astype(jnp.bfloat16)
 
 
+def slots_of(ids, rep, table):
+    experts = lax.broadcasted_iota(jnp.int32, table.shape, 1)
+    here = table < 2
+    first = jnp.sum(jnp.where(here, table, 0)[0:1], axis=1, keepdims=True)
+    hosted = jnp.sum(jnp.where(here, experts, 0)[0:1], axis=1, keepdims=True)
+    hit = ids == hosted
+    copy = jnp.where(rep == 0, first, 1 - first)
+    count = ids.shape[1]
+    to = [jnp.sum(jnp.where(hit & (copy == c), 1.0, 0.0), axis=0, keepdims=True) for c in range(2)]
+    earlier = (
+        lax.broadcasted_iota(jnp.int32, (count, count), 0)
+        < lax.broadcasted_iota(jnp.int32, (count, count), 1)
+    ).astype(jnp.float32)
+    slot = jnp.full((1, count), -1, jnp.int32)
+    for c in range(2):
+        routed = jnp.broadcast_to(to[c], (8, count))
+        position = jnp.dot(routed, earlier, preferred_element_type=jnp.float32)[0:1]
+        position = position.astype(jnp.int32)
+        keep = (to[c] > 0.5) & (position < CAP)
+        slot = jnp.where(keep, position + c * CAP, slot)
+    return slot, hit
+
+
+def copies_of(refs, sems):
+    copies = [pltpu.make_async_copy(s, t, sems.at[i]) for i, (s, t) in enumerate(refs)]
+    for copy in copies:
+        copy.start()
+    return copies
+
+
+def pick_kernel(
+    tok_hbm, ids_hbm, rep_hbm, table_hbm, w_hbm, out_ref, spread_ref,
+    tok_ref, ids_ref, rep_ref, table_ref, w_ref, sems,
+):
+    copies = copies_of(
+        [
+            (ids_hbm, ids_ref),
+            (rep_hbm, rep_ref),
+            (table_hbm, table_ref),
+            (w_hbm, w_ref),
+            (tok_hbm, tok_ref),
+        ],
+        sems,
+    )
+    for copy in copies[:4]:
+        copy.wait()
+    slot, hit = slots_of(ids_ref[...], rep_ref[...], table_ref[...])
+    weight = jnp.sum(jnp.where(hit, w_ref[...], 0.0), axis=0, keepdims=True)
+    count = slot.shape[1]
+    chosen = lax.broadcasted_iota(jnp.int32, (2 * CAP, count), 0) == slot
+    spread_ref[...] = jnp.where(chosen, weight, 0.0)
+    copies[4].wait()
+    out_ref[...] = jnp.dot(
+        chosen.astype(jnp.bfloat16), tok_ref[...], preferred_element_type=jnp.float32
+    ).astype(jnp.bfloat16)
+
+
+def activation(gate, up):
+    return (gate / (1.0 + jnp.exp(-gate)) * up).astype(jnp.bfloat16)
+
+
+def load_kernel(gate_hbm, up_hbm, down_hbm, gate_ref, up_ref, down_ref, sems):
+    steps = sems.shape[1]
+    pairs = []
+    for source, target in ((gate_hbm, gate_ref), (up_hbm, up_ref), (down_hbm, down_ref)):
+        step = source.shape[0] // steps
+        for i in range(steps):
+            part = pl.ds(i * step, step)
+            pairs.append((source.at[part], target.at[part]))
+    copies = [
+        pltpu.make_async_copy(s, t, sems.at[i // steps, i % steps])
+        for i, (s, t) in enumerate(pairs)
+    ]
+    for copy in copies:
+        copy.start()
+    for copy in copies:
+        copy.wait()
+
+
+def hold_kernel(*refs):
+    pass
+
+
+def expert_kernel(*refs):
+    gate_ref, up_ref, down_ref, mine_ref, other_ref, x_all = refs[-6:]
+    rows = refs[0].shape[0]
+    for i, ref in enumerate(refs[:-6]):
+        x_all[i * rows : (i + 1) * rows] = ref[...]
+    x = x_all[...]
+    gate = jnp.dot(x, gate_ref[...], preferred_element_type=jnp.float32)
+    up = jnp.dot(x, up_ref[...], preferred_element_type=jnp.float32)
+    hidden = activation(gate, up)
+    out = jnp.dot(hidden, down_ref[...], preferred_element_type=jnp.float32).astype(jnp.bfloat16)
+    mine_ref[...] = out[: mine_ref.shape[0]]
+    other_ref[...] = out[mine_ref.shape[0] :]
+
+
+def combine_kernel(mine_ref, met_ref, first_ref, second_ref, spread_ref, out_ref):
+    spread = spread_ref[...]
+    spread_hi = spread.astype(jnp.bfloat16)
+    spread_lo = (spread - spread_hi.astype(jnp.float32)).astype(jnp.bfloat16)
+    dims = (((0,), (0,)), ((), ()))
+    dot = functools.partial(
+        lax.dot_general, dimension_numbers=dims, preferred_element_type=jnp.float32
+    )
+    rows = first_ref.shape[0]
+    total = mine_ref[:rows].astype(jnp.float32) + met_ref[:rows].astype(jnp.float32)
+    for ref in (first_ref, second_ref):
+        total = total + ref[...].astype(jnp.float32)
+    total_hi = total.astype(jnp.bfloat16)
+    total_lo = (total - total_hi.astype(jnp.float32)).astype(jnp.bfloat16)
+    out = dot(spread_hi, total_hi) + (dot(spread_hi, total_lo) + dot(spread_lo, total_hi))
+    out_ref[...] = out.astype(jnp.bfloat16)
+
+
+def two_copies(
+    tokens, expert_ids, replica, gate_weights, slot_table, gate_pieces, up_pieces, down_pieces
+):
+    devices = lax.axis_size("expert")
+    count, width = tokens.shape
+    rows = 2 * CAP
+    hidden = gate_pieces.shape[2]
+    bf16, f32 = jnp.bfloat16, jnp.float32
+    in_hbm = pl.BlockSpec(memory_space=pltpu.HBM)
+    in_vmem = pl.BlockSpec(memory_space=pltpu.VMEM)
+
+    def partner(a):
+        return lax.ppermute(a, "expert", [(i, i ^ 1) for i in range(devices)])
+
+    def cross(a):
+        return lax.ppermute(a, "expert", [(i, i ^ (4 if i % 2 else 2)) for i in range(devices)])
+
+    def cross_back(a):
+        return lax.ppermute(a, "expert", [(i, i ^ (2 if i % 2 else 4)) for i in range(devices)])
+
+    def add(a, b):
+        return (a.astype(f32) + b.astype(f32)).astype(bf16)
+
+    def cost(total):
+        return pl.CostEstimate(
+            flops=6 * total * width * hidden, bytes_accessed=6 * width * hidden, transcendentals=0
+        )
+
+    small = [expert_ids.T, replica.T, slot_table.T, gate_weights.T]
+    own, spread = pl.pallas_call(
+        pick_kernel,
+        out_shape=[
+            jax.ShapeDtypeStruct((rows, width), bf16),
+            jax.ShapeDtypeStruct((rows, count), f32),
+        ],
+        in_specs=[in_hbm] * 5,
+        scratch_shapes=[pltpu.VMEM(a.shape, a.dtype) for a in [tokens] + small]
+        + [pltpu.SemaphoreType.DMA((5,))],
+        compiler_params=within(56),
+    )(tokens, *small)
+    gate, up, down = pl.pallas_call(
+        load_kernel,
+        out_shape=[
+            jax.ShapeDtypeStruct(a.shape[1:], bf16) for a in (gate_pieces, up_pieces, down_pieces)
+        ],
+        in_specs=[in_hbm] * 3,
+        out_specs=[in_vmem] * 3,
+        scratch_shapes=[pltpu.SemaphoreType.DMA((3, 8))],
+        compiler_params=within(40),
+        cost_estimate=cost(2 * rows),
+    )(gate_pieces[0], up_pieces[0], down_pieces[0])
+
+    def after(done, *arrays):
+        anywhere = pl.BlockSpec(memory_space=pl.ANY)
+        return pl.pallas_call(
+            hold_kernel,
+            out_shape=[jax.ShapeDtypeStruct(a.shape, a.dtype) for a in arrays],
+            in_specs=[anywhere] * (1 + len(arrays)),
+            out_specs=[anywhere] * len(arrays),
+            input_output_aliases={1 + i: i for i in range(len(arrays))},
+            compiler_params=within(1),
+        )(done, *arrays)
+
+    def experts(blocks):
+        total = 2 * rows * len(blocks)
+        return pl.pallas_call(
+            expert_kernel,
+            out_shape=[jax.ShapeDtypeStruct((total // 2, width), bf16)] * 2,
+            scratch_shapes=[pltpu.VMEM((total, width), bf16)],
+            compiler_params=within(24),
+            cost_estimate=cost(total),
+        )(*blocks, *[partner(a) for a in blocks], gate, up, down)
+
+    (near,) = after(gate, cross(own))
+    far = cross_back(near)
+    side = cross_back(own)
+    far_mine, far_other = experts([far])
+    far_met = partner(far_other)
+    (side,) = after(far_mine, side)
+    mine, other = experts([own, near, side])
+    met = partner(other)
+    block = [slice(i * rows, (i + 1) * rows) for i in range(3)]
+    passing = cross_back(add(far_mine, far_met))
+    got_side = cross_back(add(mine[block[2]], met[block[2]]))
+    to_near = mine[block[1]].astype(f32) + met[block[1]].astype(f32) + passing.astype(f32)
+    got_near = cross(to_near.astype(bf16))
+    return pl.pallas_call(
+        combine_kernel,
+        out_shape=jax.ShapeDtypeStruct((count, width), bf16),
+        compiler_params=within(24),
+    )(mine, met, got_side, got_near, spread)
+
+
 def solution(mesh):
     placed = (
         P(("groups", "expert"), None),
@@ -68,7 +284,7 @@
         P(("groups", "expert"), None, None),
     )
     return jax.shard_map(
-        on_device,
+        two_copies if mesh.shape["expert"] == 2 * PIECES else any_copies,
         mesh=mesh,
         in_specs=placed,
         out_specs=P(("groups", "expert"), None),

time: 201 us -> 48.8 us (0.24)
  the two profiles are of different devices: /device:TPU:13 before, /device:TPU:0 now
where the time goes in v2:
time: 48.8 us; the launch traced here: 48.6 us
  waiting for transfers between devices  22.4 us (46%)
  starting transfers between devices  14 us (29%)
  Pallas kernels  11.8 us (24%)
    ppermute x4, waiting for transfers between devices, cross_back(): lax.ppermute(a, 'expert', [(i, i ^ (2 if i % 2 else 4)) for i in range(de...  13.1 us
    ppermute x2, waiting for transfers between devices, cross(): lax.ppermute(a, 'expert', [(i, i ^ (4 if i % 2 else 2)) for i in range(de...  8.2 us
    ppermute x4, starting transfers between devices, cross_back(): lax.ppermute(a, 'expert', [(i, i ^ (2 if i % 2 else 4)) for i in range(de...  7.77 us
    ppermute x2, starting transfers between devices, cross(): lax.ppermute(a, 'expert', [(i, i ^ (4 if i % 2 else 2)) for i in range(de...  5.05 us
    pallas_call x1, Pallas kernels, two_copies(): pl.pallas_call(load_kernel, out_shape=[jax.ShapeDtypeStruct(a.shape[1:],...  4.32 us
    pallas_call x2, Pallas kernels, experts(): pl.pallas_call(expert_kernel, out_shape=[jax.ShapeDtypeStruct((total // 2...  4 us
    pallas_call x1, Pallas kernels, two_copies(): pl.pallas_call(pick_kernel, out_shape=[jax.ShapeDtypeStruct((rows, width)...  2.11 us
    pallas_call x1, Pallas kernels, two_copies(): pl.pallas_call(combine_kernel, out_shape=jax.ShapeDtypeStruct((count, wid...  1.35 us
  transfers between devices with their start and end apart: 12, of which 6 were waited for; matrix products, arithmetic and copies ran while one was open for 0% of the time, Pallas kernels for 17%

profile of v2, /device:TPU:0, one launch (start us, length us, event | category | flops | bytes accessed | tf_op | source)
XLA Modules:
  0.0 48.6 jit_solution(1986777818245813912)
XLA Ops:
  0.0 2.1 %shard_map.82 = (bf16[24,7168]{1,0:T(8,128)(2,1)}, f32[24,32]{1,0:T(8,128)}) custom-call(bf16[32,7168]{1,0:T(8,128)(2,1)} %tok_hbm.1, s32[8,32]{1,0:T(8,128)} %bitcast.10, s32[8,32]{1,0:T(8,128)} %bitcast.11, s32[2,256]{1,0:T(2,128)} %bitcast.13, f32[8,32]{1,0:T(8,128)} %bitcast.12), custom_call_target="tpu_custom_call" | custom-call | tf_op jit(solution)/shard_map/pallas_call | solution.py:211
  2.1 3.0 %collective-permute-start = (bf16[24,7168]{1,0:T(8,128)(2,1)}, bf16[24,7168]{1,0:T(8,128)(2,1)S(1)}, u32[]{:S(2)}, u32[]{:S(2)}) collective-permute-start(bf16[24,7168]{1,0:T(8,128)(2,1)} %get-tuple-element.14.refs_0_), channel_id=1, source_target_pairs={{0,2},{1,5},{2,0},{3,7},{4,6},{5,1},{6,4},{7,3},{8,10},{9,13},{10,... | collective-permute-start | bytes 1032200 | tf_op jit(solution)/shard_map/ppermute | solution.py:197
  5.2 4.3 %shard_map.83 = (bf16[7168,256]{1,0:T(8,128)(2,1)S(1)}, bf16[7168,256]{1,0:T(8,128)(2,1)S(1)}, bf16[256,7168]{1,0:T(8,128)(2,1)S(1)}) custom-call(bf16[7168,256]{1,0:T(8,128)(2,1)} %bitcast.7, bf16[7168,256]{1,0:T(8,128)(2,1)} %bitcast.8, bf16[256,7168]{1,0:T(8,128)(2,1)} %bitcast.9), custom_call_target="tpu_custom_call" | custom-call | flops 528482304 | bytes 11010048 | tf_op jit(solution)/shard_map/pallas_call | solution.py:222
  9.5 0.0 copy-start
  9.5 1.1 %collective-permute-done.refs_1_ = bf16[24,7168]{1,0:T(8,128)(2,1)S(1)} collective-permute-done((bf16[24,7168]{1,0:T(8,128)(2,1)}, bf16[24,7168]{1,0:T(8,128)(2,1)S(1)}, u32[]{:S(2)}, u32[]{:S(2)}) %collective-permute-start) | collective-permute-done | bytes 344096 | tf_op jit(solution)/shard_map/ppermute | solution.py:197
  10.6 2.1 %collective-permute-start.1 = (bf16[24,7168]{1,0:T(8,128)(2,1)S(1)}, bf16[24,7168]{1,0:T(8,128)(2,1)S(1)}, u32[]{:S(2)}, u32[]{:S(2)}) collective-permute-start(bf16[24,7168]{1,0:T(8,128)(2,1)S(1)} %shard_map.84.refs_1_), channel_id=1, source_target_pairs={{0,4},{1,3},{2,6},{3,1},{4,0},{5,7},{6,2},{7,5},{8,12},{9,11},{10,... | collective-permute-start | bytes 1032200 | tf_op jit(solution)/shard_map/ppermute | solution.py:200
  12.7 5.2 %collective-permute-done.1.refs_0_ = bf16[24,7168]{1,0:T(8,128)(2,1)S(1)} collective-permute-done((bf16[24,7168]{1,0:T(8,128)(2,1)S(1)}, bf16[24,7168]{1,0:T(8,128)(2,1)S(1)}, u32[]{:S(2)}, u32[]{:S(2)}) %collective-permute-start.1) | collective-permute-done | bytes 344096 | tf_op jit(solution)/shard_map/ppermute | solution.py:200
  17.9 0.0 collective-permute-start.2
  17.9 0.0 copy-done
  17.9 2.0 %collective-permute-start.3 = (bf16[24,7168]{1,0:T(8,128)(2,1)S(1)}, bf16[24,7168]{1,0:T(8,128)(2,1)S(1)}, u32[]{:S(2)}, u32[]{:S(2)}) collective-permute-start(bf16[24,7168]{1,0:T(8,128)(2,1)S(1)} %copy-done), channel_id=1, source_target_pairs={{0,4},{1,3},{2,6},{3,1},{4,0},{5,7},{6,2},{7,5},{8,12},{9,11},{10,... | collective-permute-start | bytes 1032200 | tf_op jit(solution)/shard_map/ppermute | solution.py:200
  19.9 0.2 collective-permute-start.4
  20.1 0.3 collective-permute-start.5
  20.4 0.0 collective-permute-done.2.refs_1_
  20.4 2.1 %shard_map.85 = (bf16[24,7168]{1,0:T(8,128)(2,1)S(1)}, bf16[24,7168]{1,0:T(8,128)(2,1)S(1)}) custom-call(bf16[24,7168]{1,0:T(8,128)(2,1)S(1)} %collective-permute-done.1.refs_0_, bf16[24,7168]{1,0:T(8,128)(2,1)S(1)} %collective-permute-done.2.refs_1_, bf16[7168,256]{1,0:T(8,128)(2,1)S(1)} %get-tuple-element.15.refs_0_.refs_2_.refs_6_, ...), custom_call_target="tpu_custom_call" | custom-call | flops 528482304 | bytes 11010048 | tf_op jit(solution)/shard_map/pallas_call | solution.py:247
  22.5 2.6 %collective-permute-done.3.refs_1_ = bf16[24,7168]{1,0:T(8,128)(2,1)S(1)} collective-permute-done((bf16[24,7168]{1,0:T(8,128)(2,1)S(1)}, bf16[24,7168]{1,0:T(8,128)(2,1)S(1)}, u32[]{:S(2)}, u32[]{:S(2)}) %collective-permute-start.3) | collective-permute-done | bytes 344096 | tf_op jit(solution)/shard_map/ppermute | solution.py:200
  25.2 0.0 collective-permute-start.6
  25.2 0.0 copy-start.1
  25.2 0.5 %collective-permute-start.9 = (bf16[24,7168]{1,0:T(8,128)(2,1)S(1)}, bf16[24,7168]{1,0:T(8,128)(2,1)S(1)}, u32[]{:S(2)}, u32[]{:S(2)}) collective-permute-start(bf16[24,7168]{1,0:T(8,128)(2,1)S(1)} %get-tuple-element.21), channel_id=1, source_target_pairs={{0,1},{1,0},{2,3},{3,2},{4,5},{5,4},{6,7},{7,6},{8,9},{9,8},{10,11... | collective-permute-start | bytes 1032200 | tf_op jit(solution)/shard_map/ppermute | solution.py:194
  25.7 0.0 collective-permute-done.4.refs_3_
  25.7 0.0 collective-permute-done.5.refs_4_
  25.7 1.1 %collective-permute-done.6.refs_5_ = bf16[24,7168]{1,0:T(8,128)(2,1)S(1)} collective-permute-done((bf16[24,7168]{1,0:T(8,128)(2,1)S(1)}, bf16[24,7168]{1,0:T(8,128)(2,1)S(1)}, u32[]{:S(2)}, u32[]{:S(2)}) %collective-permute-start.6) | collective-permute-done | bytes 344096 | tf_op jit(solution)/shard_map/ppermute | solution.py:194
  26.8 1.9 %shard_map.87 = (bf16[72,7168]{1,0:T(8,128)(2,1)S(1)}, bf16[72,7168]{1,0:T(8,128)(2,1)S(1)}) custom-call(bf16[24,7168]{1,0:T(8,128)(2,1)S(1)} %copy-done, bf16[24,7168]{1,0:T(8,128)(2,1)S(1)} %shard_map.84.refs_1_, bf16[24,7168]{1,0:T(8,128)(2,1)S(1)} %shard_map.86.refs_2_, bf16[24,7168]{1,0:T(8,128)(2,1)S(1)} %collective-permute-done.4.refs_3_, ...), custom_call_target="tpu_custom_call" | custom-call | flops 1585446912 | bytes 11010048 | tf_op jit(solution)/shard_map/pallas_call | solution.py:247
  28.7 0.2 collective-permute-start.7
  28.9 0.0 collective-permute-done.9
  28.9 0.1 add_convert_fusion.1
  29.0 2.1 %collective-permute-start.10 = (bf16[24,7168]{1,0:T(8,128)(2,1)S(1)}, bf16[24,7168]{1,0:T(8,128)(2,1)S(1)}, u32[]{:S(2)}, u32[]{:S(2)}) collective-permute-start(bf16[24,7168]{1,0:T(8,128)(2,1)S(1)} %add_convert_fusion.1), channel_id=1, source_target_pairs={{0,4},{1,3},{2,6},{3,1},{4,0},{5,7},{6,2},{7,5},{8,12},{9,11},{10,... | collective-permute-start | bytes 1032200 | tf_op jit(solution)/shard_map/ppermute | solution.py:200
  31.1 5.2 %collective-permute-done.10 = bf16[24,7168]{1,0:T(8,128)(2,1)S(1)} collective-permute-done((bf16[24,7168]{1,0:T(8,128)(2,1)S(1)}, bf16[24,7168]{1,0:T(8,128)(2,1)S(1)}, u32[]{:S(2)}, u32[]{:S(2)}) %collective-permute-start.10) | collective-permute-done | bytes 344096 | tf_op jit(solution)/shard_map/ppermute | solution.py:200
  36.3 0.0 collective-permute-done.7.met_ref
  36.3 0.2 add_convert_fusion
  36.5 2.0 %collective-permute-start.11 = (bf16[24,7168]{1,0:T(8,128)(2,1)S(1)}, bf16[24,7168]{1,0:T(8,128)(2,1)S(1)}, u32[]{:S(2)}, u32[]{:S(2)}) collective-permute-start(bf16[24,7168]{1,0:T(8,128)(2,1)S(1)} %get-tuple-element.23), channel_id=1, source_target_pairs={{0,2},{1,5},{2,0},{3,7},{4,6},{5,1},{6,4},{7,3},{8,10},{9,13},{10,... | collective-permute-start | bytes 1032200 | tf_op jit(solution)/shard_map/ppermute | solution.py:197
  38.6 1.6 %collective-permute-start.8 = (bf16[24,7168]{1,0:T(8,128)(2,1)S(1)}, bf16[24,7168]{1,0:T(8,128)(2,1)S(1)}, u32[]{:S(2)}, u32[]{:S(2)}) collective-permute-start(bf16[24,7168]{1,0:T(8,128)(2,1)S(1)} %get-tuple-element.24), channel_id=1, source_target_pairs={{0,4},{1,3},{2,6},{3,1},{4,0},{5,7},{6,2},{7,5},{8,12},{9,11},{10,... | collective-permute-start | bytes 1032200 | tf_op jit(solution)/shard_map/ppermute | solution.py:200
  40.1 7.1 %collective-permute-done.11.second_ref = bf16[24,7168]{1,0:T(8,128)(2,1)S(1)} collective-permute-done((bf16[24,7168]{1,0:T(8,128)(2,1)S(1)}, bf16[24,7168]{1,0:T(8,128)(2,1)S(1)}, u32[]{:S(2)}, u32[]{:S(2)}) %collective-permute-start.11) | collective-permute-done | bytes 344096 | tf_op jit(solution)/shard_map/ppermute | solution.py:197
  47.3 0.0 collective-permute-done.8.first_ref
  47.3 0.0 copy-done.1
  47.3 1.3 %shard_map.88 = bf16[32,7168]{1,0:T(8,128)(2,1)} custom-call(bf16[72,7168]{1,0:T(8,128)(2,1)S(1)} %get-tuple-element.19.mine_ref, bf16[72,7168]{1,0:T(8,128)(2,1)S(1)} %collective-permute-done.7.met_ref, bf16[24,7168]{1,0:T(8,128)(2,1)S(1)} %collective-permute-done.8.first_ref, bf16[24,7168]{1,0:T(8,128)(2,1)S(1)} %collective-permute-done.11.second_ref, ...), custom_call_target="tpu_custom_call" | custom-call | tf_op jit(solution)/shard_map/pallas_call | solution.py:268
  (2 shorter events, 0.0 us)
Async XLA Ops:
  2.1 8.5 %collective-permute-start = (bf16[24,7168]{1,0:T(8,128)(2,1)}, bf16[24,7168]{1,0:T(8,128)(2,1)S(1)}, u32[]{:S(2)}, u32[]{:S(2)}) collective-permute-start(bf16[24,7168]{1,0:T(8,128)(2,1)} %get-tuple-element.14.refs_0_), channel_id=1, source_target_pairs={{0,2},{1,5},{2,0},{3,7},{4,6},{5,1},{6,4},{7,3},{8,10},{9,13},{10,... | collective-permute-start | bytes 1032200 | tf_op jit(solution)/shard_map/ppermute | solution.py:197
  9.5 8.4 %copy-start = (bf16[24,7168]{1,0:T(8,128)(2,1)S(1)}, bf16[24,7168]{1,0:T(8,128)(2,1)}, u32[]{:S(2)}) copy-start(bf16[24,7168]{1,0:T(8,128)(2,1)} %get-tuple-element.14.refs_0_) | copy-start | bytes 1032196
  10.6 7.3 %collective-permute-start.1 = (bf16[24,7168]{1,0:T(8,128)(2,1)S(1)}, bf16[24,7168]{1,0:T(8,128)(2,1)S(1)}, u32[]{:S(2)}, u32[]{:S(2)}) collective-permute-start(bf16[24,7168]{1,0:T(8,128)(2,1)S(1)} %shard_map.84.refs_1_), channel_id=1, source_target_pairs={{0,4},{1,3},{2,6},{3,1},{4,0},{5,7},{6,2},{7,5},{8,12},{9,11},{10,... | collective-permute-start | bytes 1032200 | tf_op jit(solution)/shard_map/ppermute | solution.py:200
  17.9 2.5 %collective-permute-start.2 = (bf16[24,7168]{1,0:T(8,128)(2,1)S(1)}, bf16[24,7168]{1,0:T(8,128)(2,1)S(1)}, u32[]{:S(2)}, u32[]{:S(2)}) collective-permute-start(bf16[24,7168]{1,0:T(8,128)(2,1)S(1)} %collective-permute-done.1.refs_0_), channel_id=1, source_target_pairs={{0,1},{1,0},{2,3},{3,2},{4,5},{5,4},{6,7},{7,6},{8,9},{9,8},{10,11... | collective-permute-start | bytes 1032200 | tf_op jit(solution)/shard_map/ppermute | solution.py:194
  17.9 7.3 %collective-permute-start.3 = (bf16[24,7168]{1,0:T(8,128)(2,1)S(1)}, bf16[24,7168]{1,0:T(8,128)(2,1)S(1)}, u32[]{:S(2)}, u32[]{:S(2)}) collective-permute-start(bf16[24,7168]{1,0:T(8,128)(2,1)S(1)} %copy-done), channel_id=1, source_target_pairs={{0,4},{1,3},{2,6},{3,1},{4,0},{5,7},{6,2},{7,5},{8,12},{9,11},{10,... | collective-permute-start | bytes 1032200 | tf_op jit(solution)/shard_map/ppermute | solution.py:200
  19.9 5.7 %collective-permute-start.4 = (bf16[24,7168]{1,0:T(8,128)(2,1)S(1)}, bf16[24,7168]{1,0:T(8,128)(2,1)S(1)}, u32[]{:S(2)}, u32[]{:S(2)}) collective-permute-start(bf16[24,7168]{1,0:T(8,128)(2,1)S(1)} %copy-done), channel_id=1, source_target_pairs={{0,1},{1,0},{2,3},{3,2},{4,5},{5,4},{6,7},{7,6},{8,9},{9,8},{10,11... | collective-permute-start | bytes 1032200 | tf_op jit(solution)/shard_map/ppermute | solution.py:194
  20.1 5.6 %collective-permute-start.5 = (bf16[24,7168]{1,0:T(8,128)(2,1)S(1)}, bf16[24,7168]{1,0:T(8,128)(2,1)S(1)}, u32[]{:S(2)}, u32[]{:S(2)}) collective-permute-start(bf16[24,7168]{1,0:T(8,128)(2,1)S(1)} %shard_map.84.refs_1_), channel_id=1, source_target_pairs={{0,1},{1,0},{2,3},{3,2},{4,5},{5,4},{6,7},{7,6},{8,9},{9,8},{10,11... | collective-permute-start | bytes 1032200 | tf_op jit(solution)/shard_map/ppermute | solution.py:194
  25.2 1.7 %collective-permute-start.6 = (bf16[24,7168]{1,0:T(8,128)(2,1)S(1)}, bf16[24,7168]{1,0:T(8,128)(2,1)S(1)}, u32[]{:S(2)}, u32[]{:S(2)}) collective-permute-start(bf16[24,7168]{1,0:T(8,128)(2,1)S(1)} %shard_map.86.refs_2_), channel_id=1, source_target_pairs={{0,1},{1,0},{2,3},{3,2},{4,5},{5,4},{6,7},{7,6},{8,9},{9,8},{10,11... | collective-permute-start | bytes 1032200 | tf_op jit(solution)/shard_map/ppermute | solution.py:194
  25.2 22.1 %copy-start.1 = (f32[24,32]{1,0:T(8,128)S(1)}, f32[24,32]{1,0:T(8,128)}, u32[]{:S(2)}) copy-start(f32[24,32]{1,0:T(8,128)} %get-tuple-element.22.spread_ref) | copy-start | bytes 9220
  25.2 3.8 %collective-permute-start.9 = (bf16[24,7168]{1,0:T(8,128)(2,1)S(1)}, bf16[24,7168]{1,0:T(8,128)(2,1)S(1)}, u32[]{:S(2)}, u32[]{:S(2)}) collective-permute-start(bf16[24,7168]{1,0:T(8,128)(2,1)S(1)} %get-tuple-element.21), channel_id=1, source_target_pairs={{0,1},{1,0},{2,3},{3,2},{4,5},{5,4},{6,7},{7,6},{8,9},{9,8},{10,11... | collective-permute-start | bytes 1032200 | tf_op jit(solution)/shard_map/ppermute | solution.py:194
  28.7 7.6 %collective-permute-start.7 = (bf16[72,7168]{1,0:T(8,128)(2,1)S(1)}, bf16[72,7168]{1,0:T(8,128)(2,1)S(1)}, u32[]{:S(2)}, u32[]{:S(2)}) collective-permute-start(bf16[72,7168]{1,0:T(8,128)(2,1)S(1)} %get-tuple-element.20), channel_id=1, source_target_pairs={{0,1},{1,0},{2,3},{3,2},{4,5},{5,4},{6,7},{7,6},{8,9},{9,8},{10,11... | collective-permute-start | bytes 3096584 | tf_op jit(solution)/shard_map/ppermute | solution.py:194
  29.0 7.3 %collective-permute-start.10 = (bf16[24,7168]{1,0:T(8,128)(2,1)S(1)}, bf16[24,7168]{1,0:T(8,128)(2,1)S(1)}, u32[]{:S(2)}, u32[]{:S(2)}) collective-permute-start(bf16[24,7168]{1,0:T(8,128)(2,1)S(1)} %add_convert_fusion.1), channel_id=1, source_target_pairs={{0,4},{1,3},{2,6},{3,1},{4,0},{5,7},{6,2},{7,5},{8,12},{9,11},{10,... | collective-permute-start | bytes 1032200 | tf_op jit(solution)/shard_map/ppermute | solution.py:200
  36.5 10.7 %collective-permute-start.11 = (bf16[24,7168]{1,0:T(8,128)(2,1)S(1)}, bf16[24,7168]{1,0:T(8,128)(2,1)S(1)}, u32[]{:S(2)}, u32[]{:S(2)}) collective-permute-start(bf16[24,7168]{1,0:T(8,128)(2,1)S(1)} %get-tuple-element.23), channel_id=1, source_target_pairs={{0,2},{1,5},{2,0},{3,7},{4,6},{5,1},{6,4},{7,3},{8,10},{9,13},{10,... | collective-permute-start | bytes 1032200 | tf_op jit(solution)/shard_map/ppermute | solution.py:197
  38.6 8.7 %collective-permute-start.8 = (bf16[24,7168]{1,0:T(8,128)(2,1)S(1)}, bf16[24,7168]{1,0:T(8,128)(2,1)S(1)}, u32[]{:S(2)}, u32[]{:S(2)}) collective-permute-start(bf16[24,7168]{1,0:T(8,128)(2,1)S(1)} %get-tuple-element.24), channel_id=1, source_target_pairs={{0,4},{1,3},{2,6},{3,1},{4,0},{5,7},{6,2},{7,5},{8,12},{9,11},{10,... | collective-permute-start | bytes 1032200 | tf_op jit(solution)/shard_map/ppermute | solution.py:200

commit v3 on v2

--- a/solution.py
+++ b/solution.py
@@ -147,11 +147,11 @@
     pass
 
 
-def expert_kernel(*refs):
+def expert_kernel(parts, *refs):
     gate_ref, up_ref, down_ref, mine_ref, other_ref, x_all = refs[-6:]
-    rows = refs[0].shape[0]
-    for i, ref in enumerate(refs[:-6]):
-        x_all[i * rows : (i + 1) * rows] = ref[...]
+    rows = x_all.shape[0] // len(parts)
+    for i, (which, block) in enumerate(parts):
+        x_all[i * rows : (i + 1) * rows] = refs[which][block * rows : (block + 1) * rows]
     x = x_all[...]
     gate = jnp.dot(x, gate_ref[...], preferred_element_type=jnp.float32)
     up = jnp.dot(x, up_ref[...], preferred_element_type=jnp.float32)
@@ -161,7 +161,17 @@
     other_ref[...] = out[mine_ref.shape[0] :]
 
 
-def combine_kernel(mine_ref, met_ref, first_ref, second_ref, spread_ref, out_ref):
+def add_kernel(mine_ref, passing_ref, out_ref):
+    out_ref[...] = mine_ref[...].astype(jnp.float32) + passing_ref[...].astype(jnp.float32)
+
+
+def settle_kernel(mine_ref, met_ref, side_ref, out_ref):
+    rows = out_ref.shape[0]
+    total = mine_ref[:rows].astype(jnp.float32) + met_ref[:rows].astype(jnp.float32)
+    out_ref[...] = total + side_ref[...].astype(jnp.float32)
+
+
+def combine_kernel(settled_ref, near_ref, spread_ref, out_ref):
     spread = spread_ref[...]
     spread_hi = spread.astype(jnp.bfloat16)
     spread_lo = (spread - spread_hi.astype(jnp.float32)).astype(jnp.bfloat16)
@@ -169,10 +179,7 @@
     dot = functools.partial(
         lax.dot_general, dimension_numbers=dims, preferred_element_type=jnp.float32
     )
-    rows = first_ref.shape[0]
-    total = mine_ref[:rows].astype(jnp.float32) + met_ref[:rows].astype(jnp.float32)
-    for ref in (first_ref, second_ref):
-        total = total + ref[...].astype(jnp.float32)
+    total = settled_ref[...] + near_ref[...].astype(jnp.float32)
     total_hi = total.astype(jnp.bfloat16)
     total_lo = (total - total_hi.astype(jnp.float32)).astype(jnp.bfloat16)
     out = dot(spread_hi, total_hi) + (dot(spread_hi, total_lo) + dot(spread_lo, total_hi))
@@ -198,6 +205,9 @@
 
     def cross_back(a):
         return lax.ppermute(a, "expert", [(i, i ^ (2 if i % 2 else 4)) for i in range(devices)])
+
+    def diagonal(a):
+        return lax.ppermute(a, "expert", [(i, i ^ 6) for i in range(devices)])
 
     def add(a, b):
         return (a.astype(f32) + b.astype(f32)).astype(bf16)
@@ -242,34 +252,64 @@
             compiler_params=within(1),
         )(done, *arrays)
 
-    def experts(blocks):
-        total = 2 * rows * len(blocks)
+    def early(array, micros):
+        anywhere = pl.BlockSpec(memory_space=pl.ANY)
         return pl.pallas_call(
-            expert_kernel,
+            hold_kernel,
+            out_shape=jax.ShapeDtypeStruct(array.shape, array.dtype),
+            in_specs=[anywhere],
+            out_specs=anywhere,
+            input_output_aliases={0: 0},
+            compiler_params=within(1),
+            cost_estimate=pl.CostEstimate(
+                flops=micros * 10**9, bytes_accessed=0, transcendentals=0
+            ),
+        )(array)
+
+    def experts(parts, *arrays):
+        total = rows * len(parts)
+        return pl.pallas_call(
+            functools.partial(expert_kernel, parts),
             out_shape=[jax.ShapeDtypeStruct((total // 2, width), bf16)] * 2,
             scratch_shapes=[pltpu.VMEM((total, width), bf16)],
             compiler_params=within(24),
             cost_estimate=cost(total),
-        )(*blocks, *[partner(a) for a in blocks], gate, up, down)
-
-    (near,) = after(gate, cross(own))
+        )(*arrays, gate, up, down)
+
+    twice = ((0, 0), (1, 0))
+    near, = after(gate, cross(own))
     far = cross_back(near)
     side = cross_back(own)
-    far_mine, far_other = experts([far])
-    far_met = partner(far_other)
-    (side,) = after(far_mine, side)
-    mine, other = experts([own, near, side])
+    mine, other = experts(((0, 0), (1, 0), (2, 0), (3, 0)), own, near, partner(own), partner(near))
     met = partner(other)
-    block = [slice(i * rows, (i + 1) * rows) for i in range(3)]
-    passing = cross_back(add(far_mine, far_met))
-    got_side = cross_back(add(mine[block[2]], met[block[2]]))
-    to_near = mine[block[1]].astype(f32) + met[block[1]].astype(f32) + passing.astype(f32)
-    got_near = cross(to_near.astype(bf16))
+    to_near = add(mine[rows:], met[rows:])
+    far, = after(met, early(far, 10))
+    got_near = early(cross(to_near), 10)
+    far_mine, far_other = experts(twice, far, partner(far))
+    to_far = add(far_mine, partner(far_other))
+    settled = pl.pallas_call(
+        settle_kernel,
+        out_shape=jax.ShapeDtypeStruct((rows, width), f32),
+        compiler_params=within(8),
+    )(mine, met, got_near)
+    to_far, = after(settled, to_far)
+    passing = early(cross(to_far), 10)
+    side = early(side, 10)
+    side, side_1 = after(to_far, side, partner(side))
+    side_mine, side_other = experts(twice, side, side_1)
+    side_met = partner(side_other)
+    part = pl.pallas_call(
+        add_kernel,
+        out_shape=jax.ShapeDtypeStruct((rows, width), f32),
+        compiler_params=within(8),
+    )(side_mine, passing)
+    to_side = (part + side_met.astype(f32)).astype(bf16)
+    got_side = cross_back(to_side)
     return pl.pallas_call(
         combine_kernel,
         out_shape=jax.ShapeDtypeStruct((count, width), bf16),
         compiler_params=within(24),
-    )(mine, met, got_side, got_near, spread)
+    )(settled, got_side, spread)
 
 
 def solution(mesh):

time: 48.8 us -> 43.2 us (0.89)
  waiting for transfers between devices: 22.4 us -> 15.9 us
  Pallas kernels: 11.8 us -> 14.1 us
  starting transfers between devices: 14 us -> 12.7 us
    ppermute x2 -> x3, waiting for transfers between devices: 8.2 us -> 4.1 us  [cross(): lax.ppermute(a, 'expert', [(i, i ^ (4 if i % 2 else 2)) for i in range(de...]
    ppermute x4 -> x3, starting transfers between devices: 7.77 us -> 4.29 us  [cross_back(): lax.ppermute(a, 'expert', [(i, i ^ (2 if i % 2 else 4)) for i in range(de...]
    ppermute x4 -> x3, waiting for transfers between devices: 13.1 us -> 10.7 us  [cross_back(): lax.ppermute(a, 'expert', [(i, i ^ (2 if i % 2 else 4)) for i in range(de...]
    pallas_call x2 -> x9, Pallas kernels: 4 us -> 6.36 us  [the longest x3 6.17 us: experts(): pl.pallas_call(functools.partial(expert_kernel, parts), out_shape=[jax.Sh...]
    ppermute x2 -> x3, starting transfers between devices: 5.05 us -> 7.38 us  [cross(): lax.ppermute(a, 'expert', [(i, i ^ (4 if i % 2 else 2)) for i in range(de...]
    ppermute x6 -> x7, starting transfers between devices: 1.22 us -> 0.99 us  [partner(): return lax.ppermute(a, 'expert', [(i, i ^ 1) for i in range(devices)])]
    ppermute x6 -> x7, waiting for transfers between devices: 1.15 us -> 1.07 us  [partner(): return lax.ppermute(a, 'expert', [(i, i ^ 1) for i in range(devices)])]
  transfers between devices with their start and end apart: 12 -> 13, of which waited for: 6 -> 7; matrix products, arithmetic and copies ran while one was open for 0% -> 0% of each run, Pallas kernels for 17% -> 25%
where the time goes in v3:
time: 43.2 us; the launch traced here: 43 us
  waiting for transfers between devices  15.9 us (37%)
  Pallas kernels  14.1 us (33%)
  starting transfers between devices  12.7 us (29%)
    ppermute x3, waiting for transfers between devices, cross_back(): lax.ppermute(a, 'expert', [(i, i ^ (2 if i % 2 else 4)) for i in range(de...  10.7 us
    ppermute x3, starting transfers between devices, cross(): lax.ppermute(a, 'expert', [(i, i ^ (4 if i % 2 else 2)) for i in range(de...  7.38 us
    pallas_call x3, Pallas kernels, experts(): pl.pallas_call(functools.partial(expert_kernel, parts), out_shape=[jax.Sh...  6.17 us
    pallas_call x1, Pallas kernels, two_copies(): pl.pallas_call(load_kernel, out_shape=[jax.ShapeDtypeStruct(a.shape[1:],...  4.32 us
    ppermute x3, starting transfers between devices, cross_back(): lax.ppermute(a, 'expert', [(i, i ^ (2 if i % 2 else 4)) for i in range(de...  4.29 us
    ppermute x3, waiting for transfers between devices, cross(): lax.ppermute(a, 'expert', [(i, i ^ (4 if i % 2 else 2)) for i in range(de...  4.1 us
    pallas_call x1, Pallas kernels, two_copies(): pl.pallas_call(pick_kernel, out_shape=[jax.ShapeDtypeStruct((rows, width)...  2.11 us
    pallas_call x1, Pallas kernels, two_copies(): pl.pallas_call(combine_kernel, out_shape=jax.ShapeDtypeStruct((count, wid...  1.33 us
  transfers between devices with their start and end apart: 13, of which 7 were waited for; matrix products, arithmetic and copies ran while one was open for 0% of the time, Pallas kernels for 25%

profile of v3, /device:TPU:0, one launch (start us, length us, event | category | flops | bytes accessed | tf_op | source)
XLA Modules:
  0.0 43.0 jit_solution(17402529947158314017)
XLA Ops:
  0.0 2.1 %shard_map.82 = (bf16[24,7168]{1,0:T(8,128)(2,1)}, f32[24,32]{1,0:T(8,128)}) custom-call(bf16[32,7168]{1,0:T(8,128)(2,1)} %tok_hbm.1, s32[8,32]{1,0:T(8,128)} %bitcast.10, s32[8,32]{1,0:T(8,128)} %bitcast.11, s32[2,256]{1,0:T(2,128)} %bitcast.13, f32[8,32]{1,0:T(8,128)} %bitcast.12), custom_call_target="tpu_custom_call" | custom-call | tf_op jit(solution)/shard_map/pallas_call | solution.py:221
  2.1 3.0 %collective-permute-start = (bf16[24,7168]{1,0:T(8,128)(2,1)}, bf16[24,7168]{1,0:T(8,128)(2,1)S(1)}, u32[]{:S(2)}, u32[]{:S(2)}) collective-permute-start(bf16[24,7168]{1,0:T(8,128)(2,1)} %get-tuple-element.18.refs_0_), channel_id=1, source_target_pairs={{0,2},{1,5},{2,0},{3,7},{4,6},{5,1},{6,4},{7,3},{8,10},{9,13},{10,... | collective-permute-start | bytes 1032200 | tf_op jit(solution)/shard_map/ppermute | solution.py:204
  5.2 0.0 collective-permute-start.1
  5.2 4.3 %shard_map.83 = (bf16[7168,256]{1,0:T(8,128)(2,1)S(1)}, bf16[7168,256]{1,0:T(8,128)(2,1)S(1)}, bf16[256,7168]{1,0:T(8,128)(2,1)S(1)}) custom-call(bf16[7168,256]{1,0:T(8,128)(2,1)} %bitcast.7, bf16[7168,256]{1,0:T(8,128)(2,1)} %bitcast.8, bf16[256,7168]{1,0:T(8,128)(2,1)} %bitcast.9), custom_call_target="tpu_custom_call" | custom-call | flops 528482304 | bytes 11010048 | tf_op jit(solution)/shard_map/pallas_call | solution.py:232
  9.5 0.0 copy-start
  9.5 1.1 %collective-permute-done.refs_1_ = bf16[24,7168]{1,0:T(8,128)(2,1)S(1)} collective-permute-done((bf16[24,7168]{1,0:T(8,128)(2,1)}, bf16[24,7168]{1,0:T(8,128)(2,1)S(1)}, u32[]{:S(2)}, u32[]{:S(2)}) %collective-permute-start) | collective-permute-done | bytes 344096 | tf_op jit(solution)/shard_map/ppermute | solution.py:204
  10.6 0.0 collective-permute-start.2
  10.6 2.1 %collective-permute-start.5 = (bf16[24,7168]{1,0:T(8,128)(2,1)S(1)}, bf16[24,7168]{1,0:T(8,128)(2,1)S(1)}, u32[]{:S(2)}, u32[]{:S(2)}) collective-permute-start(bf16[24,7168]{1,0:T(8,128)(2,1)S(1)} %shard_map.84.refs_1_), channel_id=1, source_target_pairs={{0,4},{1,3},{2,6},{3,1},{4,0},{5,7},{6,2},{7,5},{8,12},{9,11},{10,... | collective-permute-start | bytes 1032200 | tf_op jit(solution)/shard_map/ppermute | solution.py:207
  12.7 0.0 copy-done
  12.7 0.1 collective-permute-start.8
  12.8 0.0 collective-permute-done.1.refs_2_
  12.8 0.0 collective-permute-done.2.refs_3_
  12.8 2.0 %shard_map.85 = (bf16[48,7168]{1,0:T(8,128)(2,1)S(1)}, bf16[48,7168]{1,0:T(8,128)(2,1)S(1)}) custom-call(bf16[24,7168]{1,0:T(8,128)(2,1)S(1)} %copy-done, bf16[24,7168]{1,0:T(8,128)(2,1)S(1)} %shard_map.84.refs_1_, bf16[24,7168]{1,0:T(8,128)(2,1)S(1)} %collective-permute-done.1.refs_2_, bf16[24,7168]{1,0:T(8,128)(2,1)S(1)} %collective-permute-done.2.refs_3_, ...), custom_call_target="tpu_custom_call" | custom-call | flops 1056964608 | bytes 11010048 | tf_op jit(solution)/shard_map/pallas_call | solution.py:271
  14.7 0.2 collective-permute-start.3
  14.9 3.0 %collective-permute-done.5.refs_0_ = bf16[24,7168]{1,0:T(8,128)(2,1)S(1)} collective-permute-done((bf16[24,7168]{1,0:T(8,128)(2,1)S(1)}, bf16[24,7168]{1,0:T(8,128)(2,1)S(1)}, u32[]{:S(2)}, u32[]{:S(2)}) %collective-permute-start.5) | collective-permute-done | bytes 344096 | tf_op jit(solution)/shard_map/ppermute | solution.py:207
  17.9 0.0 collective-permute-done.3.met_ref.refs_0_
  17.9 0.1 add_convert_fusion.2
  18.0 2.0 %collective-permute-start.4 = (bf16[24,7168]{1,0:T(8,128)(2,1)S(1)}, bf16[24,7168]{1,0:T(8,128)(2,1)S(1)}, u32[]{:S(2)}, u32[]{:S(2)}) collective-permute-start(bf16[24,7168]{1,0:T(8,128)(2,1)S(1)} %add_convert_fusion.2), channel_id=1, source_target_pairs={{0,2},{1,5},{2,0},{3,7},{4,6},{5,1},{6,4},{7,3},{8,10},{9,13},{10,... | collective-permute-start | bytes 1032200 | tf_op jit(solution)/shard_map/ppermute | solution.py:204
  20.0 0.0 collective-permute-start.6
  20.0 2.5 %collective-permute-done.8.refs_0_ = bf16[24,7168]{1,0:T(8,128)(2,1)S(1)} collective-permute-done((bf16[24,7168]{1,0:T(8,128)(2,1)S(1)}, bf16[24,7168]{1,0:T(8,128)(2,1)S(1)}, u32[]{:S(2)}, u32[]{:S(2)}) %collective-permute-start.8) | collective-permute-done | bytes 344096 | tf_op jit(solution)/shard_map/ppermute | solution.py:207
  22.5 0.0 collective-permute-start.9
  22.5 0.0 collective-permute-done.6.refs_1_
  22.5 2.1 %shard_map.90 = (bf16[24,7168]{1,0:T(8,128)(2,1)S(1)}, bf16[24,7168]{1,0:T(8,128)(2,1)S(1)}) custom-call(bf16[24,7168]{1,0:T(8,128)(2,1)S(1)} %shard_map.89.refs_0_, bf16[24,7168]{1,0:T(8,128)(2,1)S(1)} %collective-permute-done.6.refs_1_, bf16[7168,256]{1,0:T(8,128)(2,1)S(1)} %get-tuple-element.19.refs_0_.refs_4_.refs_2_, ...), custom_call_target="tpu_custom_call" | custom-call | flops 528482304 | bytes 11010048 | tf_op jit(solution)/shard_map/pallas_call | solution.py:271
  24.6 0.6 %collective-permute-start.7 = (bf16[24,7168]{1,0:T(8,128)(2,1)S(1)}, bf16[24,7168]{1,0:T(8,128)(2,1)S(1)}, u32[]{:S(2)}, u32[]{:S(2)}) collective-permute-start(bf16[24,7168]{1,0:T(8,128)(2,1)S(1)} %get-tuple-element.25), channel_id=1, source_target_pairs={{0,1},{1,0},{2,3},{3,2},{4,5},{5,4},{6,7},{7,6},{8,9},{9,8},{10,11... | collective-permute-start | bytes 1032200 | tf_op jit(solution)/shard_map/ppermute | solution.py:201
  25.2 0.1 collective-permute-done.4.refs_0_
  25.3 0.1 shard_map.87.refs_0_.settled_ref
  25.4 1.1 %collective-permute-done.7 = bf16[24,7168]{1,0:T(8,128)(2,1)S(1)} collective-permute-done((bf16[24,7168]{1,0:T(8,128)(2,1)S(1)}, bf16[24,7168]{1,0:T(8,128)(2,1)S(1)}, u32[]{:S(2)}, u32[]{:S(2)}) %collective-permute-start.7) | collective-permute-done | bytes 344096 | tf_op jit(solution)/shard_map/ppermute | solution.py:201
  26.5 0.1 add_convert_fusion.1.refs_1_
  26.6 2.3 %collective-permute-start.10 = (bf16[24,7168]{1,0:T(8,128)(2,1)S(1)}, bf16[24,7168]{1,0:T(8,128)(2,1)S(1)}, u32[]{:S(2)}, u32[]{:S(2)}) collective-permute-start(bf16[24,7168]{1,0:T(8,128)(2,1)S(1)} %shard_map.91.refs_0_), channel_id=1, source_target_pairs={{0,2},{1,5},{2,0},{3,7},{4,6},{5,1},{6,4},{7,3},{8,10},{9,13},{10,... | collective-permute-start | bytes 1032200 | tf_op jit(solution)/shard_map/ppermute | solution.py:204
  28.9 0.0 collective-permute-done.9.refs_2_
  28.9 2.1 %shard_map.94 = (bf16[24,7168]{1,0:T(8,128)(2,1)S(1)}, bf16[24,7168]{1,0:T(8,128)(2,1)S(1)}) custom-call(bf16[24,7168]{1,0:T(8,128)(2,1)S(1)} %get-tuple-element.26.refs_0_, bf16[24,7168]{1,0:T(8,128)(2,1)S(1)} %get-tuple-element.27.refs_1_, bf16[7168,256]{1,0:T(8,128)(2,1)S(1)} %get-tuple-element.19.refs_0_.refs_4_.refs_2_, ...), custom_call_target="tpu_custom_call" | custom-call | flops 528482304 | bytes 11010048 | tf_op jit(solution)/shard_map/pallas_call | solution.py:271
  31.0 0.0 copy-start.1
  31.0 0.2 collective-permute-start.11
  31.2 2.9 %collective-permute-done.10.refs_0_ = bf16[24,7168]{1,0:T(8,128)(2,1)S(1)} collective-permute-done((bf16[24,7168]{1,0:T(8,128)(2,1)S(1)}, bf16[24,7168]{1,0:T(8,128)(2,1)S(1)}, u32[]{:S(2)}, u32[]{:S(2)}) %collective-permute-start.10) | collective-permute-done | bytes 344096 | tf_op jit(solution)/shard_map/ppermute | solution.py:204
  34.1 0.1 shard_map.96
  34.2 0.0 collective-permute-done.11
  34.2 0.1 add_convert_fusion
  34.3 2.1 %collective-permute-start.12 = (bf16[24,7168]{1,0:T(8,128)(2,1)S(1)}, bf16[24,7168]{1,0:T(8,128)(2,1)S(1)}, u32[]{:S(2)}, u32[]{:S(2)}) collective-permute-start(bf16[24,7168]{1,0:T(8,128)(2,1)S(1)} %add_convert_fusion), channel_id=1, source_target_pairs={{0,4},{1,3},{2,6},{3,1},{4,0},{5,7},{6,2},{7,5},{8,12},{9,11},{10,... | collective-permute-start | bytes 1032200 | tf_op jit(solution)/shard_map/ppermute | solution.py:207
  36.4 5.2 %collective-permute-done.12.near_ref = bf16[24,7168]{1,0:T(8,128)(2,1)S(1)} collective-permute-done((bf16[24,7168]{1,0:T(8,128)(2,1)S(1)}, bf16[24,7168]{1,0:T(8,128)(2,1)S(1)}, u32[]{:S(2)}, u32[]{:S(2)}) %collective-permute-start.12) | collective-permute-done | bytes 344096 | tf_op jit(solution)/shard_map/ppermute | solution.py:207
  41.6 0.0 copy-done.1
  41.7 1.3 %shard_map.97 = bf16[32,7168]{1,0:T(8,128)(2,1)} custom-call(f32[24,7168]{1,0:T(8,128)S(1)} %shard_map.87.refs_0_.settled_ref, bf16[24,7168]{1,0:T(8,128)(2,1)S(1)} %collective-permute-done.12.near_ref, f32[24,32]{1,0:T(8,128)S(1)} %copy-done.1), custom_call_target="tpu_custom_call" | custom-call | tf_op jit(solution)/shard_map/pallas_call | solution.py:308
  (8 shorter events, 0.0 us)
Async XLA Ops:
  2.1 8.5 %collective-permute-start = (bf16[24,7168]{1,0:T(8,128)(2,1)}, bf16[24,7168]{1,0:T(8,128)(2,1)S(1)}, u32[]{:S(2)}, u32[]{:S(2)}) collective-permute-start(bf16[24,7168]{1,0:T(8,128)(2,1)} %get-tuple-element.18.refs_0_), channel_id=1, source_target_pairs={{0,2},{1,5},{2,0},{3,7},{4,6},{5,1},{6,4},{7,3},{8,10},{9,13},{10,... | collective-permute-start | bytes 1032200 | tf_op jit(solution)/shard_map/ppermute | solution.py:204
  5.2 7.6 %collective-permute-start.1 = (bf16[24,7168]{1,0:T(8,128)(2,1)}, bf16[24,7168]{1,0:T(8,128)(2,1)S(1)}, u32[]{:S(2)}, u32[]{:S(2)}) collective-permute-start(bf16[24,7168]{1,0:T(8,128)(2,1)} %get-tuple-element.18.refs_0_), channel_id=1, source_target_pairs={{0,1},{1,0},{2,3},{3,2},{4,5},{5,4},{6,7},{7,6},{8,9},{9,8},{10,11... | collective-permute-start | bytes 1032200 | tf_op jit(solution)/shard_map/ppermute | solution.py:201
  9.5 3.2 %copy-start = (bf16[24,7168]{1,0:T(8,128)(2,1)S(1)}, bf16[24,7168]{1,0:T(8,128)(2,1)}, u32[]{:S(2)}) copy-start(bf16[24,7168]{1,0:T(8,128)(2,1)} %get-tuple-element.18.refs_0_) | copy-start | bytes 1032196
  10.6 2.2 %collective-permute-start.2 = (bf16[24,7168]{1,0:T(8,128)(2,1)S(1)}, bf16[24,7168]{1,0:T(8,128)(2,1)S(1)}, u32[]{:S(2)}, u32[]{:S(2)}) collective-permute-start(bf16[24,7168]{1,0:T(8,128)(2,1)S(1)} %shard_map.84.refs_1_), channel_id=1, source_target_pairs={{0,1},{1,0},{2,3},{3,2},{4,5},{5,4},{6,7},{7,6},{8,9},{9,8},{10,11... | collective-permute-start | bytes 1032200 | tf_op jit(solution)/shard_map/ppermute | solution.py:201
  10.6 7.3 %collective-permute-start.5 = (bf16[24,7168]{1,0:T(8,128)(2,1)S(1)}, bf16[24,7168]{1,0:T(8,128)(2,1)S(1)}, u32[]{:S(2)}, u32[]{:S(2)}) collective-permute-start(bf16[24,7168]{1,0:T(8,128)(2,1)S(1)} %shard_map.84.refs_1_), channel_id=1, source_target_pairs={{0,4},{1,3},{2,6},{3,1},{4,0},{5,7},{6,2},{7,5},{8,12},{9,11},{10,... | collective-permute-start | bytes 1032200 | tf_op jit(solution)/shard_map/ppermute | solution.py:207
  12.7 9.8 %collective-permute-start.8 = (bf16[24,7168]{1,0:T(8,128)(2,1)S(1)}, bf16[24,7168]{1,0:T(8,128)(2,1)S(1)}, u32[]{:S(2)}, u32[]{:S(2)}) collective-permute-start(bf16[24,7168]{1,0:T(8,128)(2,1)S(1)} %copy-done), channel_id=1, source_target_pairs={{0,4},{1,3},{2,6},{3,1},{4,0},{5,7},{6,2},{7,5},{8,12},{9,11},{10,... | collective-permute-start | bytes 1032200 | tf_op jit(solution)/shard_map/ppermute | solution.py:207
  14.7 3.2 %collective-permute-start.3 = (bf16[48,7168]{1,0:T(8,128)(2,1)S(1)}, bf16[48,7168]{1,0:T(8,128)(2,1)S(1)}, u32[]{:S(2)}, u32[]{:S(2)}) collective-permute-start(bf16[48,7168]{1,0:T(8,128)(2,1)S(1)} %get-tuple-element.23), channel_id=1, source_target_pairs={{0,1},{1,0},{2,3},{3,2},{4,5},{5,4},{6,7},{7,6},{8,9},{9,8},{10,11... | collective-permute-start | bytes 2064392 | tf_op jit(solution)/shard_map/ppermute | solution.py:201
  18.0 7.3 %collective-permute-start.4 = (bf16[24,7168]{1,0:T(8,128)(2,1)S(1)}, bf16[24,7168]{1,0:T(8,128)(2,1)S(1)}, u32[]{:S(2)}, u32[]{:S(2)}) collective-permute-start(bf16[24,7168]{1,0:T(8,128)(2,1)S(1)} %add_convert_fusion.2), channel_id=1, source_target_pairs={{0,2},{1,5},{2,0},{3,7},{4,6},{5,1},{6,4},{7,3},{8,10},{9,13},{10,... | collective-permute-start | bytes 1032200 | tf_op jit(solution)/shard_map/ppermute | solution.py:204
  20.0 2.5 %collective-permute-start.6 = (bf16[24,7168]{1,0:T(8,128)(2,1)S(1)}, bf16[24,7168]{1,0:T(8,128)(2,1)S(1)}, u32[]{:S(2)}, u32[]{:S(2)}) collective-permute-start(bf16[24,7168]{1,0:T(8,128)(2,1)S(1)} %shard_map.89.refs_0_), channel_id=1, source_target_pairs={{0,1},{1,0},{2,3},{3,2},{4,5},{5,4},{6,7},{7,6},{8,9},{9,8},{10,11... | collective-permute-start | bytes 1032200 | tf_op jit(solution)/shard_map/ppermute | solution.py:201
  22.5 6.4 %collective-permute-start.9 = (bf16[24,7168]{1,0:T(8,128)(2,1)S(1)}, bf16[24,7168]{1,0:T(8,128)(2,1)S(1)}, u32[]{:S(2)}, u32[]{:S(2)}) collective-permute-start(bf16[24,7168]{1,0:T(8,128)(2,1)S(1)} %shard_map.92.refs_1_), channel_id=1, source_target_pairs={{0,1},{1,0},{2,3},{3,2},{4,5},{5,4},{6,7},{7,6},{8,9},{9,8},{10,11... | collective-permute-start | bytes 1032200 | tf_op jit(solution)/shard_map/ppermute | solution.py:201
  24.6 1.9 %collective-permute-start.7 = (bf16[24,7168]{1,0:T(8,128)(2,1)S(1)}, bf16[24,7168]{1,0:T(8,128)(2,1)S(1)}, u32[]{:S(2)}, u32[]{:S(2)}) collective-permute-start(bf16[24,7168]{1,0:T(8,128)(2,1)S(1)} %get-tuple-element.25), channel_id=1, source_target_pairs={{0,1},{1,0},{2,3},{3,2},{4,5},{5,4},{6,7},{7,6},{8,9},{9,8},{10,11... | collective-permute-start | bytes 1032200 | tf_op jit(solution)/shard_map/ppermute | solution.py:201
  26.6 7.5 %collective-permute-start.10 = (bf16[24,7168]{1,0:T(8,128)(2,1)S(1)}, bf16[24,7168]{1,0:T(8,128)(2,1)S(1)}, u32[]{:S(2)}, u32[]{:S(2)}) collective-permute-start(bf16[24,7168]{1,0:T(8,128)(2,1)S(1)} %shard_map.91.refs_0_), channel_id=1, source_target_pairs={{0,2},{1,5},{2,0},{3,7},{4,6},{5,1},{6,4},{7,3},{8,10},{9,13},{10,... | collective-permute-start | bytes 1032200 | tf_op jit(solution)/shard_map/ppermute | solution.py:204
  31.0 10.7 %copy-start.1 = (f32[24,32]{1,0:T(8,128)S(1)}, f32[24,32]{1,0:T(8,128)}, u32[]{:S(2)}) copy-start(f32[24,32]{1,0:T(8,128)} %get-tuple-element.30.spread_ref) | copy-start | bytes 9220
  31.0 3.2 %collective-permute-start.11 = (bf16[24,7168]{1,0:T(8,128)(2,1)S(1)}, bf16[24,7168]{1,0:T(8,128)(2,1)S(1)}, u32[]{:S(2)}, u32[]{:S(2)}) collective-permute-start(bf16[24,7168]{1,0:T(8,128)(2,1)S(1)} %get-tuple-element.29), channel_id=1, source_target_pairs={{0,1},{1,0},{2,3},{3,2},{4,5},{5,4},{6,7},{7,6},{8,9},{9,8},{10,11... | collective-permute-start | bytes 1032200 | tf_op jit(solution)/shard_map/ppermute | solution.py:201
  34.3 7.4 %collective-permute-start.12 = (bf16[24,7168]{1,0:T(8,128)(2,1)S(1)}, bf16[24,7168]{1,0:T(8,128)(2,1)S(1)}, u32[]{:S(2)}, u32[]{:S(2)}) collective-permute-start(bf16[24,7168]{1,0:T(8,128)(2,1)S(1)} %add_convert_fusion), channel_id=1, source_target_pairs={{0,4},{1,3},{2,6},{3,1},{4,0},{5,7},{6,2},{7,5},{8,12},{9,11},{10,... | collective-permute-start | bytes 1032200 | tf_op jit(solution)/shard_map/ppermute | solution.py:207

commit v4 on v3

--- a/solution.py
+++ b/solution.py
@@ -284,17 +284,10 @@
     met = partner(other)
     to_near = add(mine[rows:], met[rows:])
     far, = after(met, early(far, 10))
-    got_near = early(cross(to_near), 10)
     far_mine, far_other = experts(twice, far, partner(far))
     to_far = add(far_mine, partner(far_other))
-    settled = pl.pallas_call(
-        settle_kernel,
-        out_shape=jax.ShapeDtypeStruct((rows, width), f32),
-        compiler_params=within(8),
-    )(mine, met, got_near)
-    to_far, = after(settled, to_far)
     passing = early(cross(to_far), 10)
-    side = early(side, 10)
+    got_near = cross(to_near)
     side, side_1 = after(to_far, side, partner(side))
     side_mine, side_other = experts(twice, side, side_1)
     side_met = partner(side_other)
@@ -304,6 +297,12 @@
         compiler_params=within(8),
     )(side_mine, passing)
     to_side = (part + side_met.astype(f32)).astype(bf16)
+    got_near, = after(side_mine, got_near)
+    settled = pl.pallas_call(
+        settle_kernel,
+        out_shape=jax.ShapeDtypeStruct((rows, width), f32),
+        compiler_params=within(8),
+    )(mine, met, got_near)
     got_side = cross_back(to_side)
     return pl.pallas_call(
         combine_kernel,

time: 43.2 us -> 41.6 us (0.963)
  waiting for transfers between devices: 15.9 us -> 14.8 us
  starting transfers between devices: 12.7 us -> 12.2 us
    ppermute x3, starting transfers between devices: 7.38 us -> 5.19 us  [cross(): lax.ppermute(a, 'expert', [(i, i ^ (4 if i % 2 else 2)) for i in range(de...]
    ppermute x3, waiting for transfers between devices: 4.1 us -> 6.06 us  [cross(): lax.ppermute(a, 'expert', [(i, i ^ (4 if i % 2 else 2)) for i in range(de...]
    ppermute x3, starting transfers between devices: 4.29 us -> 6.25 us  [cross_back(): lax.ppermute(a, 'expert', [(i, i ^ (2 if i % 2 else 4)) for i in range(de...]
    ppermute x3, waiting for transfers between devices: 10.7 us -> 8.75 us  [cross_back(): lax.ppermute(a, 'expert', [(i, i ^ (2 if i % 2 else 4)) for i in range(de...]
    ppermute x7, waiting for transfers between devices: 1.07 us -> 0.02 us  [partner(): return lax.ppermute(a, 'expert', [(i, i ^ 1) for i in range(devices)])]
  transfers between devices with their start and end apart: 13 -> 13, of which waited for: 7 -> 6; matrix products, arithmetic and copies ran while one was open for 0% -> 1% of each run, Pallas kernels for 25% -> 26%
where the time goes in v4:
time: 41.6 us; the launch traced here: 41.5 us
  waiting for transfers between devices  14.8 us (36%)
  Pallas kernels  14.1 us (34%)
  starting transfers between devices  12.2 us (29%)
    ppermute x3, waiting for transfers between devices, cross_back(): lax.ppermute(a, 'expert', [(i, i ^ (2 if i % 2 else 4)) for i in range(de...  8.75 us
    ppermute x3, starting transfers between devices, cross_back(): lax.ppermute(a, 'expert', [(i, i ^ (2 if i % 2 else 4)) for i in range(de...  6.25 us
    pallas_call x3, Pallas kernels, experts(): pl.pallas_call(functools.partial(expert_kernel, parts), out_shape=[jax.Sh...  6.17 us
    ppermute x3, waiting for transfers between devices, cross(): lax.ppermute(a, 'expert', [(i, i ^ (4 if i % 2 else 2)) for i in range(de...  6.06 us
    ppermute x3, starting transfers between devices, cross(): lax.ppermute(a, 'expert', [(i, i ^ (4 if i % 2 else 2)) for i in range(de...  5.19 us
    pallas_call x1, Pallas kernels, two_copies(): pl.pallas_call(load_kernel, out_shape=[jax.ShapeDtypeStruct(a.shape[1:],...  4.32 us
    pallas_call x1, Pallas kernels, two_copies(): pl.pallas_call(pick_kernel, out_shape=[jax.ShapeDtypeStruct((rows, width)...  2.11 us
    pallas_call x1, Pallas kernels, two_copies(): pl.pallas_call(combine_kernel, out_shape=jax.ShapeDtypeStruct((count, wid...  1.33 us
  transfers between devices with their start and end apart: 13, of which 6 were waited for; matrix products, arithmetic and copies ran while one was open for 1% of the time, Pallas kernels for 26%

profile of v4, /device:TPU:0, one launch (start us, length us, event | category | flops | bytes accessed | tf_op | source)
XLA Modules:
  0.0 41.5 jit_solution(17679186386929045754)
XLA Ops:
  0.0 2.1 %shard_map.82 = (bf16[24,7168]{1,0:T(8,128)(2,1)}, f32[24,32]{1,0:T(8,128)}) custom-call(bf16[32,7168]{1,0:T(8,128)(2,1)} %tok_hbm.1, s32[8,32]{1,0:T(8,128)} %bitcast.10, s32[8,32]{1,0:T(8,128)} %bitcast.11, s32[2,256]{1,0:T(2,128)} %bitcast.13, f32[8,32]{1,0:T(8,128)} %bitcast.12), custom_call_target="tpu_custom_call" | custom-call | tf_op jit(solution)/shard_map/pallas_call | solution.py:221
  2.1 3.0 %collective-permute-start = (bf16[24,7168]{1,0:T(8,128)(2,1)}, bf16[24,7168]{1,0:T(8,128)(2,1)S(1)}, u32[]{:S(2)}, u32[]{:S(2)}) collective-permute-start(bf16[24,7168]{1,0:T(8,128)(2,1)} %get-tuple-element.18.refs_0_), channel_id=1, source_target_pairs={{0,2},{1,5},{2,0},{3,7},{4,6},{5,1},{6,4},{7,3},{8,10},{9,13},{10,... | collective-permute-start | bytes 1032200 | tf_op jit(solution)/shard_map/ppermute | solution.py:204
  5.2 0.0 collective-permute-start.1
  5.2 4.3 %shard_map.83 = (bf16[7168,256]{1,0:T(8,128)(2,1)S(1)}, bf16[7168,256]{1,0:T(8,128)(2,1)S(1)}, bf16[256,7168]{1,0:T(8,128)(2,1)S(1)}) custom-call(bf16[7168,256]{1,0:T(8,128)(2,1)} %bitcast.7, bf16[7168,256]{1,0:T(8,128)(2,1)} %bitcast.8, bf16[256,7168]{1,0:T(8,128)(2,1)} %bitcast.9), custom_call_target="tpu_custom_call" | custom-call | flops 528482304 | bytes 11010048 | tf_op jit(solution)/shard_map/pallas_call | solution.py:232
  9.5 0.0 copy-start
  9.5 1.1 %collective-permute-done.refs_1_ = bf16[24,7168]{1,0:T(8,128)(2,1)S(1)} collective-permute-done((bf16[24,7168]{1,0:T(8,128)(2,1)}, bf16[24,7168]{1,0:T(8,128)(2,1)S(1)}, u32[]{:S(2)}, u32[]{:S(2)}) %collective-permute-start) | collective-permute-done | bytes 344096 | tf_op jit(solution)/shard_map/ppermute | solution.py:204
  10.6 0.0 collective-permute-start.2
  10.6 2.1 %collective-permute-start.4 = (bf16[24,7168]{1,0:T(8,128)(2,1)S(1)}, bf16[24,7168]{1,0:T(8,128)(2,1)S(1)}, u32[]{:S(2)}, u32[]{:S(2)}) collective-permute-start(bf16[24,7168]{1,0:T(8,128)(2,1)S(1)} %shard_map.84.refs_1_), channel_id=1, source_target_pairs={{0,4},{1,3},{2,6},{3,1},{4,0},{5,7},{6,2},{7,5},{8,12},{9,11},{10,... | collective-permute-start | bytes 1032200 | tf_op jit(solution)/shard_map/ppermute | solution.py:207
  12.7 0.0 collective-permute-done.1.refs_2_
  12.7 0.0 collective-permute-done.2.refs_3_
  12.7 0.0 copy-done
  12.7 2.0 %shard_map.85 = (bf16[48,7168]{1,0:T(8,128)(2,1)S(1)}, bf16[48,7168]{1,0:T(8,128)(2,1)S(1)}) custom-call(bf16[24,7168]{1,0:T(8,128)(2,1)S(1)} %copy-done, bf16[24,7168]{1,0:T(8,128)(2,1)S(1)} %shard_map.84.refs_1_, bf16[24,7168]{1,0:T(8,128)(2,1)S(1)} %collective-permute-done.1.refs_2_, bf16[24,7168]{1,0:T(8,128)(2,1)S(1)} %collective-permute-done.2.refs_3_, ...), custom_call_target="tpu_custom_call" | custom-call | flops 1056964608 | bytes 11010048 | tf_op jit(solution)/shard_map/pallas_call | solution.py:271
  14.7 0.2 collective-permute-start.3
  14.9 3.0 %collective-permute-done.4.refs_0_ = bf16[24,7168]{1,0:T(8,128)(2,1)S(1)} collective-permute-done((bf16[24,7168]{1,0:T(8,128)(2,1)S(1)}, bf16[24,7168]{1,0:T(8,128)(2,1)S(1)}, u32[]{:S(2)}, u32[]{:S(2)}) %collective-permute-start.4) | collective-permute-done | bytes 344096 | tf_op jit(solution)/shard_map/ppermute | solution.py:207
  17.9 0.0 collective-permute-done.3.refs_0_.met_ref
  17.9 0.0 collective-permute-start.5
  17.9 2.1 %collective-permute-start.7 = (bf16[24,7168]{1,0:T(8,128)(2,1)S(1)}, bf16[24,7168]{1,0:T(8,128)(2,1)S(1)}, u32[]{:S(2)}, u32[]{:S(2)}) collective-permute-start(bf16[24,7168]{1,0:T(8,128)(2,1)S(1)} %copy-done), channel_id=1, source_target_pairs={{0,4},{1,3},{2,6},{3,1},{4,0},{5,7},{6,2},{7,5},{8,12},{9,11},{10,... | collective-permute-start | bytes 1032200 | tf_op jit(solution)/shard_map/ppermute | solution.py:207
  20.0 0.0 collective-permute-done.5.refs_1_
  20.0 2.1 %shard_map.88 = (bf16[24,7168]{1,0:T(8,128)(2,1)S(1)}, bf16[24,7168]{1,0:T(8,128)(2,1)S(1)}) custom-call(bf16[24,7168]{1,0:T(8,128)(2,1)S(1)} %shard_map.87.refs_0_, bf16[24,7168]{1,0:T(8,128)(2,1)S(1)} %collective-permute-done.5.refs_1_, bf16[7168,256]{1,0:T(8,128)(2,1)S(1)} %get-tuple-element.19.refs_0_.refs_4_.refs_2_, ...), custom_call_target="tpu_custom_call" | custom-call | flops 528482304 | bytes 11010048 | tf_op jit(solution)/shard_map/pallas_call | solution.py:271
  22.1 0.2 collective-permute-start.6
  22.3 3.0 %collective-permute-done.7.refs_1_ = bf16[24,7168]{1,0:T(8,128)(2,1)S(1)} collective-permute-done((bf16[24,7168]{1,0:T(8,128)(2,1)S(1)}, bf16[24,7168]{1,0:T(8,128)(2,1)S(1)}, u32[]{:S(2)}, u32[]{:S(2)}) %collective-permute-start.7) | collective-permute-done | bytes 344096 | tf_op jit(solution)/shard_map/ppermute | solution.py:207
  25.2 0.0 collective-permute-start.8
  25.2 0.0 collective-permute-done.6
  25.2 0.1 add_convert_fusion.2.refs_0_
  25.3 2.0 %collective-permute-start.10 = (bf16[24,7168]{1,0:T(8,128)(2,1)S(1)}, bf16[24,7168]{1,0:T(8,128)(2,1)S(1)}, u32[]{:S(2)}, u32[]{:S(2)}) collective-permute-start(bf16[24,7168]{1,0:T(8,128)(2,1)S(1)} %add_convert_fusion.2.refs_0_), channel_id=1, source_target_pairs={{0,2},{1,5},{2,0},{3,7},{4,6},{5,1},{6,4},{7,3},{8,10},{9,13},{10,... | collective-permute-start | bytes 1032200 | tf_op jit(solution)/shard_map/ppermute | solution.py:204
  27.4 0.1 add_convert_fusion.1
  27.4 0.1 collective-permute-start.9
  27.6 0.0 collective-permute-done.8.refs_2_
  27.6 2.1 %shard_map.90 = (bf16[24,7168]{1,0:T(8,128)(2,1)S(1)}, bf16[24,7168]{1,0:T(8,128)(2,1)S(1)}) custom-call(bf16[24,7168]{1,0:T(8,128)(2,1)S(1)} %get-tuple-element.26.refs_0_, bf16[24,7168]{1,0:T(8,128)(2,1)S(1)} %get-tuple-element.27.refs_1_, bf16[7168,256]{1,0:T(8,128)(2,1)S(1)} %get-tuple-element.19.refs_0_.refs_4_.refs_2_, ...), custom_call_target="tpu_custom_call" | custom-call | flops 528482304 | bytes 11010048 | tf_op jit(solution)/shard_map/pallas_call | solution.py:271
  29.7 0.3 collective-permute-start.11
  30.0 2.7 %collective-permute-done.10.refs_0_ = bf16[24,7168]{1,0:T(8,128)(2,1)S(1)} collective-permute-done((bf16[24,7168]{1,0:T(8,128)(2,1)S(1)}, bf16[24,7168]{1,0:T(8,128)(2,1)S(1)}, u32[]{:S(2)}, u32[]{:S(2)}) %collective-permute-start.10) | collective-permute-done | bytes 344096 | tf_op jit(solution)/shard_map/ppermute | solution.py:204
  32.6 0.0 copy-start.1
  32.6 0.1 shard_map.94
  32.7 0.0 collective-permute-done.11
  32.7 0.1 add_convert_fusion
  32.8 2.1 %collective-permute-start.12 = (bf16[24,7168]{1,0:T(8,128)(2,1)S(1)}, bf16[24,7168]{1,0:T(8,128)(2,1)S(1)}, u32[]{:S(2)}, u32[]{:S(2)}) collective-permute-start(bf16[24,7168]{1,0:T(8,128)(2,1)S(1)} %add_convert_fusion), channel_id=1, source_target_pairs={{0,4},{1,3},{2,6},{3,1},{4,0},{5,7},{6,2},{7,5},{8,12},{9,11},{10,... | collective-permute-start | bytes 1032200 | tf_op jit(solution)/shard_map/ppermute | solution.py:207
  34.9 2.3 %collective-permute-done.9.refs_1_ = bf16[24,7168]{1,0:T(8,128)(2,1)S(1)} collective-permute-done((bf16[24,7168]{1,0:T(8,128)(2,1)S(1)}, bf16[24,7168]{1,0:T(8,128)(2,1)S(1)}, u32[]{:S(2)}, u32[]{:S(2)}) %collective-permute-start.9) | collective-permute-done | bytes 344096 | tf_op jit(solution)/shard_map/ppermute | solution.py:204
  37.2 0.1 shard_map.92.settled_ref
  37.3 2.8 %collective-permute-done.12.near_ref = bf16[24,7168]{1,0:T(8,128)(2,1)S(1)} collective-permute-done((bf16[24,7168]{1,0:T(8,128)(2,1)S(1)}, bf16[24,7168]{1,0:T(8,128)(2,1)S(1)}, u32[]{:S(2)}, u32[]{:S(2)}) %collective-permute-start.12) | collective-permute-done | bytes 344096 | tf_op jit(solution)/shard_map/ppermute | solution.py:207
  40.1 0.0 copy-done.1
  40.1 1.3 %shard_map.95 = bf16[32,7168]{1,0:T(8,128)(2,1)} custom-call(f32[24,7168]{1,0:T(8,128)S(1)} %shard_map.92.settled_ref, bf16[24,7168]{1,0:T(8,128)(2,1)S(1)} %collective-permute-done.12.near_ref, f32[24,32]{1,0:T(8,128)S(1)} %copy-done.1), custom_call_target="tpu_custom_call" | custom-call | tf_op jit(solution)/shard_map/pallas_call | solution.py:307
  (6 shorter events, 0.0 us)
Async XLA Ops:
  2.1 8.5 %collective-permute-start = (bf16[24,7168]{1,0:T(8,128)(2,1)}, bf16[24,7168]{1,0:T(8,128)(2,1)S(1)}, u32[]{:S(2)}, u32[]{:S(2)}) collective-permute-start(bf16[24,7168]{1,0:T(8,128)(2,1)} %get-tuple-element.18.refs_0_), channel_id=1, source_target_pairs={{0,2},{1,5},{2,0},{3,7},{4,6},{5,1},{6,4},{7,3},{8,10},{9,13},{10,... | collective-permute-start | bytes 1032200 | tf_op jit(solution)/shard_map/ppermute | solution.py:204
  5.2 7.5 %collective-permute-start.1 = (bf16[24,7168]{1,0:T(8,128)(2,1)}, bf16[24,7168]{1,0:T(8,128)(2,1)S(1)}, u32[]{:S(2)}, u32[]{:S(2)}) collective-permute-start(bf16[24,7168]{1,0:T(8,128)(2,1)} %get-tuple-element.18.refs_0_), channel_id=1, source_target_pairs={{0,1},{1,0},{2,3},{3,2},{4,5},{5,4},{6,7},{7,6},{8,9},{9,8},{10,11... | collective-permute-start | bytes 1032200 | tf_op jit(solution)/shard_map/ppermute | solution.py:201
  9.5 3.2 %copy-start = (bf16[24,7168]{1,0:T(8,128)(2,1)S(1)}, bf16[24,7168]{1,0:T(8,128)(2,1)}, u32[]{:S(2)}) copy-start(bf16[24,7168]{1,0:T(8,128)(2,1)} %get-tuple-element.18.refs_0_) | copy-start | bytes 1032196
  10.6 2.1 %collective-permute-start.2 = (bf16[24,7168]{1,0:T(8,128)(2,1)S(1)}, bf16[24,7168]{1,0:T(8,128)(2,1)S(1)}, u32[]{:S(2)}, u32[]{:S(2)}) collective-permute-start(bf16[24,7168]{1,0:T(8,128)(2,1)S(1)} %shard_map.84.refs_1_), channel_id=1, source_target_pairs={{0,1},{1,0},{2,3},{3,2},{4,5},{5,4},{6,7},{7,6},{8,9},{9,8},{10,11... | collective-permute-start | bytes 1032200 | tf_op jit(solution)/shard_map/ppermute | solution.py:201
  10.6 7.3 %collective-permute-start.4 = (bf16[24,7168]{1,0:T(8,128)(2,1)S(1)}, bf16[24,7168]{1,0:T(8,128)(2,1)S(1)}, u32[]{:S(2)}, u32[]{:S(2)}) collective-permute-start(bf16[24,7168]{1,0:T(8,128)(2,1)S(1)} %shard_map.84.refs_1_), channel_id=1, source_target_pairs={{0,4},{1,3},{2,6},{3,1},{4,0},{5,7},{6,2},{7,5},{8,12},{9,11},{10,... | collective-permute-start | bytes 1032200 | tf_op jit(solution)/shard_map/ppermute | solution.py:207
  14.7 3.2 %collective-permute-start.3 = (bf16[48,7168]{1,0:T(8,128)(2,1)S(1)}, bf16[48,7168]{1,0:T(8,128)(2,1)S(1)}, u32[]{:S(2)}, u32[]{:S(2)}) collective-permute-start(bf16[48,7168]{1,0:T(8,128)(2,1)S(1)} %get-tuple-element.23), channel_id=1, source_target_pairs={{0,1},{1,0},{2,3},{3,2},{4,5},{5,4},{6,7},{7,6},{8,9},{9,8},{10,11... | collective-permute-start | bytes 2064392 | tf_op jit(solution)/shard_map/ppermute | solution.py:201
  17.9 2.1 %collective-permute-start.5 = (bf16[24,7168]{1,0:T(8,128)(2,1)S(1)}, bf16[24,7168]{1,0:T(8,128)(2,1)S(1)}, u32[]{:S(2)}, u32[]{:S(2)}) collective-permute-start(bf16[24,7168]{1,0:T(8,128)(2,1)S(1)} %shard_map.87.refs_0_), channel_id=1, source_target_pairs={{0,1},{1,0},{2,3},{3,2},{4,5},{5,4},{6,7},{7,6},{8,9},{9,8},{10,11... | collective-permute-start | bytes 1032200 | tf_op jit(solution)/shard_map/ppermute | solution.py:201
  17.9 7.3 %collective-permute-start.7 = (bf16[24,7168]{1,0:T(8,128)(2,1)S(1)}, bf16[24,7168]{1,0:T(8,128)(2,1)S(1)}, u32[]{:S(2)}, u32[]{:S(2)}) collective-permute-start(bf16[24,7168]{1,0:T(8,128)(2,1)S(1)} %copy-done), channel_id=1, source_target_pairs={{0,4},{1,3},{2,6},{3,1},{4,0},{5,7},{6,2},{7,5},{8,12},{9,11},{10,... | collective-permute-start | bytes 1032200 | tf_op jit(solution)/shard_map/ppermute | solution.py:207
  22.1 3.1 %collective-permute-start.6 = (bf16[24,7168]{1,0:T(8,128)(2,1)S(1)}, bf16[24,7168]{1,0:T(8,128)(2,1)S(1)}, u32[]{:S(2)}, u32[]{:S(2)}) collective-permute-start(bf16[24,7168]{1,0:T(8,128)(2,1)S(1)} %get-tuple-element.25), channel_id=1, source_target_pairs={{0,1},{1,0},{2,3},{3,2},{4,5},{5,4},{6,7},{7,6},{8,9},{9,8},{10,11... | collective-permute-start | bytes 1032200 | tf_op jit(solution)/shard_map/ppermute | solution.py:201
  25.2 2.3 %collective-permute-start.8 = (bf16[24,7168]{1,0:T(8,128)(2,1)S(1)}, bf16[24,7168]{1,0:T(8,128)(2,1)S(1)}, u32[]{:S(2)}, u32[]{:S(2)}) collective-permute-start(bf16[24,7168]{1,0:T(8,128)(2,1)S(1)} %collective-permute-done.7.refs_1_), channel_id=1, source_target_pairs={{0,1},{1,0},{2,3},{3,2},{4,5},{5,4},{6,7},{7,6},{8,9},{9,8},{10,11... | collective-permute-start | bytes 1032200 | tf_op jit(solution)/shard_map/ppermute | solution.py:201
  25.3 7.3 %collective-permute-start.10 = (bf16[24,7168]{1,0:T(8,128)(2,1)S(1)}, bf16[24,7168]{1,0:T(8,128)(2,1)S(1)}, u32[]{:S(2)}, u32[]{:S(2)}) collective-permute-start(bf16[24,7168]{1,0:T(8,128)(2,1)S(1)} %add_convert_fusion.2.refs_0_), channel_id=1, source_target_pairs={{0,2},{1,5},{2,0},{3,7},{4,6},{5,1},{6,4},{7,3},{8,10},{9,13},{10,... | collective-permute-start | bytes 1032200 | tf_op jit(solution)/shard_map/ppermute | solution.py:204
  27.4 9.8 %collective-permute-start.9 = (bf16[24,7168]{1,0:T(8,128)(2,1)S(1)}, bf16[24,7168]{1,0:T(8,128)(2,1)S(1)}, u32[]{:S(2)}, u32[]{:S(2)}) collective-permute-start(bf16[24,7168]{1,0:T(8,128)(2,1)S(1)} %add_convert_fusion.1), channel_id=1, source_target_pairs={{0,2},{1,5},{2,0},{3,7},{4,6},{5,1},{6,4},{7,3},{8,10},{9,13},{10,... | collective-permute-start | bytes 1032200 | tf_op jit(solution)/shard_map/ppermute | solution.py:204
  29.7 3.1 %collective-permute-start.11 = (bf16[24,7168]{1,0:T(8,128)(2,1)S(1)}, bf16[24,7168]{1,0:T(8,128)(2,1)S(1)}, u32[]{:S(2)}, u32[]{:S(2)}) collective-permute-start(bf16[24,7168]{1,0:T(8,128)(2,1)S(1)} %get-tuple-element.29), channel_id=1, source_target_pairs={{0,1},{1,0},{2,3},{3,2},{4,5},{5,4},{6,7},{7,6},{8,9},{9,8},{10,11... | collective-permute-start | bytes 1032200 | tf_op jit(solution)/shard_map/ppermute | solution.py:201
  32.6 7.5 %copy-start.1 = (f32[24,32]{1,0:T(8,128)S(1)}, f32[24,32]{1,0:T(8,128)}, u32[]{:S(2)}) copy-start(f32[24,32]{1,0:T(8,128)} %get-tuple-element.30.spread_ref) | copy-start | bytes 9220
  32.8 7.3 %collective-permute-start.12 = (bf16[24,7168]{1,0:T(8,128)(2,1)S(1)}, bf16[24,7168]{1,0:T(8,128)(2,1)S(1)}, u32[]{:S(2)}, u32[]{:S(2)}) collective-permute-start(bf16[24,7168]{1,0:T(8,128)(2,1)S(1)} %add_convert_fusion), channel_id=1, source_target_pairs={{0,4},{1,3},{2,6},{3,1},{4,0},{5,7},{6,2},{7,5},{8,12},{9,11},{10,... | collective-permute-start | bytes 1032200 | tf_op jit(solution)/shard_map/ppermute | solution.py:207

commit v5 on v4

--- a/solution.py
+++ b/solution.py
@@ -72,18 +72,17 @@
     hit = ids == hosted
     copy = jnp.where(rep == 0, first, 1 - first)
     count = ids.shape[1]
-    to = [jnp.sum(jnp.where(hit & (copy == c), 1.0, 0.0), axis=0, keepdims=True) for c in range(2)]
+    some = jnp.sum(jnp.where(hit, 1, 0), axis=0, keepdims=True)
+    copy = jnp.sum(jnp.where(hit, copy, 0), axis=0, keepdims=True)
+    lanes = lax.broadcasted_iota(jnp.int32, (8, count), 0)
+    routed = ((lanes == copy) & (some > 0)).astype(jnp.float32)
     earlier = (
         lax.broadcasted_iota(jnp.int32, (count, count), 0)
         < lax.broadcasted_iota(jnp.int32, (count, count), 1)
     ).astype(jnp.float32)
-    slot = jnp.full((1, count), -1, jnp.int32)
-    for c in range(2):
-        routed = jnp.broadcast_to(to[c], (8, count))
-        position = jnp.dot(routed, earlier, preferred_element_type=jnp.float32)[0:1]
-        position = position.astype(jnp.int32)
-        keep = (to[c] > 0.5) & (position < CAP)
-        slot = jnp.where(keep, position + c * CAP, slot)
+    position = jnp.dot(routed, earlier, preferred_element_type=jnp.float32)
+    position = jnp.sum(routed * position, axis=0, keepdims=True).astype(jnp.int32)
+    slot = jnp.where((some > 0) & (position < CAP), position + copy * CAP, -1)
     return slot, hit
 
 
@@ -95,7 +94,7 @@
 
 
 def pick_kernel(
-    tok_hbm, ids_hbm, rep_hbm, table_hbm, w_hbm, out_ref, spread_ref,
+    tok_hbm, ids_hbm, rep_hbm, table_hbm, w_hbm, out_ref, chosen_ref, weight_ref,
     tok_ref, ids_ref, rep_ref, table_ref, w_ref, sems,
 ):
     copies = copies_of(
@@ -111,21 +110,25 @@
     for copy in copies[:4]:
         copy.wait()
     slot, hit = slots_of(ids_ref[...], rep_ref[...], table_ref[...])
-    weight = jnp.sum(jnp.where(hit, w_ref[...], 0.0), axis=0, keepdims=True)
     count = slot.shape[1]
     chosen = lax.broadcasted_iota(jnp.int32, (2 * CAP, count), 0) == slot
-    spread_ref[...] = jnp.where(chosen, weight, 0.0)
+    chosen = chosen.astype(jnp.bfloat16)
     copies[4].wait()
     out_ref[...] = jnp.dot(
-        chosen.astype(jnp.bfloat16), tok_ref[...], preferred_element_type=jnp.float32
+        chosen, tok_ref[...], preferred_element_type=jnp.float32
     ).astype(jnp.bfloat16)
+    chosen_ref[...] = chosen
+    weight = jnp.sum(jnp.where(hit, w_ref[...], 0.0), axis=0, keepdims=True)
+    square = [lax.broadcasted_iota(jnp.int32, (count, count), i) for i in range(2)]
+    diagonal = jnp.where(square[0] == square[1], weight, 0.0)
+    weight_ref[...] = jnp.sum(diagonal, axis=1, keepdims=True)
 
 
 def activation(gate, up):
     return (gate / (1.0 + jnp.exp(-gate)) * up).astype(jnp.bfloat16)
 
 
-def load_kernel(gate_hbm, up_hbm, down_hbm, gate_ref, up_ref, down_ref, sems):
+def load_kernel(_, gate_hbm, up_hbm, down_hbm, gate_ref, up_ref, down_ref, sems):
     steps = sems.shape[1]
     pairs = []
     for source, target in ((gate_hbm, gate_ref), (up_hbm, up_ref), (down_hbm, down_ref)):
@@ -147,22 +150,25 @@
     pass
 
 
-def expert_kernel(parts, *refs):
+def expert_kernel(*refs):
     gate_ref, up_ref, down_ref, mine_ref, other_ref, x_all = refs[-6:]
-    rows = x_all.shape[0] // len(parts)
-    for i, (which, block) in enumerate(parts):
-        x_all[i * rows : (i + 1) * rows] = refs[which][block * rows : (block + 1) * rows]
+    rows = refs[0].shape[0]
+    for i, ref in enumerate(refs[:-6]):
+        x_all[i * rows : (i + 1) * rows] = ref[...]
+    for i in range(len(refs) - 6, x_all.shape[0] // rows):
+        x_all[i * rows : (i + 1) * rows] = refs[0][...]
     x = x_all[...]
     gate = jnp.dot(x, gate_ref[...], preferred_element_type=jnp.float32)
     up = jnp.dot(x, up_ref[...], preferred_element_type=jnp.float32)
     hidden = activation(gate, up)
     out = jnp.dot(hidden, down_ref[...], preferred_element_type=jnp.float32).astype(jnp.bfloat16)
     mine_ref[...] = out[: mine_ref.shape[0]]
-    other_ref[...] = out[mine_ref.shape[0] :]
-
-
-def add_kernel(mine_ref, passing_ref, out_ref):
-    out_ref[...] = mine_ref[...].astype(jnp.float32) + passing_ref[...].astype(jnp.float32)
+    other_ref[...] = out[mine_ref.shape[0] : mine_ref.shape[0] + other_ref.shape[0]]
+
+
+def side_kernel(mine_ref, met_ref, _, out_ref):
+    rows = out_ref.shape[0]
+    out_ref[...] = mine_ref[rows:].astype(jnp.float32) + met_ref[2 * rows :].astype(jnp.float32)
 
 
 def settle_kernel(mine_ref, met_ref, side_ref, out_ref):
@@ -171,19 +177,23 @@
     out_ref[...] = total + side_ref[...].astype(jnp.float32)
 
 
-def combine_kernel(settled_ref, near_ref, spread_ref, out_ref):
-    spread = spread_ref[...]
-    spread_hi = spread.astype(jnp.bfloat16)
-    spread_lo = (spread - spread_hi.astype(jnp.float32)).astype(jnp.bfloat16)
-    dims = (((0,), (0,)), ((), ()))
-    dot = functools.partial(
-        lax.dot_general, dimension_numbers=dims, preferred_element_type=jnp.float32
-    )
-    total = settled_ref[...] + near_ref[...].astype(jnp.float32)
-    total_hi = total.astype(jnp.bfloat16)
-    total_lo = (total - total_hi.astype(jnp.float32)).astype(jnp.bfloat16)
-    out = dot(spread_hi, total_hi) + (dot(spread_hi, total_lo) + dot(spread_lo, total_hi))
-    out_ref[...] = out.astype(jnp.bfloat16)
+def combine_kernel(settled_ref, side_ref, chosen_ref, weight_ref, out_hbm, out_ref, sems):
+    chosen, weight = chosen_ref[...], weight_ref[...]
+    steps = sems.shape[0]
+    step = out_ref.shape[1] // steps
+    copies = []
+    for i in range(steps):
+        part = slice(i * step, (i + 1) * step)
+        total = settled_ref[:, part] + side_ref[:, part].astype(jnp.float32)
+        out = lax.dot_general(
+            chosen, total.astype(jnp.bfloat16), (((0,), (0,)), ((), ())),
+            preferred_element_type=jnp.float32,
+        )
+        out_ref[:, part] = (weight * out).astype(jnp.bfloat16)
+        copies.append(pltpu.make_async_copy(out_ref.at[:, part], out_hbm.at[:, part], sems.at[i]))
+        copies[-1].start()
+    for copy in copies:
+        copy.wait()
 
 
 def two_copies(
@@ -218,28 +228,30 @@
         )
 
     small = [expert_ids.T, replica.T, slot_table.T, gate_weights.T]
-    own, spread = pl.pallas_call(
+    own, chosen, weight = pl.pallas_call(
         pick_kernel,
         out_shape=[
             jax.ShapeDtypeStruct((rows, width), bf16),
-            jax.ShapeDtypeStruct((rows, count), f32),
+            jax.ShapeDtypeStruct((rows, count), bf16),
+            jax.ShapeDtypeStruct((count, 1), f32),
         ],
         in_specs=[in_hbm] * 5,
         scratch_shapes=[pltpu.VMEM(a.shape, a.dtype) for a in [tokens] + small]
         + [pltpu.SemaphoreType.DMA((5,))],
         compiler_params=within(56),
     )(tokens, *small)
+    own_1 = partner(own)
     gate, up, down = pl.pallas_call(
         load_kernel,
         out_shape=[
             jax.ShapeDtypeStruct(a.shape[1:], bf16) for a in (gate_pieces, up_pieces, down_pieces)
         ],
-        in_specs=[in_hbm] * 3,
+        in_specs=[pl.BlockSpec(memory_space=pl.ANY)] + [in_hbm] * 3,
         out_specs=[in_vmem] * 3,
         scratch_shapes=[pltpu.SemaphoreType.DMA((3, 8))],
         compiler_params=within(40),
         cost_estimate=cost(2 * rows),
-    )(gate_pieces[0], up_pieces[0], down_pieces[0])
+    )(own_1, gate_pieces[0], up_pieces[0], down_pieces[0])
 
     def after(done, *arrays):
         anywhere = pl.BlockSpec(memory_space=pl.ANY)
@@ -266,49 +278,52 @@
             ),
         )(array)
 
-    def experts(parts, *arrays):
-        total = rows * len(parts)
+    def experts(blocks, mine, *arrays):
+        total = rows * blocks
         return pl.pallas_call(
-            functools.partial(expert_kernel, parts),
-            out_shape=[jax.ShapeDtypeStruct((total // 2, width), bf16)] * 2,
-            scratch_shapes=[pltpu.VMEM((total, width), bf16)],
+            expert_kernel,
+            out_shape=[
+                jax.ShapeDtypeStruct((rows * mine, width), bf16),
+                jax.ShapeDtypeStruct((rows * (blocks - mine), width), bf16),
+            ],
+            scratch_shapes=[pltpu.VMEM((max(total, 5 * rows), width), bf16)],
             compiler_params=within(24),
             cost_estimate=cost(total),
         )(*arrays, gate, up, down)
 
-    twice = ((0, 0), (1, 0))
     near, = after(gate, cross(own))
+    side_1, = after(gate, cross(own_1))
     far = cross_back(near)
-    side = cross_back(own)
-    mine, other = experts(((0, 0), (1, 0), (2, 0), (3, 0)), own, near, partner(own), partner(near))
+    mine, other = experts(5, 2, own, near, own_1, partner(near), side_1)
     met = partner(other)
-    to_near = add(mine[rows:], met[rows:])
+    block = [slice(i * rows, (i + 1) * rows) for i in range(3)]
+    to_near = add(mine[block[1]], met[block[1]])
+    side = partner(side_1)
     far, = after(met, early(far, 10))
-    far_mine, far_other = experts(twice, far, partner(far))
-    to_far = add(far_mine, partner(far_other))
+    last_mine, last_other = experts(3, 2, far, side, partner(far))
+    to_far = add(last_mine[:rows], partner(last_other))
     passing = early(cross(to_far), 10)
-    got_near = cross(to_near)
-    side, side_1 = after(to_far, side, partner(side))
-    side_mine, side_other = experts(twice, side, side_1)
-    side_met = partner(side_other)
-    part = pl.pallas_call(
-        add_kernel,
+    to_side = pl.pallas_call(
+        side_kernel,
         out_shape=jax.ShapeDtypeStruct((rows, width), f32),
+        in_specs=[in_vmem] * 2 + [pl.BlockSpec(memory_space=pl.ANY)],
         compiler_params=within(8),
-    )(side_mine, passing)
-    to_side = (part + side_met.astype(f32)).astype(bf16)
-    got_near, = after(side_mine, got_near)
+        cost_estimate=cost(10 * rows),
+    )(last_mine, met, to_far)
+    got_side = cross_back((to_side + passing.astype(f32)).astype(bf16))
+    got_near, = after(to_side, cross(to_near))
     settled = pl.pallas_call(
         settle_kernel,
         out_shape=jax.ShapeDtypeStruct((rows, width), f32),
         compiler_params=within(8),
     )(mine, met, got_near)
-    got_side = cross_back(to_side)
     return pl.pallas_call(
         combine_kernel,
         out_shape=jax.ShapeDtypeStruct((count, width), bf16),
+        out_specs=pl.BlockSpec(memory_space=pl.ANY),
+        scratch_shapes=[pltpu.VMEM((count, width), bf16), pltpu.SemaphoreType.DMA((4,))],
         compiler_params=within(24),
-    )(settled, got_side, spread)
+    )(settled, got_side, chosen, weight)
 
 
 def solution(mesh):

time: 41.6 us -> 40.4 us (0.971)
  Pallas kernels: 14.1 us -> 11.1 us
  waiting for transfers between devices: 14.8 us -> 16.8 us
    ppermute x3 -> x2, waiting for transfers between devices: 8.75 us -> 4.29 us  [cross_back(): lax.ppermute(a, 'expert', [(i, i ^ (2 if i % 2 else 4)) for i in range(de...]
    ppermute x3 -> x4, waiting for transfers between devices: 6.06 us -> 9.36 us  [cross(): lax.ppermute(a, 'expert', [(i, i ^ (4 if i % 2 else 2)) for i in range(de...]
    ppermute x7 -> x6, waiting for transfers between devices: 0.02 us -> 3.12 us  [partner(): return lax.ppermute(a, 'expert', [(i, i ^ 1) for i in range(devices)])]
    ppermute x3 -> x2, starting transfers between devices: 6.25 us -> 3.52 us  [cross_back(): lax.ppermute(a, 'expert', [(i, i ^ (2 if i % 2 else 4)) for i in range(de...]
    pallas_call x4 -> x3, Pallas kernels: 6.24 us -> 3.53 us  [the longest x2 3.46 us: experts(): pl.pallas_call(expert_kernel, out_shape=[jax.ShapeDtypeStruct((rows * min...]
    ppermute x3 -> x4, starting transfers between devices: 5.19 us -> 7 us  [cross(): lax.ppermute(a, 'expert', [(i, i ^ (4 if i % 2 else 2)) for i in range(de...]
    ppermute x7 -> x6, starting transfers between devices: 0.73 us -> 1.5 us  [partner(): return lax.ppermute(a, 'expert', [(i, i ^ 1) for i in range(devices)])]
  transfers between devices with their start and end apart: 13 -> 12, of which waited for: 6 -> 9; matrix products, arithmetic and copies ran while one was open for 1% -> 0% of each run, Pallas kernels for 26% -> 16%
where the time goes in v5:
time: 40.4 us; the launch traced here: 40.2 us
  waiting for transfers between devices  16.8 us (42%)
  starting transfers between devices  12 us (30%)
  Pallas kernels  11.1 us (27%)
    ppermute x4, waiting for transfers between devices, cross(): lax.ppermute(a, 'expert', [(i, i ^ (4 if i % 2 else 2)) for i in range(de...  9.36 us
    ppermute x4, starting transfers between devices, cross(): lax.ppermute(a, 'expert', [(i, i ^ (4 if i % 2 else 2)) for i in range(de...  7 us
    pallas_call x1, Pallas kernels, two_copies(): pl.pallas_call(load_kernel, out_shape=[jax.ShapeDtypeStruct(a.shape[1:],...  4.32 us
    ppermute x2, waiting for transfers between devices, cross_back(): lax.ppermute(a, 'expert', [(i, i ^ (2 if i % 2 else 4)) for i in range(de...  4.29 us
    ppermute x2, starting transfers between devices, cross_back(): lax.ppermute(a, 'expert', [(i, i ^ (2 if i % 2 else 4)) for i in range(de...  3.52 us
    pallas_call x2, Pallas kernels, experts(): pl.pallas_call(expert_kernel, out_shape=[jax.ShapeDtypeStruct((rows * min...  3.46 us
    ppermute x6, waiting for transfers between devices, partner(): return lax.ppermute(a, 'expert', [(i, i ^ 1) for i in range(devices)])  3.12 us
    pallas_call x1, Pallas kernels, two_copies(): pl.pallas_call(pick_kernel, out_shape=[jax.ShapeDtypeStruct((rows, width)...  2.11 us
  transfers between devices with their start and end apart: 12, of which 9 were waited for; matrix products, arithmetic and copies ran while one was open for 0% of the time, Pallas kernels for 16%

profile of v5, /device:TPU:0, one launch (start us, length us, event | category | flops | bytes accessed | tf_op | source)
XLA Modules:
  0.0 40.2 jit_solution(17683803323114930531)
XLA Ops:
  0.0 2.1 %shard_map.82 = (bf16[24,7168]{1,0:T(8,128)(2,1)}, bf16[24,32]{1,0:T(8,128)(2,1)}, f32[32,1]{1,0:T(8,128)}) custom-call(bf16[32,7168]{1,0:T(8,128)(2,1)} %tok_hbm.1, s32[8,32]{1,0:T(8,128)} %bitcast.10, s32[8,32]{1,0:T(8,128)} %bitcast.11, s32[2,256]{1,0:T(2,128)} %bitcast.13, f32[8,32]{1,0:T(8,128)} %bitcast.12), custom_call_target="tpu_custom_call" | custom-call | tf_op jit(solution)/shard_map/pallas_call | solution.py:231
  2.1 0.5 %collective-permute-start = (bf16[24,7168]{1,0:T(8,128)(2,1)}, bf16[24,7168]{1,0:T(8,128)(2,1)S(1)}, u32[]{:S(2)}, u32[]{:S(2)}) collective-permute-start(bf16[24,7168]{1,0:T(8,128)(2,1)} %get-tuple-element.15.refs_0_), channel_id=1, source_target_pairs={{0,1},{1,0},{2,3},{3,2},{4,5},{5,4},{6,7},{7,6},{8,9},{9,8},{10,11... | collective-permute-start | bytes 1032200 | tf_op jit(solution)/shard_map/ppermute | solution.py:211
  2.6 2.6 %collective-permute-start.1 = (bf16[24,7168]{1,0:T(8,128)(2,1)}, bf16[24,7168]{1,0:T(8,128)(2,1)S(1)}, u32[]{:S(2)}, u32[]{:S(2)}) collective-permute-start(bf16[24,7168]{1,0:T(8,128)(2,1)} %get-tuple-element.15.refs_0_), channel_id=1, source_target_pairs={{0,2},{1,5},{2,0},{3,7},{4,6},{5,1},{6,4},{7,3},{8,10},{9,13},{10,... | collective-permute-start | bytes 1032200 | tf_op jit(solution)/shard_map/ppermute | solution.py:214
  5.2 0.0 collective-permute-done._.refs_2_
  5.2 1.8 %collective-permute-start.3 = (bf16[24,7168]{1,0:T(8,128)(2,1)S(1)}, bf16[24,7168]{1,0:T(8,128)(2,1)S(1)}, u32[]{:S(2)}, u32[]{:S(2)}) collective-permute-start(bf16[24,7168]{1,0:T(8,128)(2,1)S(1)} %collective-permute-done._.refs_2_), channel_id=1, source_target_pairs={{0,2},{1,5},{2,0},{3,7},{4,6},{5,1},{6,4},{7,3},{8,10},{9,13},{10,... | collective-permute-start | bytes 1032200 | tf_op jit(solution)/shard_map/ppermute | solution.py:214
  7.0 4.3 %shard_map.83 = (bf16[7168,256]{1,0:T(8,128)(2,1)S(1)}, bf16[7168,256]{1,0:T(8,128)(2,1)S(1)}, bf16[256,7168]{1,0:T(8,128)(2,1)S(1)}) custom-call(bf16[24,7168]{1,0:T(8,128)(2,1)S(1)} %collective-permute-done._.refs_2_, bf16[7168,256]{1,0:T(8,128)(2,1)} %bitcast.7, bf16[7168,256]{1,0:T(8,128)(2,1)} %bitcast.8, bf16[256,7168]{1,0:T(8,128)(2,1)} %bitcast.9), custom_call_target="tpu_custom_call" | custom-call | flops 528482304 | bytes 11010048 | tf_op jit(solution)/shard_map/pallas_call | solution.py:244
  11.3 0.0 collective-permute-done.1.refs_1_
  11.4 0.0 copy-start
  11.4 0.1 collective-permute-start.2
  11.5 1.6 %collective-permute-start.5 = (bf16[24,7168]{1,0:T(8,128)(2,1)S(1)}, bf16[24,7168]{1,0:T(8,128)(2,1)S(1)}, u32[]{:S(2)}, u32[]{:S(2)}) collective-permute-start(bf16[24,7168]{1,0:T(8,128)(2,1)S(1)} %shard_map.84.refs_1_), channel_id=1, source_target_pairs={{0,4},{1,3},{2,6},{3,1},{4,0},{5,7},{6,2},{7,5},{8,12},{9,11},{10,... | collective-permute-start | bytes 1032200 | tf_op jit(solution)/shard_map/ppermute | solution.py:217
  13.1 1.3 %collective-permute-done.3.refs_1_ = bf16[24,7168]{1,0:T(8,128)(2,1)S(1)} collective-permute-done((bf16[24,7168]{1,0:T(8,128)(2,1)S(1)}, bf16[24,7168]{1,0:T(8,128)(2,1)S(1)}, u32[]{:S(2)}, u32[]{:S(2)}) %collective-permute-start.3) | collective-permute-done | bytes 344096 | tf_op jit(solution)/shard_map/ppermute | solution.py:214
  14.4 0.0 collective-permute-done.2.refs_3_
  14.4 0.0 copy-done
  14.4 1.7 %shard_map.86 = (bf16[48,7168]{1,0:T(8,128)(2,1)S(1)}, bf16[72,7168]{1,0:T(8,128)(2,1)S(1)}) custom-call(bf16[24,7168]{1,0:T(8,128)(2,1)S(1)} %copy-done, bf16[24,7168]{1,0:T(8,128)(2,1)S(1)} %shard_map.84.refs_1_, bf16[24,7168]{1,0:T(8,128)(2,1)S(1)} %collective-permute-done._.refs_2_, bf16[24,7168]{1,0:T(8,128)(2,1)S(1)} %collective-permute-done.2.refs_3_, ...), custom_call_target="tpu_custom_call" | custom-call | flops 1321205760 | bytes 11010048 | tf_op jit(solution)/shard_map/pallas_call | solution.py:283
  16.2 0.1 collective-permute-start.4
  16.2 0.5 %collective-permute-start.6 = (bf16[24,7168]{1,0:T(8,128)(2,1)S(1)}, bf16[24,7168]{1,0:T(8,128)(2,1)S(1)}, u32[]{:S(2)}, u32[]{:S(2)}) collective-permute-start(bf16[24,7168]{1,0:T(8,128)(2,1)S(1)} %shard_map.85.refs_4_), channel_id=1, source_target_pairs={{0,1},{1,0},{2,3},{3,2},{4,5},{5,4},{6,7},{7,6},{8,9},{9,8},{10,11... | collective-permute-start | bytes 1032200 | tf_op jit(solution)/shard_map/ppermute | solution.py:211
  16.7 2.0 %collective-permute-done.5.refs_0_ = bf16[24,7168]{1,0:T(8,128)(2,1)S(1)} collective-permute-done((bf16[24,7168]{1,0:T(8,128)(2,1)S(1)}, bf16[24,7168]{1,0:T(8,128)(2,1)S(1)}, u32[]{:S(2)}, u32[]{:S(2)}) %collective-permute-start.5) | collective-permute-done | bytes 344096 | tf_op jit(solution)/shard_map/ppermute | solution.py:217
  18.8 0.1 collective-permute-done.4.refs_0_.met_ref
  18.9 0.1 collective-permute-start.7
  19.0 0.4 collective-permute-done.6.refs_1_
  19.4 1.2 %collective-permute-done.7.refs_2_ = bf16[24,7168]{1,0:T(8,128)(2,1)S(1)} collective-permute-done((bf16[24,7168]{1,0:T(8,128)(2,1)S(1)}, bf16[24,7168]{1,0:T(8,128)(2,1)S(1)}, u32[]{:S(2)}, u32[]{:S(2)}) %collective-permute-start.7) | collective-permute-done | bytes 344096 | tf_op jit(solution)/shard_map/ppermute | solution.py:211
  20.5 1.7 %shard_map.89 = (bf16[48,7168]{1,0:T(8,128)(2,1)S(1)}, bf16[24,7168]{1,0:T(8,128)(2,1)S(1)}) custom-call(bf16[24,7168]{1,0:T(8,128)(2,1)S(1)} %shard_map.88.refs_0_, bf16[24,7168]{1,0:T(8,128)(2,1)S(1)} %collective-permute-done.6.refs_1_, bf16[24,7168]{1,0:T(8,128)(2,1)S(1)} %collective-permute-done.7.refs_2_, ...), custom_call_target="tpu_custom_call" | custom-call | flops 792723456 | bytes 11010048 | tf_op jit(solution)/shard_map/pallas_call | solution.py:283
  22.3 0.2 collective-permute-start.8
  22.5 1.5 %collective-permute-done.8 = bf16[24,7168]{1,0:T(8,128)(2,1)S(1)} collective-permute-done((bf16[24,7168]{1,0:T(8,128)(2,1)S(1)}, bf16[24,7168]{1,0:T(8,128)(2,1)S(1)}, u32[]{:S(2)}, u32[]{:S(2)}) %collective-permute-start.8) | collective-permute-done | bytes 344096 | tf_op jit(solution)/shard_map/ppermute | solution.py:211
  24.0 0.1 add_convert_fusion.2._
  24.1 2.5 %collective-permute-start.10 = (bf16[24,7168]{1,0:T(8,128)(2,1)S(1)}, bf16[24,7168]{1,0:T(8,128)(2,1)S(1)}, u32[]{:S(2)}, u32[]{:S(2)}) collective-permute-start(bf16[24,7168]{1,0:T(8,128)(2,1)S(1)} %add_convert_fusion.2._), channel_id=1, source_target_pairs={{0,2},{1,5},{2,0},{3,7},{4,6},{5,1},{6,4},{7,3},{8,10},{9,13},{10,... | collective-permute-start | bytes 1032200 | tf_op jit(solution)/shard_map/ppermute | solution.py:214
  26.6 0.1 add_convert_fusion.1
  26.7 0.1 collective-permute-start.9
  26.8 0.1 shard_map.90.refs_0_
  26.8 5.0 %collective-permute-done.10.refs_0_ = bf16[24,7168]{1,0:T(8,128)(2,1)S(1)} collective-permute-done((bf16[24,7168]{1,0:T(8,128)(2,1)S(1)}, bf16[24,7168]{1,0:T(8,128)(2,1)S(1)}, u32[]{:S(2)}, u32[]{:S(2)}) %collective-permute-start.10) | collective-permute-done | bytes 344096 | tf_op jit(solution)/shard_map/ppermute | solution.py:214
  31.8 0.0 copy-start.1
  31.8 0.0 copy-start.2
  31.8 0.1 add_convert_fusion
  31.9 1.9 %collective-permute-start.11 = (bf16[24,7168]{1,0:T(8,128)(2,1)S(1)}, bf16[24,7168]{1,0:T(8,128)(2,1)S(1)}, u32[]{:S(2)}, u32[]{:S(2)}) collective-permute-start(bf16[24,7168]{1,0:T(8,128)(2,1)S(1)} %add_convert_fusion), channel_id=1, source_target_pairs={{0,4},{1,3},{2,6},{3,1},{4,0},{5,7},{6,2},{7,5},{8,12},{9,11},{10,... | collective-permute-start | bytes 1032200 | tf_op jit(solution)/shard_map/ppermute | solution.py:217
  33.8 3.1 %collective-permute-done.9.refs_1_ = bf16[24,7168]{1,0:T(8,128)(2,1)S(1)} collective-permute-done((bf16[24,7168]{1,0:T(8,128)(2,1)S(1)}, bf16[24,7168]{1,0:T(8,128)(2,1)S(1)}, u32[]{:S(2)}, u32[]{:S(2)}) %collective-permute-start.9) | collective-permute-done | bytes 344096 | tf_op jit(solution)/shard_map/ppermute | solution.py:214
  36.8 0.1 shard_map.92.settled_ref
  37.0 2.3 %collective-permute-done.11.side_ref = bf16[24,7168]{1,0:T(8,128)(2,1)S(1)} collective-permute-done((bf16[24,7168]{1,0:T(8,128)(2,1)S(1)}, bf16[24,7168]{1,0:T(8,128)(2,1)S(1)}, u32[]{:S(2)}, u32[]{:S(2)}) %collective-permute-start.11) | collective-permute-done | bytes 344096 | tf_op jit(solution)/shard_map/ppermute | solution.py:217
  39.2 0.0 copy-done.1
  39.2 0.0 copy-done.2
  39.2 1.0 %shard_map.94 = bf16[32,7168]{1,0:T(8,128)(2,1)} custom-call(f32[24,7168]{1,0:T(8,128)S(1)} %shard_map.92.settled_ref, bf16[24,7168]{1,0:T(8,128)(2,1)S(1)} %collective-permute-done.11.side_ref, bf16[24,32]{1,0:T(8,128)(2,1)S(1)} %copy-done.2, f32[32,1]{1,0:T(8,128)S(1)} %copy-done.1), custom_call_target="tpu_custom_call" | custom-call | tf_op jit(solution)/shard_map/pallas_call | solution.py:320
  (6 shorter events, 0.0 us)
Async XLA Ops:
  2.1 3.1 %collective-permute-start = (bf16[24,7168]{1,0:T(8,128)(2,1)}, bf16[24,7168]{1,0:T(8,128)(2,1)S(1)}, u32[]{:S(2)}, u32[]{:S(2)}) collective-permute-start(bf16[24,7168]{1,0:T(8,128)(2,1)} %get-tuple-element.15.refs_0_), channel_id=1, source_target_pairs={{0,1},{1,0},{2,3},{3,2},{4,5},{5,4},{6,7},{7,6},{8,9},{9,8},{10,11... | collective-permute-start | bytes 1032200 | tf_op jit(solution)/shard_map/ppermute | solution.py:211
  2.6 8.7 %collective-permute-start.1 = (bf16[24,7168]{1,0:T(8,128)(2,1)}, bf16[24,7168]{1,0:T(8,128)(2,1)S(1)}, u32[]{:S(2)}, u32[]{:S(2)}) collective-permute-start(bf16[24,7168]{1,0:T(8,128)(2,1)} %get-tuple-element.15.refs_0_), channel_id=1, source_target_pairs={{0,2},{1,5},{2,0},{3,7},{4,6},{5,1},{6,4},{7,3},{8,10},{9,13},{10,... | collective-permute-start | bytes 1032200 | tf_op jit(solution)/shard_map/ppermute | solution.py:214
  5.2 9.2 %collective-permute-start.3 = (bf16[24,7168]{1,0:T(8,128)(2,1)S(1)}, bf16[24,7168]{1,0:T(8,128)(2,1)S(1)}, u32[]{:S(2)}, u32[]{:S(2)}) collective-permute-start(bf16[24,7168]{1,0:T(8,128)(2,1)S(1)} %collective-permute-done._.refs_2_), channel_id=1, source_target_pairs={{0,2},{1,5},{2,0},{3,7},{4,6},{5,1},{6,4},{7,3},{8,10},{9,13},{10,... | collective-permute-start | bytes 1032200 | tf_op jit(solution)/shard_map/ppermute | solution.py:214
  11.4 3.1 %copy-start = (bf16[24,7168]{1,0:T(8,128)(2,1)S(1)}, bf16[24,7168]{1,0:T(8,128)(2,1)}, u32[]{:S(2)}) copy-start(bf16[24,7168]{1,0:T(8,128)(2,1)} %get-tuple-element.15.refs_0_) | copy-start | bytes 1032196
  11.4 3.0 %collective-permute-start.2 = (bf16[24,7168]{1,0:T(8,128)(2,1)S(1)}, bf16[24,7168]{1,0:T(8,128)(2,1)S(1)}, u32[]{:S(2)}, u32[]{:S(2)}) collective-permute-start(bf16[24,7168]{1,0:T(8,128)(2,1)S(1)} %shard_map.84.refs_1_), channel_id=1, source_target_pairs={{0,1},{1,0},{2,3},{3,2},{4,5},{5,4},{6,7},{7,6},{8,9},{9,8},{10,11... | collective-permute-start | bytes 1032200 | tf_op jit(solution)/shard_map/ppermute | solution.py:211
  11.5 7.3 %collective-permute-start.5 = (bf16[24,7168]{1,0:T(8,128)(2,1)S(1)}, bf16[24,7168]{1,0:T(8,128)(2,1)S(1)}, u32[]{:S(2)}, u32[]{:S(2)}) collective-permute-start(bf16[24,7168]{1,0:T(8,128)(2,1)S(1)} %shard_map.84.refs_1_), channel_id=1, source_target_pairs={{0,4},{1,3},{2,6},{3,1},{4,0},{5,7},{6,2},{7,5},{8,12},{9,11},{10,... | collective-permute-start | bytes 1032200 | tf_op jit(solution)/shard_map/ppermute | solution.py:217
  16.2 2.7 %collective-permute-start.4 = (bf16[72,7168]{1,0:T(8,128)(2,1)S(1)}, bf16[72,7168]{1,0:T(8,128)(2,1)S(1)}, u32[]{:S(2)}, u32[]{:S(2)}) collective-permute-start(bf16[72,7168]{1,0:T(8,128)(2,1)S(1)} %get-tuple-element.20), channel_id=1, source_target_pairs={{0,1},{1,0},{2,3},{3,2},{4,5},{5,4},{6,7},{7,6},{8,9},{9,8},{10,11... | collective-permute-start | bytes 3096584 | tf_op jit(solution)/shard_map/ppermute | solution.py:211
  16.2 3.1 %collective-permute-start.6 = (bf16[24,7168]{1,0:T(8,128)(2,1)S(1)}, bf16[24,7168]{1,0:T(8,128)(2,1)S(1)}, u32[]{:S(2)}, u32[]{:S(2)}) collective-permute-start(bf16[24,7168]{1,0:T(8,128)(2,1)S(1)} %shard_map.85.refs_4_), channel_id=1, source_target_pairs={{0,1},{1,0},{2,3},{3,2},{4,5},{5,4},{6,7},{7,6},{8,9},{9,8},{10,11... | collective-permute-start | bytes 1032200 | tf_op jit(solution)/shard_map/ppermute | solution.py:211
  18.9 1.7 %collective-permute-start.7 = (bf16[24,7168]{1,0:T(8,128)(2,1)S(1)}, bf16[24,7168]{1,0:T(8,128)(2,1)S(1)}, u32[]{:S(2)}, u32[]{:S(2)}) collective-permute-start(bf16[24,7168]{1,0:T(8,128)(2,1)S(1)} %shard_map.88.refs_0_), channel_id=1, source_target_pairs={{0,1},{1,0},{2,3},{3,2},{4,5},{5,4},{6,7},{7,6},{8,9},{9,8},{10,11... | collective-permute-start | bytes 1032200 | tf_op jit(solution)/shard_map/ppermute | solution.py:211
  22.3 1.7 %collective-permute-start.8 = (bf16[24,7168]{1,0:T(8,128)(2,1)S(1)}, bf16[24,7168]{1,0:T(8,128)(2,1)S(1)}, u32[]{:S(2)}, u32[]{:S(2)}) collective-permute-start(bf16[24,7168]{1,0:T(8,128)(2,1)S(1)} %get-tuple-element.22), channel_id=1, source_target_pairs={{0,1},{1,0},{2,3},{3,2},{4,5},{5,4},{6,7},{7,6},{8,9},{9,8},{10,11... | collective-permute-start | bytes 1032200 | tf_op jit(solution)/shard_map/ppermute | solution.py:211
  24.1 7.8 %collective-permute-start.10 = (bf16[24,7168]{1,0:T(8,128)(2,1)S(1)}, bf16[24,7168]{1,0:T(8,128)(2,1)S(1)}, u32[]{:S(2)}, u32[]{:S(2)}) collective-permute-start(bf16[24,7168]{1,0:T(8,128)(2,1)S(1)} %add_convert_fusion.2._), channel_id=1, source_target_pairs={{0,2},{1,5},{2,0},{3,7},{4,6},{5,1},{6,4},{7,3},{8,10},{9,13},{10,... | collective-permute-start | bytes 1032200 | tf_op jit(solution)/shard_map/ppermute | solution.py:214
  26.7 10.2 %collective-permute-start.9 = (bf16[24,7168]{1,0:T(8,128)(2,1)S(1)}, bf16[24,7168]{1,0:T(8,128)(2,1)S(1)}, u32[]{:S(2)}, u32[]{:S(2)}) collective-permute-start(bf16[24,7168]{1,0:T(8,128)(2,1)S(1)} %add_convert_fusion.1), channel_id=1, source_target_pairs={{0,2},{1,5},{2,0},{3,7},{4,6},{5,1},{6,4},{7,3},{8,10},{9,13},{10,... | collective-permute-start | bytes 1032200 | tf_op jit(solution)/shard_map/ppermute | solution.py:214
  31.8 7.4 %copy-start.1 = (f32[32,1]{1,0:T(8,128)S(1)}, f32[32,1]{1,0:T(8,128)}, u32[]{:S(2)}) copy-start(f32[32,1]{1,0:T(8,128)} %get-tuple-element.24.weight_ref) | copy-start | bytes 388
  31.8 7.4 %copy-start.2 = (bf16[24,32]{1,0:T(8,128)(2,1)S(1)}, bf16[24,32]{1,0:T(8,128)(2,1)}, u32[]{:S(2)}) copy-start(bf16[24,32]{1,0:T(8,128)(2,1)} %get-tuple-element.23.chosen_ref) | copy-start | bytes 4612
  31.9 7.3 %collective-permute-start.11 = (bf16[24,7168]{1,0:T(8,128)(2,1)S(1)}, bf16[24,7168]{1,0:T(8,128)(2,1)S(1)}, u32[]{:S(2)}, u32[]{:S(2)}) collective-permute-start(bf16[24,7168]{1,0:T(8,128)(2,1)S(1)} %add_convert_fusion), channel_id=1, source_target_pairs={{0,4},{1,3},{2,6},{3,1},{4,0},{5,7},{6,2},{7,5},{8,12},{9,11},{10,... | collective-permute-start | bytes 1032200 | tf_op jit(solution)/shard_map/ppermute | solution.py:217

commit v6 on v5

--- a/solution.py
+++ b/solution.py
@@ -128,10 +128,11 @@
     return (gate / (1.0 + jnp.exp(-gate)) * up).astype(jnp.bfloat16)
 
 
-def load_kernel(_, gate_hbm, up_hbm, down_hbm, gate_ref, up_ref, down_ref, sems):
-    steps = sems.shape[1]
+def load_kernel(*refs):
+    refs, sems = refs[1:-1], refs[-1]
+    count, steps = sems.shape
     pairs = []
-    for source, target in ((gate_hbm, gate_ref), (up_hbm, up_ref), (down_hbm, down_ref)):
+    for source, target in zip(refs[:count], refs[count:]):
         step = source.shape[0] // steps
         for i in range(steps):
             part = pl.ds(i * step, step)
@@ -150,25 +151,28 @@
     pass
 
 
-def expert_kernel(*refs):
-    gate_ref, up_ref, down_ref, mine_ref, other_ref, x_all = refs[-6:]
+def expert_kernel(blocks, *refs):
+    gate_ref, up_ref, down_ref = refs[blocks : blocks + 3]
+    out_refs, x_all = refs[blocks + 3 : -1], refs[-1]
     rows = refs[0].shape[0]
-    for i, ref in enumerate(refs[:-6]):
-        x_all[i * rows : (i + 1) * rows] = ref[...]
-    for i in range(len(refs) - 6, x_all.shape[0] // rows):
+    for i in range(blocks):
+        x_all[i * rows : (i + 1) * rows] = refs[i][...]
+    for i in range(blocks, x_all.shape[0] // rows):
         x_all[i * rows : (i + 1) * rows] = refs[0][...]
     x = x_all[...]
     gate = jnp.dot(x, gate_ref[...], preferred_element_type=jnp.float32)
     up = jnp.dot(x, up_ref[...], preferred_element_type=jnp.float32)
     hidden = activation(gate, up)
     out = jnp.dot(hidden, down_ref[...], preferred_element_type=jnp.float32).astype(jnp.bfloat16)
-    mine_ref[...] = out[: mine_ref.shape[0]]
-    other_ref[...] = out[mine_ref.shape[0] : mine_ref.shape[0] + other_ref.shape[0]]
+    row = 0
+    for ref in out_refs:
+        ref[...] = out[row : row + ref.shape[0]]
+        row += ref.shape[0]
 
 
 def side_kernel(mine_ref, met_ref, _, out_ref):
     rows = out_ref.shape[0]
-    out_ref[...] = mine_ref[rows:].astype(jnp.float32) + met_ref[2 * rows :].astype(jnp.float32)
+    out_ref[...] = mine_ref[rows:].astype(jnp.float32) + met_ref[rows:].astype(jnp.float32)
 
 
 def settle_kernel(mine_ref, met_ref, side_ref, out_ref):
@@ -241,17 +245,20 @@
         compiler_params=within(56),
     )(tokens, *small)
     own_1 = partner(own)
-    gate, up, down = pl.pallas_call(
-        load_kernel,
-        out_shape=[
-            jax.ShapeDtypeStruct(a.shape[1:], bf16) for a in (gate_pieces, up_pieces, down_pieces)
-        ],
-        in_specs=[pl.BlockSpec(memory_space=pl.ANY)] + [in_hbm] * 3,
-        out_specs=[in_vmem] * 3,
-        scratch_shapes=[pltpu.SemaphoreType.DMA((3, 8))],
-        compiler_params=within(40),
-        cost_estimate=cost(2 * rows),
-    )(own_1, gate_pieces[0], up_pieces[0], down_pieces[0])
+
+    def load(done, *weights):
+        return pl.pallas_call(
+            load_kernel,
+            out_shape=[jax.ShapeDtypeStruct(a.shape[1:], bf16) for a in weights],
+            in_specs=[pl.BlockSpec(memory_space=pl.ANY)] + [in_hbm] * len(weights),
+            out_specs=[in_vmem] * len(weights),
+            scratch_shapes=[pltpu.SemaphoreType.DMA((len(weights), 8))],
+            compiler_params=within(44),
+            cost_estimate=cost(2 * rows),
+        )(done, *[a[0] for a in weights])
+
+    gate, up = load(own_1, gate_pieces, up_pieces)
+    down = down_pieces[0]
 
     def after(done, *arrays):
         anywhere = pl.BlockSpec(memory_space=pl.ANY)
@@ -278,30 +285,28 @@
             ),
         )(array)
 
-    def experts(blocks, mine, *arrays):
-        total = rows * blocks
+    def experts(outs, *arrays):
+        blocks = len(arrays)
         return pl.pallas_call(
-            expert_kernel,
-            out_shape=[
-                jax.ShapeDtypeStruct((rows * mine, width), bf16),
-                jax.ShapeDtypeStruct((rows * (blocks - mine), width), bf16),
-            ],
-            scratch_shapes=[pltpu.VMEM((max(total, 5 * rows), width), bf16)],
+            functools.partial(expert_kernel, blocks),
+            out_shape=[jax.ShapeDtypeStruct((rows * out, width), bf16) for out in outs],
+            scratch_shapes=[pltpu.VMEM((rows * max(blocks, 5), width), bf16)],
             compiler_params=within(24),
-            cost_estimate=cost(total),
+            cost_estimate=cost(rows * blocks),
         )(*arrays, gate, up, down)
 
     near, = after(gate, cross(own))
     side_1, = after(gate, cross(own_1))
     far = cross_back(near)
-    mine, other = experts(5, 2, own, near, own_1, partner(near), side_1)
+    mine, near_other, other = experts((2, 1, 2), own, near, partner(near), own_1, side_1)
+    near_met = partner(near_other)
+    to_near = add(mine[rows:], near_met)
+    side = early(partner(side_1), 10)
+    far, = after(near_met, early(far, 10))
+    last_mine, last_other = experts((2, 1), far, side, partner(far))
+    to_far = add(last_mine[:rows], partner(last_other))
+    other, = after(to_far, other)
     met = partner(other)
-    block = [slice(i * rows, (i + 1) * rows) for i in range(3)]
-    to_near = add(mine[block[1]], met[block[1]])
-    side = partner(side_1)
-    far, = after(met, early(far, 10))
-    last_mine, last_other = experts(3, 2, far, side, partner(far))
-    to_far = add(last_mine[:rows], partner(last_other))
     passing = early(cross(to_far), 10)
     to_side = pl.pallas_call(
         side_kernel,

time: 40.4 us -> 39.7 us (0.983)
  starting transfers between devices: 12 us -> 13.2 us
  Pallas kernels: 11.1 us -> 10 us
  waiting for transfers between devices: 16.8 us -> 16 us
    pallas_call x3, Pallas kernels: 7.79 us -> 6.68 us  [the longest x2 3.47 us: experts(): pl.pallas_call(functools.partial(expert_kernel, blocks), out_shape=[jax.S...]
    ppermute x2, starting transfers between devices: 3.52 us -> 4.29 us  [cross_back(): lax.ppermute(a, 'expert', [(i, i ^ (2 if i % 2 else 4)) for i in range(de...]
    ppermute x6 -> x7, starting transfers between devices: 1.5 us -> 2.12 us  [partner(): return lax.ppermute(a, 'expert', [(i, i ^ 1) for i in range(devices)])]
    ppermute x6 -> x7, waiting for transfers between devices: 3.12 us -> 2.71 us  [partner(): return lax.ppermute(a, 'expert', [(i, i ^ 1) for i in range(devices)])]
  transfers between devices with their start and end apart: 12 -> 13, of which waited for: 9 -> 9; matrix products, arithmetic and copies ran while one was open for 0% -> 0% of each run, Pallas kernels for 16% -> 13%
where the time goes in v6:
time: 39.7 us; the launch traced here: 39.6 us
  waiting for transfers between devices  16 us (40%)
  starting transfers between devices  13.2 us (33%)
  Pallas kernels  10 us (25%)
    ppermute x4, waiting for transfers between devices, cross(): lax.ppermute(a, 'expert', [(i, i ^ (4 if i % 2 else 2)) for i in range(de...  9.35 us
    ppermute x4, starting transfers between devices, cross(): lax.ppermute(a, 'expert', [(i, i ^ (4 if i % 2 else 2)) for i in range(de...  6.82 us
    ppermute x2, starting transfers between devices, cross_back(): lax.ppermute(a, 'expert', [(i, i ^ (2 if i % 2 else 4)) for i in range(de...  4.29 us
    ppermute x2, waiting for transfers between devices, cross_back(): lax.ppermute(a, 'expert', [(i, i ^ (2 if i % 2 else 4)) for i in range(de...  3.94 us
    pallas_call x2, Pallas kernels, experts(): pl.pallas_call(functools.partial(expert_kernel, blocks), out_shape=[jax.S...  3.47 us
    pallas_call x1, Pallas kernels, load(): pl.pallas_call(load_kernel, out_shape=[jax.ShapeDtypeStruct(a.shape[1:],...  3.21 us
    ppermute x7, waiting for transfers between devices, partner(): return lax.ppermute(a, 'expert', [(i, i ^ 1) for i in range(devices)])  2.71 us
    ppermute x7, starting transfers between devices, partner(): return lax.ppermute(a, 'expert', [(i, i ^ 1) for i in range(devices)])  2.12 us
  transfers between devices with their start and end apart: 13, of which 9 were waited for; matrix products, arithmetic and copies ran while one was open for 0% of the time, Pallas kernels for 13%

profile of v6, /device:TPU:0, one launch (start us, length us, event | category | flops | bytes accessed | tf_op | source)
XLA Modules:
  0.0 39.6 jit_solution(10579990617208599844)
XLA Ops:
  0.0 2.1 %shard_map.82 = (bf16[24,7168]{1,0:T(8,128)(2,1)}, bf16[24,32]{1,0:T(8,128)(2,1)}, f32[32,1]{1,0:T(8,128)}) custom-call(bf16[32,7168]{1,0:T(8,128)(2,1)} %tok_hbm.1, s32[8,32]{1,0:T(8,128)} %bitcast.11, s32[8,32]{1,0:T(8,128)} %bitcast.12, s32[2,256]{1,0:T(2,128)} %bitcast.14, f32[8,32]{1,0:T(8,128)} %bitcast.13), custom_call_target="tpu_custom_call" | custom-call | tf_op jit(solution)/shard_map/pallas_call | solution.py:235
  2.1 0.5 %collective-permute-start = (bf16[24,7168]{1,0:T(8,128)(2,1)}, bf16[24,7168]{1,0:T(8,128)(2,1)S(1)}, u32[]{:S(2)}, u32[]{:S(2)}) collective-permute-start(bf16[24,7168]{1,0:T(8,128)(2,1)} %get-tuple-element.15.refs_0_), channel_id=1, source_target_pairs={{0,1},{1,0},{2,3},{3,2},{4,5},{5,4},{6,7},{7,6},{8,9},{9,8},{10,11... | collective-permute-start | bytes 1032200 | tf_op jit(solution)/shard_map/ppermute | solution.py:215
  2.6 2.6 %collective-permute-start.1 = (bf16[24,7168]{1,0:T(8,128)(2,1)}, bf16[24,7168]{1,0:T(8,128)(2,1)S(1)}, u32[]{:S(2)}, u32[]{:S(2)}) collective-permute-start(bf16[24,7168]{1,0:T(8,128)(2,1)} %get-tuple-element.15.refs_0_), channel_id=1, source_target_pairs={{0,2},{1,5},{2,0},{3,7},{4,6},{5,1},{6,4},{7,3},{8,10},{9,13},{10,... | collective-permute-start | bytes 1032200 | tf_op jit(solution)/shard_map/ppermute | solution.py:218
  5.2 0.0 collective-permute-done.refs_0_.refs_3_
  5.2 1.8 %collective-permute-start.3 = (bf16[24,7168]{1,0:T(8,128)(2,1)S(1)}, bf16[24,7168]{1,0:T(8,128)(2,1)S(1)}, u32[]{:S(2)}, u32[]{:S(2)}) collective-permute-start(bf16[24,7168]{1,0:T(8,128)(2,1)S(1)} %collective-permute-done.refs_0_.refs_3_), channel_id=1, source_target_pairs={{0,2},{1,5},{2,0},{3,7},{4,6},{5,1},{6,4},{7,3},{8,10},{9,13},{10,... | collective-permute-start | bytes 1032200 | tf_op jit(solution)/shard_map/ppermute | solution.py:218
  7.0 3.2 %shard_map.83 = (bf16[7168,256]{1,0:T(8,128)(2,1)S(1)}, bf16[7168,256]{1,0:T(8,128)(2,1)S(1)}) custom-call(bf16[24,7168]{1,0:T(8,128)(2,1)S(1)} %collective-permute-done.refs_0_.refs_3_, bf16[7168,256]{1,0:T(8,128)(2,1)} %bitcast.9, bf16[7168,256]{1,0:T(8,128)(2,1)} %bitcast.10), custom_call_target="tpu_custom_call" | custom-call | flops 528482304 | bytes 11010048 | tf_op jit(solution)/shard_map/pallas_call | solution.py:250
  10.2 0.4 %collective-permute-done.1.refs_1_ = bf16[24,7168]{1,0:T(8,128)(2,1)S(1)} collective-permute-done((bf16[24,7168]{1,0:T(8,128)(2,1)}, bf16[24,7168]{1,0:T(8,128)(2,1)S(1)}, u32[]{:S(2)}, u32[]{:S(2)}) %collective-permute-start.1) | collective-permute-done | bytes 344096 | tf_op jit(solution)/shard_map/ppermute | solution.py:218
  10.7 0.0 copy-start
  10.7 0.0 copy-start.1
  10.7 0.0 collective-permute-start.2
  10.7 2.1 %collective-permute-start.5 = (bf16[24,7168]{1,0:T(8,128)(2,1)S(1)}, bf16[24,7168]{1,0:T(8,128)(2,1)S(1)}, u32[]{:S(2)}, u32[]{:S(2)}) collective-permute-start(bf16[24,7168]{1,0:T(8,128)(2,1)S(1)} %shard_map.84.refs_1_), channel_id=1, source_target_pairs={{0,4},{1,3},{2,6},{3,1},{4,0},{5,7},{6,2},{7,5},{8,12},{9,11},{10,... | collective-permute-start | bytes 1032200 | tf_op jit(solution)/shard_map/ppermute | solution.py:221
  12.8 1.8 %collective-permute-done.3.refs_1_ = bf16[24,7168]{1,0:T(8,128)(2,1)S(1)} collective-permute-done((bf16[24,7168]{1,0:T(8,128)(2,1)S(1)}, bf16[24,7168]{1,0:T(8,128)(2,1)S(1)}, u32[]{:S(2)}, u32[]{:S(2)}) %collective-permute-start.3) | collective-permute-done | bytes 344096 | tf_op jit(solution)/shard_map/ppermute | solution.py:218
  14.6 0.0 collective-permute-start.6
  14.6 0.0 collective-permute-done.2.refs_2_
  14.6 0.0 copy-done
  14.6 0.0 copy-done.1
  14.6 1.7 %shard_map.86 = (bf16[48,7168]{1,0:T(8,128)(2,1)S(1)}, bf16[24,7168]{1,0:T(8,128)(2,1)S(1)}, bf16[48,7168]{1,0:T(8,128)(2,1)S(1)}) custom-call(bf16[24,7168]{1,0:T(8,128)(2,1)S(1)} %copy-done.1, bf16[24,7168]{1,0:T(8,128)(2,1)S(1)} %shard_map.84.refs_1_, bf16[24,7168]{1,0:T(8,128)(2,1)S(1)} %collective-permute-done.2.refs_2_, ...), custom_call_target="tpu_custom_call" | custom-call | flops 1321205760 | bytes 11010048 | tf_op jit(solution)/shard_map/pallas_call | solution.py:290
  16.4 0.6 %collective-permute-start.4 = (bf16[24,7168]{1,0:T(8,128)(2,1)S(1)}, bf16[24,7168]{1,0:T(8,128)(2,1)S(1)}, u32[]{:S(2)}, u32[]{:S(2)}) collective-permute-start(bf16[24,7168]{1,0:T(8,128)(2,1)S(1)} %get-tuple-element.19), channel_id=1, source_target_pairs={{0,1},{1,0},{2,3},{3,2},{4,5},{5,4},{6,7},{7,6},{8,9},{9,8},{10,11... | collective-permute-start | bytes 1032200 | tf_op jit(solution)/shard_map/ppermute | solution.py:215
  16.9 1.1 %collective-permute-done.5.refs_0_ = bf16[24,7168]{1,0:T(8,128)(2,1)S(1)} collective-permute-done((bf16[24,7168]{1,0:T(8,128)(2,1)S(1)}, bf16[24,7168]{1,0:T(8,128)(2,1)S(1)}, u32[]{:S(2)}, u32[]{:S(2)}) %collective-permute-start.5) | collective-permute-done | bytes 344096 | tf_op jit(solution)/shard_map/ppermute | solution.py:221
  18.1 0.1 collective-permute-done.4.refs_0_
  18.2 0.4 collective-permute-start.7
  18.6 0.0 collective-permute-done.6.refs_0_
  18.6 1.3 %collective-permute-done.7.refs_2_ = bf16[24,7168]{1,0:T(8,128)(2,1)S(1)} collective-permute-done((bf16[24,7168]{1,0:T(8,128)(2,1)S(1)}, bf16[24,7168]{1,0:T(8,128)(2,1)S(1)}, u32[]{:S(2)}, u32[]{:S(2)}) %collective-permute-start.7) | collective-permute-done | bytes 344096 | tf_op jit(solution)/shard_map/ppermute | solution.py:215
  19.9 1.7 %shard_map.90 = (bf16[48,7168]{1,0:T(8,128)(2,1)S(1)}, bf16[24,7168]{1,0:T(8,128)(2,1)S(1)}) custom-call(bf16[24,7168]{1,0:T(8,128)(2,1)S(1)} %shard_map.88.refs_0_, bf16[24,7168]{1,0:T(8,128)(2,1)S(1)} %shard_map.89.refs_1_, bf16[24,7168]{1,0:T(8,128)(2,1)S(1)} %collective-permute-done.7.refs_2_, ...), custom_call_target="tpu_custom_call" | custom-call | flops 792723456 | bytes 11010048 | tf_op jit(solution)/shard_map/pallas_call | solution.py:290
  21.6 0.4 %collective-permute-start.8 = (bf16[24,7168]{1,0:T(8,128)(2,1)S(1)}, bf16[24,7168]{1,0:T(8,128)(2,1)S(1)}, u32[]{:S(2)}, u32[]{:S(2)}) collective-permute-start(bf16[24,7168]{1,0:T(8,128)(2,1)S(1)} %get-tuple-element.21), channel_id=1, source_target_pairs={{0,1},{1,0},{2,3},{3,2},{4,5},{5,4},{6,7},{7,6},{8,9},{9,8},{10,11... | collective-permute-start | bytes 1032200 | tf_op jit(solution)/shard_map/ppermute | solution.py:215
  22.0 1.3 %collective-permute-done.8 = bf16[24,7168]{1,0:T(8,128)(2,1)S(1)} collective-permute-done((bf16[24,7168]{1,0:T(8,128)(2,1)S(1)}, bf16[24,7168]{1,0:T(8,128)(2,1)S(1)}, u32[]{:S(2)}, u32[]{:S(2)}) %collective-permute-start.8) | collective-permute-done | bytes 344096 | tf_op jit(solution)/shard_map/ppermute | solution.py:215
  23.3 0.1 add_convert_fusion.2.refs_0_._
  23.4 2.4 %collective-permute-start.11 = (bf16[24,7168]{1,0:T(8,128)(2,1)S(1)}, bf16[24,7168]{1,0:T(8,128)(2,1)S(1)}, u32[]{:S(2)}, u32[]{:S(2)}) collective-permute-start(bf16[24,7168]{1,0:T(8,128)(2,1)S(1)} %add_convert_fusion.2.refs_0_._), channel_id=1, source_target_pairs={{0,2},{1,5},{2,0},{3,7},{4,6},{5,1},{6,4},{7,3},{8,10},{9,13},{10,... | collective-permute-start | bytes 1032200 | tf_op jit(solution)/shard_map/ppermute | solution.py:218
  25.8 0.1 add_convert_fusion.1
  25.9 0.1 collective-permute-start.10
  25.9 0.2 collective-permute-start.9
  26.2 4.8 %collective-permute-done.11.refs_0_ = bf16[24,7168]{1,0:T(8,128)(2,1)S(1)} collective-permute-done((bf16[24,7168]{1,0:T(8,128)(2,1)S(1)}, bf16[24,7168]{1,0:T(8,128)(2,1)S(1)}, u32[]{:S(2)}, u32[]{:S(2)}) %collective-permute-start.11) | collective-permute-done | bytes 344096 | tf_op jit(solution)/shard_map/ppermute | solution.py:218
  31.0 0.0 collective-permute-done.9.met_ref
  31.0 0.1 shard_map.92.refs_0_
  31.1 0.0 copy-start.2
  31.1 0.0 copy-start.3
  31.1 0.1 add_convert_fusion
  31.2 2.1 %collective-permute-start.12 = (bf16[24,7168]{1,0:T(8,128)(2,1)S(1)}, bf16[24,7168]{1,0:T(8,128)(2,1)S(1)}, u32[]{:S(2)}, u32[]{:S(2)}) collective-permute-start(bf16[24,7168]{1,0:T(8,128)(2,1)S(1)} %add_convert_fusion), channel_id=1, source_target_pairs={{0,4},{1,3},{2,6},{3,1},{4,0},{5,7},{6,2},{7,5},{8,12},{9,11},{10,... | collective-permute-start | bytes 1032200 | tf_op jit(solution)/shard_map/ppermute | solution.py:221
  33.3 2.3 %collective-permute-done.10.refs_1_ = bf16[24,7168]{1,0:T(8,128)(2,1)S(1)} collective-permute-done((bf16[24,7168]{1,0:T(8,128)(2,1)S(1)}, bf16[24,7168]{1,0:T(8,128)(2,1)S(1)}, u32[]{:S(2)}, u32[]{:S(2)}) %collective-permute-start.10) | collective-permute-done | bytes 344096 | tf_op jit(solution)/shard_map/ppermute | solution.py:218
  35.6 0.1 shard_map.94.settled_ref
  35.7 2.8 %collective-permute-done.12.side_ref = bf16[24,7168]{1,0:T(8,128)(2,1)S(1)} collective-permute-done((bf16[24,7168]{1,0:T(8,128)(2,1)S(1)}, bf16[24,7168]{1,0:T(8,128)(2,1)S(1)}, u32[]{:S(2)}, u32[]{:S(2)}) %collective-permute-start.12) | collective-permute-done | bytes 344096 | tf_op jit(solution)/shard_map/ppermute | solution.py:221
  38.5 0.0 copy-done.2
  38.5 0.0 copy-done.3
  38.5 1.0 %shard_map.96 = bf16[32,7168]{1,0:T(8,128)(2,1)} custom-call(f32[24,7168]{1,0:T(8,128)S(1)} %shard_map.94.settled_ref, bf16[24,7168]{1,0:T(8,128)(2,1)S(1)} %collective-permute-done.12.side_ref, bf16[24,32]{1,0:T(8,128)(2,1)S(1)} %copy-done.3, f32[32,1]{1,0:T(8,128)S(1)} %copy-done.2), custom_call_target="tpu_custom_call" | custom-call | tf_op jit(solution)/shard_map/pallas_call | solution.py:325
  (8 shorter events, 0.0 us)
Async XLA Ops:
  2.1 3.1 %collective-permute-start = (bf16[24,7168]{1,0:T(8,128)(2,1)}, bf16[24,7168]{1,0:T(8,128)(2,1)S(1)}, u32[]{:S(2)}, u32[]{:S(2)}) collective-permute-start(bf16[24,7168]{1,0:T(8,128)(2,1)} %get-tuple-element.15.refs_0_), channel_id=1, source_target_pairs={{0,1},{1,0},{2,3},{3,2},{4,5},{5,4},{6,7},{7,6},{8,9},{9,8},{10,11... | collective-permute-start | bytes 1032200 | tf_op jit(solution)/shard_map/ppermute | solution.py:215
  2.6 8.0 %collective-permute-start.1 = (bf16[24,7168]{1,0:T(8,128)(2,1)}, bf16[24,7168]{1,0:T(8,128)(2,1)S(1)}, u32[]{:S(2)}, u32[]{:S(2)}) collective-permute-start(bf16[24,7168]{1,0:T(8,128)(2,1)} %get-tuple-element.15.refs_0_), channel_id=1, source_target_pairs={{0,2},{1,5},{2,0},{3,7},{4,6},{5,1},{6,4},{7,3},{8,10},{9,13},{10,... | collective-permute-start | bytes 1032200 | tf_op jit(solution)/shard_map/ppermute | solution.py:218
  5.2 9.4 %collective-permute-start.3 = (bf16[24,7168]{1,0:T(8,128)(2,1)S(1)}, bf16[24,7168]{1,0:T(8,128)(2,1)S(1)}, u32[]{:S(2)}, u32[]{:S(2)}) collective-permute-start(bf16[24,7168]{1,0:T(8,128)(2,1)S(1)} %collective-permute-done.refs_0_.refs_3_), channel_id=1, source_target_pairs={{0,2},{1,5},{2,0},{3,7},{4,6},{5,1},{6,4},{7,3},{8,10},{9,13},{10,... | collective-permute-start | bytes 1032200 | tf_op jit(solution)/shard_map/ppermute | solution.py:218
  10.7 3.9 %copy-start = (bf16[1,256,7168]{2,1,0:T(8,128)(2,1)S(1)}, bf16[1,256,7168]{2,1,0:T(8,128)(2,1)}, u32[]{:S(2)}) copy-start(bf16[1,256,7168]{2,1,0:T(8,128)(2,1)} %param.15) | copy-start | bytes 11010052
  10.7 3.9 %copy-start.1 = (bf16[24,7168]{1,0:T(8,128)(2,1)S(1)}, bf16[24,7168]{1,0:T(8,128)(2,1)}, u32[]{:S(2)}) copy-start(bf16[24,7168]{1,0:T(8,128)(2,1)} %get-tuple-element.15.refs_0_) | copy-start | bytes 1032196
  10.7 3.9 %collective-permute-start.2 = (bf16[24,7168]{1,0:T(8,128)(2,1)S(1)}, bf16[24,7168]{1,0:T(8,128)(2,1)S(1)}, u32[]{:S(2)}, u32[]{:S(2)}) collective-permute-start(bf16[24,7168]{1,0:T(8,128)(2,1)S(1)} %shard_map.84.refs_1_), channel_id=1, source_target_pairs={{0,1},{1,0},{2,3},{3,2},{4,5},{5,4},{6,7},{7,6},{8,9},{9,8},{10,11... | collective-permute-start | bytes 1032200 | tf_op jit(solution)/shard_map/ppermute | solution.py:215
  10.7 7.4 %collective-permute-start.5 = (bf16[24,7168]{1,0:T(8,128)(2,1)S(1)}, bf16[24,7168]{1,0:T(8,128)(2,1)S(1)}, u32[]{:S(2)}, u32[]{:S(2)}) collective-permute-start(bf16[24,7168]{1,0:T(8,128)(2,1)S(1)} %shard_map.84.refs_1_), channel_id=1, source_target_pairs={{0,4},{1,3},{2,6},{3,1},{4,0},{5,7},{6,2},{7,5},{8,12},{9,11},{10,... | collective-permute-start | bytes 1032200 | tf_op jit(solution)/shard_map/ppermute | solution.py:221
  14.6 4.0 %collective-permute-start.6 = (bf16[24,7168]{1,0:T(8,128)(2,1)S(1)}, bf16[24,7168]{1,0:T(8,128)(2,1)S(1)}, u32[]{:S(2)}, u32[]{:S(2)}) collective-permute-start(bf16[24,7168]{1,0:T(8,128)(2,1)S(1)} %shard_map.85.refs_4_), channel_id=1, source_target_pairs={{0,1},{1,0},{2,3},{3,2},{4,5},{5,4},{6,7},{7,6},{8,9},{9,8},{10,11... | collective-permute-start | bytes 1032200 | tf_op jit(solution)/shard_map/ppermute | solution.py:215
  16.4 1.8 %collective-permute-start.4 = (bf16[24,7168]{1,0:T(8,128)(2,1)S(1)}, bf16[24,7168]{1,0:T(8,128)(2,1)S(1)}, u32[]{:S(2)}, u32[]{:S(2)}) collective-permute-start(bf16[24,7168]{1,0:T(8,128)(2,1)S(1)} %get-tuple-element.19), channel_id=1, source_target_pairs={{0,1},{1,0},{2,3},{3,2},{4,5},{5,4},{6,7},{7,6},{8,9},{9,8},{10,11... | collective-permute-start | bytes 1032200 | tf_op jit(solution)/shard_map/ppermute | solution.py:215
  18.2 1.7 %collective-permute-start.7 = (bf16[24,7168]{1,0:T(8,128)(2,1)S(1)}, bf16[24,7168]{1,0:T(8,128)(2,1)S(1)}, u32[]{:S(2)}, u32[]{:S(2)}) collective-permute-start(bf16[24,7168]{1,0:T(8,128)(2,1)S(1)} %shard_map.88.refs_0_), channel_id=1, source_target_pairs={{0,1},{1,0},{2,3},{3,2},{4,5},{5,4},{6,7},{7,6},{8,9},{9,8},{10,11... | collective-permute-start | bytes 1032200 | tf_op jit(solution)/shard_map/ppermute | solution.py:215
  21.6 1.7 %collective-permute-start.8 = (bf16[24,7168]{1,0:T(8,128)(2,1)S(1)}, bf16[24,7168]{1,0:T(8,128)(2,1)S(1)}, u32[]{:S(2)}, u32[]{:S(2)}) collective-permute-start(bf16[24,7168]{1,0:T(8,128)(2,1)S(1)} %get-tuple-element.21), channel_id=1, source_target_pairs={{0,1},{1,0},{2,3},{3,2},{4,5},{5,4},{6,7},{7,6},{8,9},{9,8},{10,11... | collective-permute-start | bytes 1032200 | tf_op jit(solution)/shard_map/ppermute | solution.py:215
  23.4 7.6 %collective-permute-start.11 = (bf16[24,7168]{1,0:T(8,128)(2,1)S(1)}, bf16[24,7168]{1,0:T(8,128)(2,1)S(1)}, u32[]{:S(2)}, u32[]{:S(2)}) collective-permute-start(bf16[24,7168]{1,0:T(8,128)(2,1)S(1)} %add_convert_fusion.2.refs_0_._), channel_id=1, source_target_pairs={{0,2},{1,5},{2,0},{3,7},{4,6},{5,1},{6,4},{7,3},{8,10},{9,13},{10,... | collective-permute-start | bytes 1032200 | tf_op jit(solution)/shard_map/ppermute | solution.py:218
  25.9 9.8 %collective-permute-start.10 = (bf16[24,7168]{1,0:T(8,128)(2,1)S(1)}, bf16[24,7168]{1,0:T(8,128)(2,1)S(1)}, u32[]{:S(2)}, u32[]{:S(2)}) collective-permute-start(bf16[24,7168]{1,0:T(8,128)(2,1)S(1)} %add_convert_fusion.1), channel_id=1, source_target_pairs={{0,2},{1,5},{2,0},{3,7},{4,6},{5,1},{6,4},{7,3},{8,10},{9,13},{10,... | collective-permute-start | bytes 1032200 | tf_op jit(solution)/shard_map/ppermute | solution.py:218
  25.9 5.1 %collective-permute-start.9 = (bf16[48,7168]{1,0:T(8,128)(2,1)S(1)}, bf16[48,7168]{1,0:T(8,128)(2,1)S(1)}, u32[]{:S(2)}, u32[]{:S(2)}) collective-permute-start(bf16[48,7168]{1,0:T(8,128)(2,1)S(1)} %shard_map.91), channel_id=1, source_target_pairs={{0,1},{1,0},{2,3},{3,2},{4,5},{5,4},{6,7},{7,6},{8,9},{9,8},{10,11... | collective-permute-start | bytes 2064392 | tf_op jit(solution)/shard_map/ppermute | solution.py:215
  31.1 7.5 %copy-start.2 = (f32[32,1]{1,0:T(8,128)S(1)}, f32[32,1]{1,0:T(8,128)}, u32[]{:S(2)}) copy-start(f32[32,1]{1,0:T(8,128)} %get-tuple-element.24.weight_ref) | copy-start | bytes 388
  31.1 7.5 %copy-start.3 = (bf16[24,32]{1,0:T(8,128)(2,1)S(1)}, bf16[24,32]{1,0:T(8,128)(2,1)}, u32[]{:S(2)}) copy-start(bf16[24,32]{1,0:T(8,128)(2,1)} %get-tuple-element.23.chosen_ref) | copy-start | bytes 4612
  31.2 7.4 %collective-permute-start.12 = (bf16[24,7168]{1,0:T(8,128)(2,1)S(1)}, bf16[24,7168]{1,0:T(8,128)(2,1)S(1)}, u32[]{:S(2)}, u32[]{:S(2)}) collective-permute-start(bf16[24,7168]{1,0:T(8,128)(2,1)S(1)} %add_convert_fusion), channel_id=1, source_target_pairs={{0,4},{1,3},{2,6},{3,1},{4,0},{5,7},{6,2},{7,5},{8,12},{9,11},{10,... | collective-permute-start | bytes 1032200 | tf_op jit(solution)/shard_map/ppermute | solution.py:221
